TPU v7x, 32 devices: a whole 2x2x4 slice. The times are simulated.
32 devices in a mesh: row: 2 (over y), col: 4 (over z), own: 4 (over x, core).
Axes of the slice: x: 2, y: 2, z: 4, core: 2. Of those that a mesh axis runs over, the one named last changes fastest.
Arguments:
- viscosity: float32 [2048, 512], P(('row', 'own'), 'col'), may hold values from 0.5 to 8
- friction: float32 [2048, 512], P(('row', 'own'), 'col'), may hold values from 0.3 to 6
- driving: float32 [2, 2048, 512], P(None, ('row', 'own'), 'col'), may hold values from -32 to 32
- observed: float32 [2, 2048, 512], P(None, ('row', 'own'), 'col'), may hold values from -6 to 6
- ice_mask: int32 [2048, 512], P(('row', 'own'), 'col'), may hold values 0 or 1
- tile_block: int32 [16, 4], P(('row', 'own'), 'col'), may hold values from 0 to 15, as said below
- owner_list: int32 [16], replicated, may hold values from 0 to 15, each once
Outputs:
- velocity: float32 [2, 2048, 512], P(None, ('row', 'own'), 'col')
- block_gradient: float32 [4, 4, 1024], P('own')
Inputs may be any that keep to these rules, and one draw needn't show every extreme that they name: `tile_block`: tile rows 2r and 2r+1 carry the same ids; along the tile columns they run through r*2 to r*2 + 1 in order, each id on one run of consecutive tile columns of ragged length. `owner_list`: every block appears once.
All inputs are finite; a program needn't handle non-finite values. No bound on the sum of `ice_mask` on one device may be relied on, other than what follows from the above.
Results may differ from a plain program's by a relative error of at most 0.000088.
Values sent between devices are 32-bit elements; how exact they have to be, the bound alone decides.
No kernel may reach another device: no remote copies, remote signals or barrier semaphores. Data moves between devices by JAX's collectives and lax.ppermute only.
A program may use at most 64 MiB of HBM per device.

v0:
```python
import math

import jax
import jax.numpy as jnp
import numpy as np
from jax import lax
from jax.experimental import pallas as pl
from jax.experimental.pallas import tpu as pltpu
from jax.sharding import PartitionSpec as P

TILE = 128
MODES = 32
SWEEPS = 3
SUB = 8
HALO = 8
INNER = 2 * HALO
STRIP = 40
LEAD = HALO - 1
KEPT = 12
OUTER = (LEAD, STRIP - 2 * HALO)
NEAR, FAR = 7, 6
ARRAYS = 7
VISC, FRIC, DRIV, MASK, OBS = 0, 1, 2, 4, 5
EDGE = ARRAYS * HALO
SLOT = 2 * INNER
PER = TILE // SLOT
GROUPS = 5
SENT = 2 * GROUPS * HALO + HALO
PARTS = 3
UPPER, LOWER = 32, 64
ROW_AXES = ("row", "own")
COL_AXES = ("col",)
F32 = jnp.float32
LIMIT = 40 * 1024 * 1024


def swap(x, axis, first):
    sizes = lax.axis_size(ROW_AXES), lax.axis_size(COL_AXES)
    owners = lax.axis_size("own")

    def device(i, j):
        return (i // owners * sizes[1] + j) * owners + i % owners

    pairs = []
    for i in range(sizes[0]):
        for j in range(sizes[1]):
            place = [i, j]
            if first and place[axis] in (0, sizes[axis] - 1):
                place[1 - axis] ^= 1
            else:
                place[axis] = ((place[axis] + first) ^ 1) - first
            pairs.append((device(i, j), device(*place)))
    return lax.ppermute(x, ("row", "col", "own"), pairs)


def position(axes):
    index, size = 0, 1
    for axis in axes:
        index = index * lax.axis_size(axis) + lax.axis_index(axis)
        size *= lax.axis_size(axis)
    assert size % 2 == 0
    return lax.rem(index, 2) == 0, (index == 0) | (index == size - 1)


def is_even(axes):
    return position(axes)[0]


def lanes():
    return lax.broadcasted_iota(jnp.int32, (SUB, TILE), 1)


def call(kernel, name, outs, scratch, cost, *args, aliases={}):
    return pl.pallas_call(
        kernel,
        out_shape=outs,
        scratch_shapes=scratch,
        input_output_aliases=aliases,
        compiler_params=pltpu.CompilerParams(vmem_limit_bytes=LIMIT),
        cost_estimate=pl.CostEstimate(flops=cost, bytes_accessed=cost, transcendentals=0),
        name=name,
    )(*args)


def vmem(*shape):
    return pltpu.VMEM(shape, F32)


FIELDS = 14
STRIP_FIELDS = 24


class Domain:
    def __init__(self, refs, base, span, source, seam=None):
        self.refs, self.base, self.span, self.source, self.seam = refs, base, span, source, seam

    def at(self, j):
        return pl.ds(self.base + SUB * j, SUB)

    def prepare(self, flipped):
        n2, n4, c, i, b0, b1 = self.refs[:6]
        visc = [self.source(VISC, j) for j in range(self.span)]
        for j in range(self.span):
            at = self.at(j)
            before = visc[j - 1] if j else pltpu.roll(visc[-1], 1, 0)
            if self.seam and not j:
                row = lax.broadcasted_iota(jnp.int32, (SUB, TILE), 0)
                before = jnp.where(row == SUB // 2, self.seam(), before)
            pair = visc[j] + before
            fric = self.source(FRIC, j)
            diag = 1.25 * (pair + pltpu.roll(pair, 1, 1)) + fric
            on = self.source(MASK, j) > 0.0
            inv = jnp.where(on, 0.5 / jnp.where(on, diag, 1.0), 0.0)
            half = 0.5 * visc[j]
            n2[at, :] = half
            n4[at, :] = 0.5 * half
            c[at, :] = 1.0 - fric * inv
            i[at, :] = inv
            for k, b in enumerate((b0, b1)):
                value = inv * self.source(DRIV + (1 - k if flipped else k), j)
                b[at, :] = value
                self.write(k, at, value + value)

    def write(self, k, at, value):
        self.refs[6 + k][at, :] = value
        self.refs[8 + k][at, :] = pltpu.roll(value, TILE - 1, 1)

    def retarget(self, flipped, velocity=None):
        i, b0, b1 = self.refs[3:6]
        w0, w1 = velocity or self.refs[6:8]
        for j in range(self.span):
            at = self.at(j)
            for k, (b, w) in enumerate(((b0, w0), (b1, w1))):
                value = i[at, :] * (w[at, :] - self.source(OBS + (1 - k if flipped else k), j))
                b[at, :] = value
                self.write(k, at, value + value)

    def differences(self):
        n2, n4 = self.refs[:2]
        fields = self.refs[6:10]
        parts = self.refs[10:14]

        def corners(j, here, below):
            w0, w1, r0, r1 = here
            v0, v1, s0, s1 = below
            a1, a2 = s0 - w0, v0 - r0
            e1, e2 = s1 - w1, v1 - r1
            x, y = a1 + a2, e1 - e2
            q = (a1 - a2) + (e1 + e2)
            both = x + y
            at = self.at(j)
            half = n2[at, :]
            return half * (both + x), n4[at, :] * q, half * (both + y)

        def load(j):
            at = self.at(j)
            return [field[at, :] for field in fields]

        top = load(0)
        last = corners(self.span - 1, load(self.span - 1), [pltpu.roll(v, SUB - 1, 0) for v in top])
        up = [pltpu.roll(v, 1, 0) for v in last]
        here = top
        for j in range(self.span):
            at = self.at(j)
            if j < self.span - 1:
                below = load(j + 1)
                p, q, r = corners(j, here, below)
                here = below
            else:
                p, q, r = last
            g, t = up[0] - p, up[1] + q
            gq, tr = up[1] - q, up[2] + r
            parts[0][at, :] = g - t
            parts[1][at, :] = gq - tr
            parts[2][at, :] = pltpu.roll(g + t, 1, 1)
            parts[3][at, :] = pltpu.roll(gq + tr, 1, 1)
            up = (p, q, r)

    def update(self):
        c, i, b0, b1, w0, w1 = self.refs[2:8]
        parts = self.refs[10:14]
        for j in range(self.span):
            at = self.at(j)
            cv, iv = c[at, :], i[at, :]
            for k, (b, w) in enumerate(((b0, w0), (b1, w1))):
                value = (cv * w[at, :] + b[at, :]) - iv * (parts[k][at, :] + parts[k + 2][at, :])
                self.write(k, at, value)


class Strips(Domain):
    def prepare(self, flipped):
        super().prepare(flipped)
        for j in range(self.span):
            at = self.at(j)
            for now, later in zip(self.refs[2:6], self.refs[10:14]):
                later[at, :] = pltpu.roll(now[at, :], TILE - 1, 1)
        for now, before in zip(self.refs[:2], self.refs[14:16]):
            before[self.at(0), :] = pltpu.roll(now[self.at(self.span - 1), :], 1, 0)

    def retarget(self, flipped, velocity=None):
        super().retarget(flipped, velocity)
        for j in range(self.span):
            at = self.at(j)
            for now, later in zip(self.refs[4:6], self.refs[12:14]):
                later[at, :] = pltpu.roll(now[at, :], TILE - 1, 1)

    def differences(self):
        fields = self.refs[6:10]
        kept, turned, kept_next, turned_next = (self.refs[16 + 2 * k : 18 + 2 * k] for k in range(4))

        def corners(halves, quarters, j, here, below):
            w0, w1, r0, r1 = here
            v0, v1, s0, s1 = below
            a1, a2 = s0 - w0, v0 - r0
            e1, e2 = s1 - w1, v1 - r1
            x, y = a1 + a2, e1 - e2
            q = (a1 - a2) + (e1 + e2)
            both = x + y
            at = self.at(j)
            half = halves[at, :]
            return half * (both + x), quarters[at, :] * q, half * (both + y)

        def load(j):
            at = self.at(j)
            return [field[at, :] for field in fields]

        top, end = load(0), load(self.span - 1)
        up = corners(*self.refs[14:16], 0, [pltpu.roll(v, 1, 0) for v in end], top)
        here = top
        for j in range(self.span):
            at = self.at(j)
            below = load(j + 1) if j < self.span - 1 else [pltpu.roll(v, SUB - 1, 0) for v in top]
            p, q, r = corners(*self.refs[:2], j, here, below)
            g, t = up[0] - p, up[1] + q
            gq, tr = up[1] - q, up[2] + r
            for k, (stay, move) in enumerate(((g - t, g + t), (gq - tr, gq + tr))):
                kept[k][at, :] = stay
                turned_next[k][at, :] = move
                turned[k][at, :] = pltpu.roll(move, 1, 1)
                kept_next[k][at, :] = pltpu.roll(stay, TILE - 1, 1)
            up, here = (p, q, r), below

    def update(self):
        for first, offset, parts in ((2, 6, (16, 18)), (10, 8, (20, 22))):
            c, i, *b = self.refs[first : first + 4]
            for j in range(self.span):
                at = self.at(j)
                cv, iv = c[at, :], i[at, :]
                for k in range(2):
                    w = self.refs[offset + k]
                    change = self.refs[parts[0] + k][at, :] + self.refs[parts[1] + k][at, :]
                    w[at, :] = (cv * w[at, :] + b[k][at, :]) - iv * change


def run(domains, written_out=False):
    def body(_, carry):
        for domain in domains:
            domain.differences()
        for domain in domains:
            domain.update()
        return carry

    if written_out:
        for k in range(SWEEPS):
            body(k, 0)
    else:
        lax.fori_loop(0, SWEEPS, body, 0)


def ends_kernel(visc, fric, driv, mask, obs, to_b, to_a, one, two, flags, sems):
    rows = visc.shape[0]
    copies = []
    for e, first in enumerate((0, rows - HALO)):
        at = pl.ds(first, HALO)
        pieces = [
            (visc.at[at], one.at[e, 0]),
            (fric.at[at], one.at[e, 1]),
            (driv.at[:, at], two.at[e, 0]),
            (mask.at[at], flags.at[e]),
            (obs.at[:, at], two.at[e, 1]),
        ]
        for n, (source, place) in enumerate(pieces):
            copies.append(pltpu.make_async_copy(source, place, sems.at[e, n]))
    for copy in copies:
        copy.start()
    for copy in copies:
        copy.wait()
    even, at_end = position(ROW_AXES)

    def edge(e):
        return [one[e, 0], one[e, 1], two[e, 0, 0], two[e, 0, 1], flags[e].astype(F32), two[e, 1, 0], two[e, 1, 1]]

    for a, (head, tail) in enumerate(zip(edge(0), edge(1))):
        at = slice(HALO * a, HALO * (a + 1))
        to_a[at, :] = jnp.where(even, tail, head)
        to_b[at, :] = jnp.where(at_end, 0.0, jnp.where(even, head, tail))


def field_of(visc, fric, driv, mask, obs):
    def field(a, at):
        if a == MASK:
            return mask[at, :].astype(F32)
        if a >= OBS:
            return obs[a - OBS, at, :]
        if a >= DRIV:
            return driv[a - DRIV, at, :]
        return (visc, fric)[a][at, :]

    return field


def first_row(part, lane):
    if part < 2:
        return TILE * part + lane
    if lane < INNER + HALO:
        return TILE + lane
    if lane >= TILE - INNER - HALO:
        return lane
    if UPPER + HALO <= lane < UPPER + SLOT:
        return lane - UPPER - HALO
    if LOWER <= lane < LOWER + INNER + HALO:
        return 2 * TILE - INNER - HALO + lane - LOWER
    return None


def right_part(row):
    seam = TILE - HALO <= row < TILE + HALO
    part = 2 if seam or row == 0 or row == 2 * TILE - HALO else row // TILE
    return part, [lane for lane in range(0, TILE, SUB) if first_row(part, lane) == row][-1]


def slot(part, a):
    return TILE * (2 * part + a // PER) + SLOT * (a % PER)


def interior_kernel(visc, fric, driv, mask, obs, edge, n2, n4, c, i, v0, v1, *refs):
    span = visc.shape[0] // SUB
    field = field_of(visc, fric, driv, mask, obs)
    lane = lanes()
    for part in range(PARTS):
        for m in range(-(-ARRAYS // PER)):
            strips = []
            for at in range(0, TILE, SUB):
                row = first_row(part, at)
                packed = jnp.zeros((SUB, TILE), F32)
                if row is not None:
                    for k in range(min(PER, ARRAYS - PER * m)):
                        value = field(PER * m + k, slice(row, row + SUB))
                        moved = pltpu.roll(value, (SLOT * k + INNER) % TILE, 1)
                        packed = jnp.where(lax.div(lane, SLOT) == k, moved, packed)
                strips.append(packed)
            base = TILE * (2 * part + m)
            edge[base : base + TILE, :] = jnp.concatenate(strips, axis=0).T
    refs = (n2, n4, c, i, *refs[:2], v0, v1, *refs[2:])
    domain = Domain(refs, 0, span, lambda a, j: field(a, pl.ds(j, SUB, stride=span)))
    domain.prepare(False)
    run([domain])


def columns_kernel(row_b, row_a, edge, to_b, to_a, turned):
    even = is_even(ROW_AXES)
    above = jnp.where(even, row_b[...], row_a[...])
    below = jnp.where(even, row_a[...], row_b[...])
    halo = jnp.concatenate([above, below, jnp.zeros((TILE - 2 * EDGE, TILE), F32)], axis=0).T
    turned[:INNER, :] = halo[TILE - INNER :]
    turned[INNER:, :] = halo[:INNER]
    even, at_end = position(COL_AXES)
    row = lax.broadcasted_iota(jnp.int32, (SUB, TILE), 0)

    def put(out, right, left):
        right = pltpu.roll(right, LEAD, 0)
        to_a[out : out + HALO, :] = jnp.where(even, right, left)
        to_b[out : out + HALO, :] = jnp.where(at_end, 0.0, jnp.where(even, left, right))

    for part in range(2):
        right, left = [], []
        for a in range(ARRAYS):
            at = slot(part, a) + INNER
            right.append(edge[at - HALO : at, :])
            left.append(edge[at : at + HALO, :])
        for k in range(2):
            seen_r, seen_l = right[OBS + k], left[OBS + k]
            g = 1 + 2 * k
            right[g] = jnp.where(row < 2, pltpu.roll(seen_r, 2, 0), right[g])
            right[g + 1] = jnp.where(row < 2, pltpu.roll(seen_r, 4, 0), right[g + 1])
            left[g] = jnp.where(row >= 6, pltpu.roll(seen_l, 6, 0), left[g])
            left[g + 1] = jnp.where(row >= 6, pltpu.roll(seen_l, 4, 0), left[g + 1])
        for g in range(GROUPS):
            put(HALO * (GROUPS * part + g), right[g], left[g])
    put(2 * GROUPS * HALO, halo[TILE - HALO :], halo[:HALO])


def strided(stack, base):
    span = STRIP // SUB
    return lambda a, j: stack[pl.ds(base + STRIP * a + j, SUB, stride=span), :]


def fill(stack, base, first, last):
    row = lax.broadcasted_iota(jnp.int32, (SUB, TILE), 0)
    one, two = (pltpu.roll(value, LEAD, 0) for value in first)
    mixed = [jnp.where(row == LEAD, two, one), jnp.where(row < SUB // 2, two, last[0])]
    for k, value in enumerate((one, *mixed, last[1])):
        stack[base + SUB * k : base + SUB * (k + 1), :] = value


def velocity(domain, plain, base):
    for j in range(domain.span):
        at = domain.at(j)
        for k in range(2):
            plain[pl.ds(base + STRIP * k + j, SUB, stride=domain.span), :] = domain.refs[6 + k][at, :]


def density(domain, plain, base, out, place):
    w0, w1 = domain.refs[6:8]
    for j in range(domain.span):
        at = domain.at(j)
        v0, v1 = (plain[pl.ds(base + STRIP * k + j, SUB, stride=domain.span), :] for k in range(2))
        value = -domain.source(FRIC, j) * (w0[at, :] * v0 + w1[at, :] * v1)
        out[pl.ds(place + j, SUB, stride=domain.span), :] = value


def beside():
    lane = lanes()
    return (lane < NEAR) | (lane >= TILE - FAR)


def ends(second):
    row = lax.broadcasted_iota(jnp.int32, (SUB, TILE), 0)
    return row >= SUB - FAR if second else row < NEAR


def adjoint_kernel(
    row_b, row_a, visc, fric, driv, mask, obs, n2, n4, c, i, v0, v1, basis_p, basis_q, edge, turned,
    vel, wide, sides, seams,
    stack, plain, dens, total, *refs,
):
    rows = visc.shape[0]
    span = rows // SUB
    even = is_even(ROW_AXES)
    field = field_of(visc, fric, driv, mask, obs)
    for a in range(ARRAYS):
        at = slice(HALO * a, HALO * (a + 1))
        got_a, got_b = row_a[at, :], row_b[at, :]
        base = STRIP * a
        first = [field(a, slice(at, at + SUB)) for at in (0, SUB)]
        last = [field(a, slice(at, at + SUB)) for at in (rows - 2 * SUB, rows - SUB)]
        fill(stack, base, first, last)
        stack[base : base + LEAD, :] = jnp.where(even, got_b, got_a)[HALO - LEAD :]
        stack[base + STRIP - HALO : base + STRIP, :] = jnp.where(even, got_a, got_b)
    strips = Strips(refs[:STRIP_FIELDS], 0, STRIP // SUB, strided(stack, 0), lambda: visc[rows - KEPT - 1 : rows - KEPT, :])
    strips.prepare(False)
    run([strips])
    velocity(strips, plain, 0)
    for k in range(2):
        for e in range(2):
            out = HALO * (2 * k + e)
            vel[out : out + HALO, :] = plain[STRIP * k + OUTER[e] : STRIP * k + OUTER[e] + HALO, :]
    interior = Domain(
        (n2, n4, c, i, *refs[STRIP_FIELDS:]), 0, span, lambda a, j: field(a, pl.ds(j, SUB, stride=span))
    )
    strips.retarget(False)
    interior.retarget(False, (v0, v1))
    run([interior, strips])
    w0, w1 = interior.refs[6:8]
    for j in range(span):
        at = interior.at(j)
        value = -interior.source(FRIC, j) * (w0[at, :] * v0[at, :] + w1[at, :] * v1[at, :])
        dens[pl.ds(j, SUB, stride=span), :] = value
    density(strips, plain, 0, dens, rows)

    side = beside()
    for s in range(0, TILE, SUB):
        summed = jnp.zeros((SUB, TILE), F32)
        for row in range(s, rows, TILE):
            value = dens[row : row + SUB, :]
            if row in (0, rows - SUB):
                at = rows + OUTER[row > 0]
                value = jnp.where(ends(row > 0), dens[at : at + SUB, :], value)
            summed += value
        total[s : s + SUB, :] = jnp.where(side, 0.0, summed)
    exact = dict(precision=lax.Precision.HIGHEST, preferred_element_type=F32)
    half = jnp.dot(basis_p[...], total[...], **exact)
    wide[...] = jnp.dot(half, basis_q[...], **exact)

    corner = corners()
    for part in range(PARTS):
        for a in range(ARRAYS):
            columns = []
            for r in range(0, SLOT, SUB):
                value = edge[slot(part, a) + r : slot(part, a) + r + SUB, :]
                if part == 2:
                    moved = pltpu.roll(turned[r : r + SUB, :], (UPPER - HALO * a) % TILE, 1)
                    value = jnp.where(corner, moved, value)
                columns.append(value)
            fill(sides, strip(part, a), columns[2:], columns[:2])
            if a == VISC:
                seams[SUB * part : SUB * (part + 1), :] = columns[0]


def strip(part, a):
    return STRIP * (ARRAYS * part + a)


def corners():
    lane = lanes()
    above = (lane >= UPPER) & (lane < UPPER + HALO)
    return above | ((lane >= LOWER + INNER + HALO) & (lane < LOWER + SLOT))


def split(x, axis):
    high = x.astype(jnp.bfloat16)
    low = (x - high.astype(F32)).astype(jnp.bfloat16)
    return jnp.concatenate([high, high, low], axis=axis)


def split_constant(x, axis):
    x = np.asarray(x, np.float32)
    high = np.asarray(x, jnp.bfloat16)
    low = np.asarray(x - np.asarray(high, np.float32), jnp.bfloat16)
    return jnp.asarray(np.concatenate([high, low, high], axis=axis))


def left_right_kernel(
    _, seams, col_b, col_a, wide_in, block, basis_rows, basis_cols,
    stack, strips, coef,
    plain, *refs,
):
    even = is_even(COL_AXES)
    lane = lanes()
    row = lax.broadcasted_iota(jnp.int32, (SUB, TILE), 0)
    upper = (lane >= UPPER + HALO) & (lane < UPPER + SLOT)
    lower = (lane >= LOWER) & (lane < LOWER + INNER + HALO)
    seam_t0 = lane >= TILE - INNER - HALO
    seam_t1 = lane < INNER + HALO
    corner = corners()
    for from_left in (True, False):
        groups = []
        for g in range(2 * GROUPS + 1):
            got_a, got_b = col_a[HALO * g : HALO * (g + 1), :], col_b[HALO * g : HALO * (g + 1), :]
            groups.append(jnp.where(even, got_b, got_a) if from_left else jnp.where(even, got_a, got_b))
        tiles = []
        for part in range(2):
            tile = groups[GROUPS * part : GROUPS * (part + 1)]
            for k in range(2):
                g, h = tile[1 + 2 * k], tile[2 + 2 * k]
                if from_left:
                    tile.append(jnp.where(row >= 5, pltpu.roll(g, 6, 0), pltpu.roll(h, 4, 0)))
                else:
                    tile.append(jnp.where(row < 2, pltpu.roll(g, 2, 0), pltpu.roll(h, 4, 0)))
            tiles.append(tile)
        for a in range(ARRAYS):
            t0, t1 = tiles[0][a], tiles[1][a]
            third = jnp.where(corner, pltpu.roll(groups[-1], (UPPER - HALO * a) % TILE, 1), 0.0)
            third = jnp.where(upper, pltpu.roll(t0, UPPER + HALO, 1), third)
            third = jnp.where(lower, pltpu.roll(t1, LOWER + INNER + HALO, 1), third)
            third = jnp.where(seam_t0, t0, jnp.where(seam_t1, t1, third))
            for part, value in enumerate((t0, t1, third)):
                base = strip(part, a)
                if from_left:
                    stack[base : base + LEAD, :] = value[:LEAD]
                else:
                    stack[base + STRIP - HALO : base + STRIP, :] = value
    last = INNER - KEPT - 1
    before = [lambda at=SUB * part + last: seams[at : at + 1, :] for part in range(PARTS)]
    domains = [
        Strips(refs, STRIP * part, STRIP // SUB, strided(stack, strip(part, 0)), seam)
        for part, seam in enumerate(before)
    ]
    for domain in domains:
        domain.prepare(True)
    run(domains, True)
    for part, domain in enumerate(domains):
        velocity(domain, strips, 2 * STRIP * part)
        domain.retarget(True)
    run(domains, True)
    for part, domain in enumerate(domains):
        density(domain, strips, 2 * STRIP * part, plain, STRIP * part)

    def side(part):
        base = STRIP * part
        return jnp.concatenate(
            [plain[base + at : base + at + HALO, :] for at in OUTER], axis=0
        )

    lane = lax.broadcasted_iota(jnp.int32, (2 * HALO, TILE), 1)
    row = lax.broadcasted_iota(jnp.int32, (2 * HALO, TILE), 0)
    right = (row < NEAR) | (row >= 2 * HALO - FAR)
    straight = (lane >= HALO) & (lane < TILE - HALO)
    seam = (lane < HALO) | (lane >= TILE - HALO)
    top = (lane >= UPPER + HALO) & (lane < UPPER + 2 * HALO)
    bottom = (lane >= LOWER + INNER) & (lane < LOWER + INNER + HALO)
    dens = jnp.concatenate(
        [
            jnp.where(right & straight, side(0) + side(1), 0.0),
            jnp.where(right & (seam | top | bottom), side(2), 0.0),
        ],
        axis=1,
    )
    half = lax.dot_general(
        basis_rows[...], split(dens, 1), (((1,), (1,)), ((), ())), preferred_element_type=F32
    )
    wide = wide_in[...] + jnp.dot(split(half, 1), basis_cols[...], preferred_element_type=F32)
    lane = lanes()
    which = lax.div(lane, MODES)
    flat = wide[:SUB]
    for j in range(1, MODES // SUB):
        flat = jnp.where(which == j, wide[SUB * j : SUB * (j + 1)], flat)
    mark = jnp.broadcast_to(block[:1, :].astype(F32), (SUB, TILE))
    row = lax.broadcasted_iota(jnp.int32, (SUB, TILE), 0)
    moved = [flat] + [pltpu.roll(flat, r, 0) for r in range(1, SUB)] + [flat]
    lines = [flat] + [
        jnp.where(row < r - 1, moved[r - 1], jnp.where(row == r - 1, mark, moved[r])) for r in range(1, SUB + 1)
    ]
    cycle = SUB * (SUB + 1)
    chunk = min(4, coef.shape[0] // cycle)

    def spread(d, carry):
        for e in range(chunk):
            for r, line in enumerate(lines):
                coef[pl.ds(pl.multiple_of((d * chunk + e) * cycle + SUB * r, SUB), SUB), :] = line
        return carry

    lax.fori_loop(0, coef.shape[0] // cycle // chunk, spread, 0)


def join_kernel(v0, v1, vel_ends, strips, vel, turned):
    rows = vel.shape[1]
    span = rows // SUB
    middle = jnp.zeros((TILE - 2 * HALO, TILE), F32)
    side = beside()
    for k, v in enumerate((v0, v1)):
        for part in range(PARTS):
            base = STRIP * (2 * part + 1 - k)
            first, last = (strips[base + at : base + at + HALO, :] for at in OUTER)
            at = TILE * (2 * part + k)
            turned[at : at + TILE, :] = jnp.concatenate([first, middle, last], axis=0).T
        for row in range(0, rows, SUB):
            value = v[pl.ds(SUB * (row % span) + row // span, SUB, stride=SUB), :]
            if row in (0, rows - SUB):
                at = HALO * (2 * k + (row > 0))
                value = jnp.where(ends(row > 0), vel_ends[at : at + HALO, :], value)
            part, lane = right_part(row)
            at = TILE * (2 * part + k) + lane
            vel[k, row : row + SUB, :] = jnp.where(side, turned[at : at + SUB, :], value)


def bases():
    places = np.arange(TILE) + 0.5
    basis = np.cos(math.pi * places[:, None] * np.arange(MODES)[None, :] / TILE)
    groups = MODES // SUB
    order = np.arange(MODES).reshape(SUB, groups).T.reshape(-1)
    rows = basis[:, order] / TILE
    cols = np.tile(basis, (1, groups))
    placed = np.zeros((2 * TILE, MODES))
    for row in range(0, 2 * TILE, SUB):
        part, lane = right_part(row)
        at = lane + (TILE if part == 2 else 0)
        placed[at : at + SUB] = rows[row % TILE : row % TILE + SUB]
    outer = np.concatenate([cols[:HALO], cols[TILE - HALO :]])
    return jnp.asarray(rows.T, F32), jnp.asarray(cols, F32), split_constant(placed.T, 1), split_constant(outer, 0)


def pick_kernel(owners, every, out):
    mine = out.shape[1]
    own = lax.axis_index("own")
    wanted = [owners[pl.ds(own, 1), k : k + 1].astype(F32) for k in range(mine)]
    lines = SUB + 1
    devices = every.shape[0] // lines
    chunk = min(4, devices // SUB)

    def body(d, sums):
        sums = list(sums)
        for e in range(chunk):
            base = (d * chunk + e) * SUB * lines
            mark = every[pl.ds(base + SUB, SUB, stride=lines), :]
            hits = [mark == wanted[k] for k in range(mine)]
            for r in range(SUB):
                part = every[pl.ds(base + r, SUB, stride=lines), :]
                for k in range(mine):
                    sums[SUB * k + r] += jnp.where(hits[k], part, 0.0)
        return tuple(sums)

    start = (jnp.zeros((SUB, TILE), F32),) * (mine * SUB)
    sums = lax.fori_loop(0, devices // SUB // chunk, body, start)
    for k in range(mine):
        for r in range(SUB):
            total = jnp.sum(sums[SUB * k + r], axis=0, keepdims=True)
            out[0, k : k + 1, TILE * r : TILE * (r + 1)] = total


def local(viscosity, friction, driving, observed, ice_mask, tile_block, owner_list):
    rows, cols = viscosity.shape
    assert (rows, cols) == (2 * TILE, TILE)
    inputs = (viscosity, friction, driving, ice_mask, observed)
    near = [pltpu.with_memory_space_constraint(x, pltpu.VMEM) for x in inputs]
    basis_p, basis_q, basis_rows, basis_cols = bases()
    to_b, to_a = call(
        ends_kernel,
        "ends",
        (vmem(EDGE, cols), vmem(EDGE, cols)),
        [
            vmem(2, 2, HALO, cols),
            vmem(2, 2, 2, HALO, cols),
            pltpu.VMEM((2, HALO, cols), jnp.int32),
            pltpu.SemaphoreType.DMA((2, 5)),
        ],
        10**6,
        *(pltpu.with_memory_space_constraint(x, pltpu.HBM) for x in inputs),
    )
    row_b = swap(to_b, 0, 1)
    row_a = swap(to_a, 0, 0)
    edge, *forward = call(
        interior_kernel,
        "interior",
        (vmem(2 * PARTS * TILE, TILE),) + (vmem(rows, cols),) * 6,
        [vmem(rows, cols)] * (FIELDS - 6),
        8 * 10**6,
        *near,
    )
    to_b, to_a, turned = call(
        columns_kernel,
        "columns",
        (vmem(SENT, TILE), vmem(SENT, TILE), vmem(SLOT, TILE)),
        [],
        10**5,
        row_b,
        row_a,
        edge,
    )
    col_b = swap(to_b, 1, 1)
    col_a = swap(to_a, 1, 0)
    vel_ends, wide, sides, seams = call(
        adjoint_kernel,
        "adjoint",
        (
            vmem(4 * HALO, cols),
            vmem(MODES, TILE),
            vmem(PARTS * ARRAYS * STRIP, TILE),
            vmem(PARTS * SUB, TILE),
        ),
        [vmem(ARRAYS * STRIP, cols), vmem(2 * STRIP, cols), vmem(rows + STRIP, cols), vmem(TILE, cols)]
        + [vmem(STRIP, cols)] * STRIP_FIELDS
        + [vmem(rows, cols)] * (FIELDS - 4),
        8 * 10**6,
        row_b,
        row_a,
        *near,
        *forward,
        basis_p,
        basis_q,
        edge,
        turned,
    )
    devices = lax.axis_size(ROW_AXES + COL_AXES)
    _, strips, coef = call(
        left_right_kernel,
        "left_right",
        (
            vmem(PARTS * ARRAYS * STRIP, TILE),
            vmem(PARTS * 2 * STRIP, TILE),
            vmem(devices * (SUB + 1), TILE),
        ),
        [vmem(PARTS * STRIP, TILE)] * (STRIP_FIELDS + 1),
        4 * 10**6,
        sides,
        seams,
        col_b,
        col_a,
        wide,
        tile_block,
        basis_rows,
        basis_cols,
        aliases={0: 0},
    )
    coef = coef.reshape(devices, 1, (SUB + 1) * TILE)
    parts = lax.all_to_all(coef, ROW_AXES + COL_AXES, 0, 0, tiled=True)
    state = call(
        join_kernel,
        "join",
        jax.ShapeDtypeStruct((2, rows, cols), F32),
        [vmem(2 * PARTS * TILE, TILE)],
        4 * 10**6,
        *forward[4:],
        vel_ends,
        strips,
    )
    owners = owner_list.reshape(lax.axis_size("own"), -1)
    picked = call(
        pick_kernel,
        "pick",
        jax.ShapeDtypeStruct((1, owners.shape[1], MODES * MODES), F32),
        [],
        10**5,
        owners,
        parts.reshape(-1, TILE),
    )
    return (state, picked)


def solution(mesh):
    return jax.shard_map(
        local,
        mesh=mesh,
        in_specs=(
            P(("row", "own"), "col"),
            P(("row", "own"), "col"),
            P(None, ("row", "own"), "col"),
            P(None, ("row", "own"), "col"),
            P(("row", "own"), "col"),
            P(("row", "own"), "col"),
            P(),
        ),
        out_specs=(P(None, ("row", "own"), "col"), P("own", None, None)),
        check_vma=False,
    )
```

profile of v0, /device:TPU:0, one launch (start us, length us, event | category | flops | bytes accessed | tf_op | source)
XLA Modules:
  0.0 28.8 jit_solution(4675373545241303003)
XLA Ops:
  0.6 0.0 copy-start.2
  0.6 0.0 copy-start.3
  0.7 0.0 copy-start
  0.7 0.0 copy-start.1
  0.7 0.0 copy-start.4
  0.7 1.4 %ends.1 = (f32[56,128]{1,0:T(8,128)S(1)}, f32[56,128]{1,0:T(8,128)S(1)}) custom-call(f32[256,128]{1,0:T(8,128)} %visc.5, f32[256,128]{1,0:T(8,128)} %fric.5, f32[2,256,128]{2,1,0:T(8,128)} %driv.5, s32[256,128]{1,0:T(8,128)} %mask.5, f32[2,256,128]{2,1,0:T(8,128)} %obs.5), custom_call_target="tpu_custom_call" | custom-call | flops 1000000 | bytes 1000000 | tf_op jit(solution)/shard_map/ends/pallas_call | solution.py:74
  2.1 3.1 %collective-permute-start = (f32[56,128]{1,0:T(8,128)S(1)}, f32[56,128]{1,0:T(8,128)S(1)}, u32[]{:S(2)}, u32[]{:S(2)}) collective-permute-start(f32[56,128]{1,0:T(8,128)S(1)} %get-tuple-element.22), channel_id=1, source_target_pairs={{0,4},{4,0},{8,12},{12,8},{1,2},{5,6},{9,10},{13,14},{2,1},{6,5},{... | collective-permute-start | bytes 86024 | tf_op jit(solution)/shard_map/ppermute | solution.py:53
  5.2 0.0 collective-permute-start.1
  5.3 0.0 copy-done.2
  5.3 0.0 copy-done.4
  5.3 2.1 %interior.1 = (f32[768,128]{1,0:T(8,128)S(1)}, f32[256,128]{1,0:T(8,128)S(1)}, f32[256,128]{1,0:T(8,128)S(1)}, f32[256,128]{1,0:T(8,128)S(1)}, f32[256,128]{1,0:...) custom-call(f32[256,128]{1,0:T(8,128)S(1)} %copy-done.2, f32[256,128]{1,0:T(8,128)S(1)} %copy-done.3, ...), custom_call_target="tpu_custom_call" | custom-call | flops 8000000 | bytes 8000000 | tf_op jit(solution)/shard_map/interior/pallas_call | solution.py:74
  7.4 0.0 collective-permute-done.row_b
  7.4 0.0 collective-permute-done.1.row_a
  7.4 0.0 copy-start.10
  7.4 0.0 copy-start.5
  7.4 0.1 columns.1
  7.5 0.0 copy-start.7
  7.5 0.5 %collective-permute-start.2 = (f32[88,128]{1,0:T(8,128)S(1)}, f32[88,128]{1,0:T(8,128)S(1)}, u32[]{:S(2)}, u32[]{:S(2)}) collective-permute-start(f32[88,128]{1,0:T(8,128)S(1)} %get-tuple-element.33), channel_id=1, source_target_pairs={{0,1},{4,8},{8,4},{12,13},{1,0},{5,9},{9,5},{13,12},{2,3},{6,10},{... | collective-permute-start | bytes 135176 | tf_op jit(solution)/shard_map/ppermute | solution.py:53
  8.1 2.8 %collective-permute-start.3 = (f32[88,128]{1,0:T(8,128)S(1)}, f32[88,128]{1,0:T(8,128)S(1)}, u32[]{:S(2)}, u32[]{:S(2)}) collective-permute-start(f32[88,128]{1,0:T(8,128)S(1)} %get-tuple-element.34), channel_id=1, source_target_pairs={{0,4},{4,0},{8,12},{12,8},{1,5},{5,1},{9,13},{13,9},{2,6},{6,2},{1... | collective-permute-start | bytes 135176 | tf_op jit(solution)/shard_map/ppermute | solution.py:53
  10.9 0.1 copy.15.block
  11.0 0.0 copy-done.5
  11.0 0.0 copy-start.8
  11.0 2.2 %adjoint.1 = (f32[32,128]{1,0:T(8,128)S(1)}, f32[32,128]{1,0:T(8,128)S(1)}, f32[840,128]{1,0:T(8,128)S(1)}, f32[24,128]{1,0:T(8,128)S(1)}) custom-call(f32[56,128]{1,0:T(8,128)S(1)} %collective-permute-done.row_b, f32[56,128]{1,0:T(8,128)S(1)} %collective-permute-done.1.row_a, f32[256,128]{1,0:T(8,128)S(1)} %copy-done.2, f32[256,128]{1,0:T(8,128)S(1)} %copy-done.3, ...), custom_call_target="tpu_custom_call" | custom-call | flops 8000000 | bytes 8000000 | tf_op jit(solution)/shard_map/adjoint/pallas_call | solution.py:74
  13.1 0.0 collective-permute-done.2.col_b
  13.1 0.0 collective-permute-done.3.col_a
  13.2 2.0 %left_right.1 = (f32[840,128]{1,0:T(8,128)S(1)}, f32[240,128]{1,0:T(8,128)S(1)}, f32[288,128]{1,0:T(8,128)}) custom-call(f32[840,128]{1,0:T(8,128)S(1)} %get-tuple-element.31._, f32[24,128]{1,0:T(8,128)S(1)} %get-tuple-element.32.seams, f32[88,128]{1,0:T(8,128)S(1)} %collective-permute-done.2.col_b, ...), custom_call_target="tpu_custom_call", output_to_operand_aliasing={{0}: (0, {})} | custom-call | flops 4000000 | bytes 4000000 | tf_op jit(solution)/shard_map/left_right/pallas_call | solution.py:74
  15.2 4.2 %all-to-all-start = ((f32[32,1,1152]{2,1,0:T(1,128)}), f32[32,1,1152]{2,1,0:T(1,128)S(1)}, u32[]{:S(2)}, u32[]{:S(2)}) async-start(f32[32,1,1152]{2,1,0:T(1,128)} %bitcast), calls=%async_computation | async-start | bytes 294912 | tf_op jit(solution)/shard_map/all_to_all | solution.py:776
  19.4 0.0 copy-done.9
  19.4 0.1 reshape.13.owners
  19.5 0.9 %join.1 = f32[2,256,128]{2,1,0:T(8,128)} custom-call(f32[256,128]{1,0:T(8,128)S(1)} %get-tuple-element.20.v0, f32[256,128]{1,0:T(8,128)S(1)} %get-tuple-element.21.v1, f32[32,128]{1,0:T(8,128)S(1)} %get-tuple-element.30.vel_ends, f32[240,128]{1,0:T(8,128)S(1)} %get-tuple-element.36.strips), custom_call_target="tpu_custom_call" | custom-call | flops 4000000 | bytes 4000000 | tf_op jit(solution)/shard_map/join/pallas_call | solution.py:74
  20.4 7.7 %all-to-all-done = f32[32,1,1152]{2,1,0:T(1,128)S(1)} async-done(((f32[32,1,1152]{2,1,0:T(1,128)}), f32[32,1,1152]{2,1,0:T(1,128)S(1)}, u32[]{:S(2)}, u32[]{:S(2)}) %all-to-all-start) | async-done | bytes 147488 | tf_op jit(solution)/shard_map/all_to_all | solution.py:776
  28.1 0.8 %pick.1 = f32[1,4,1024]{2,1,0:T(4,128)} custom-call(s32[4,4]{1,0:T(4,128)S(1)} %reshape.13.owners, f32[288,128]{1,0:T(8,128)S(1)} %bitcast.2), custom_call_target="tpu_custom_call" | custom-call | flops 100000 | bytes 100000 | tf_op jit(solution)/shard_map/pick/pallas_call | solution.py:74
  (9 shorter events, 0.0 us)
Async XLA Ops:
  0.6 4.6 %copy-start.2 = (f32[256,128]{1,0:T(8,128)S(1)}, f32[256,128]{1,0:T(8,128)}, u32[]{:S(2)}) copy-start(f32[256,128]{1,0:T(8,128)} %visc.5) | copy-start | bytes 393220
  0.6 4.6 %copy-start.3 = (f32[256,128]{1,0:T(8,128)S(1)}, f32[256,128]{1,0:T(8,128)}, u32[]{:S(2)}) copy-start(f32[256,128]{1,0:T(8,128)} %fric.5) | copy-start | bytes 393220
  0.7 4.6 %copy-start = (f32[2,256,128]{2,1,0:T(8,128)S(1)}, f32[2,256,128]{2,1,0:T(8,128)}, u32[]{:S(2)}) copy-start(f32[2,256,128]{2,1,0:T(8,128)} %driv.5) | copy-start | bytes 786436
  0.7 4.6 %copy-start.1 = (f32[2,256,128]{2,1,0:T(8,128)S(1)}, f32[2,256,128]{2,1,0:T(8,128)}, u32[]{:S(2)}) copy-start(f32[2,256,128]{2,1,0:T(8,128)} %obs.5) | copy-start | bytes 786436
  0.7 4.6 %copy-start.4 = (s32[256,128]{1,0:T(8,128)S(1)}, s32[256,128]{1,0:T(8,128)}, u32[]{:S(2)}) copy-start(s32[256,128]{1,0:T(8,128)} %mask.5) | copy-start | bytes 393220
  2.1 5.2 %collective-permute-start = (f32[56,128]{1,0:T(8,128)S(1)}, f32[56,128]{1,0:T(8,128)S(1)}, u32[]{:S(2)}, u32[]{:S(2)}) collective-permute-start(f32[56,128]{1,0:T(8,128)S(1)} %get-tuple-element.22), channel_id=1, source_target_pairs={{0,4},{4,0},{8,12},{12,8},{1,2},{5,6},{9,10},{13,14},{2,1},{6,5},{... | collective-permute-start | bytes 86024 | tf_op jit(solution)/shard_map/ppermute | solution.py:53
  5.2 2.2 %collective-permute-start.1 = (f32[56,128]{1,0:T(8,128)S(1)}, f32[56,128]{1,0:T(8,128)S(1)}, u32[]{:S(2)}, u32[]{:S(2)}) collective-permute-start(f32[56,128]{1,0:T(8,128)S(1)} %get-tuple-element.23), channel_id=1, source_target_pairs={{0,1},{4,5},{8,9},{12,13},{1,0},{5,4},{9,8},{13,12},{2,3},{6,7},{1... | collective-permute-start | bytes 86024 | tf_op jit(solution)/shard_map/ppermute | solution.py:53
  7.4 3.5 %copy-start.10 = (s32[2,1]{0,1:T(1,128)S(1)}, s32[2,1]{0,1:T(1,128)}, u32[]{:S(2)}) copy-start(s32[2,1]{0,1:T(1,128)} %param.16) | copy-start | bytes 28
  7.4 3.6 %copy-start.5 = (f32[128,128]{1,0:T(8,128)S(1)}, f32[128,128]{1,0:T(8,128)}, u32[]{:S(2)}) copy-start(f32[128,128]{1,0:T(8,128)} %constant.9.clone.basis_q) | copy-start | bytes 196612
  7.5 3.5 %copy-start.7 = (f32[32,128]{1,0:T(8,128)S(1)}, f32[32,128]{1,0:T(8,128)}, u32[]{:S(2)}) copy-start(f32[32,128]{1,0:T(8,128)} %constant.8.clone.basis_p) | copy-start | bytes 49156
  7.5 5.6 %collective-permute-start.2 = (f32[88,128]{1,0:T(8,128)S(1)}, f32[88,128]{1,0:T(8,128)S(1)}, u32[]{:S(2)}, u32[]{:S(2)}) collective-permute-start(f32[88,128]{1,0:T(8,128)S(1)} %get-tuple-element.33), channel_id=1, source_target_pairs={{0,1},{4,8},{8,4},{12,13},{1,0},{5,9},{9,5},{13,12},{2,3},{6,10},{... | collective-permute-start | bytes 135176 | tf_op jit(solution)/shard_map/ppermute | solution.py:53
  8.1 5.1 %collective-permute-start.3 = (f32[88,128]{1,0:T(8,128)S(1)}, f32[88,128]{1,0:T(8,128)S(1)}, u32[]{:S(2)}, u32[]{:S(2)}) collective-permute-start(f32[88,128]{1,0:T(8,128)S(1)} %get-tuple-element.34), channel_id=1, source_target_pairs={{0,4},{4,0},{8,12},{12,8},{1,5},{5,1},{9,13},{13,9},{2,6},{6,2},{1... | collective-permute-start | bytes 135176 | tf_op jit(solution)/shard_map/ppermute | solution.py:53
  11.0 2.2 %copy-start.6 = (bf16[32,768]{1,0:T(8,128)(2,1)S(1)}, bf16[32,768]{1,0:T(8,128)(2,1)}, u32[]{:S(2)}) copy-start(bf16[32,768]{1,0:T(8,128)(2,1)} %constant.10.clone.basis_rows) | copy-start | bytes 147460
  11.0 2.2 %copy-start.8 = (bf16[48,128]{1,0:T(8,128)(2,1)S(1)}, bf16[48,128]{1,0:T(8,128)(2,1)}, u32[]{:S(2)}) copy-start(bf16[48,128]{1,0:T(8,128)(2,1)} %constant.11.clone.basis_cols) | copy-start | bytes 36868
  15.2 4.2 %copy-start.9 = (s32[16]{0:T(128)S(1)}, s32[16]{0:T(128)}, u32[]{:S(2)}) copy-start(s32[16]{0:T(128)} %param.17) | copy-start | bytes 196
  15.2 12.8 %all-to-all-start = ((f32[32,1,1152]{2,1,0:T(1,128)}), f32[32,1,1152]{2,1,0:T(1,128)S(1)}, u32[]{:S(2)}, u32[]{:S(2)}) async-start(f32[32,1,1152]{2,1,0:T(1,128)} %bitcast), calls=%async_computation | async-start | bytes 294912 | tf_op jit(solution)/shard_map/all_to_all | solution.py:776
where the time goes:
time: 29 us; the launch traced here: 28.8 us
  starting transfers between devices  10.7 us (37%)
  Pallas kernels  9.46 us (33%)
  waiting for transfers between devices  7.68 us (26%)
  between operations  0.79 us (3%)
    pallas_call x7, Pallas kernels, call(): pl.pallas_call(kernel, out_shape=outs, scratch_shapes=scratch, input_outp...  9.46 us
    all_to_all x1, waiting for transfers between devices, local(): parts = lax.all_to_all(coef, ROW_AXES + COL_AXES, 0, 0, tiled=True)  7.67 us
    ppermute x4, starting transfers between devices, swap(): return lax.ppermute(x, ('row', 'col', 'own'), pairs)  6.46 us
    all_to_all x1, starting transfers between devices, local(): parts = lax.all_to_all(coef, ROW_AXES + COL_AXES, 0, 0, tiled=True)  4.2 us
  transfers between devices with their start and end apart: 5, of which 1 were waited for; matrix products, arithmetic and copies ran while one was open for 1% of the time, Pallas kernels for 18%

commit v1 on v0

--- a/solution.py
+++ b/solution.py
@@ -773,7 +773,9 @@
         aliases={0: 0},
     )
     coef = coef.reshape(devices, 1, (SUB + 1) * TILE)
-    parts = lax.all_to_all(coef, ROW_AXES + COL_AXES, 0, 0, tiled=True)
+    first = (lax.axis_size(COL_AXES) - 1) // 2 * lax.axis_size("own") + 1
+    members = [(first + k) % devices for k in range(devices)]
+    parts = lax.all_to_all(coef, ("row", "col", "own"), 0, 0, axis_index_groups=[members], tiled=True)
     state = call(
         join_kernel,
         "join",

time: 29 us -> 28.8 us (level)
  no operation moved by 1% of the time
where the time goes in v1:
time: 28.8 us; the launch traced here: 28.6 us
  starting transfers between devices  10.7 us (37%)
  Pallas kernels  9.46 us (33%)
  waiting for transfers between devices  7.47 us (26%)
  between operations  0.79 us (3%)
    pallas_call x7, Pallas kernels, call(): pl.pallas_call(kernel, out_shape=outs, scratch_shapes=scratch, input_outp...  9.46 us
    all_to_all x1, waiting for transfers between devices, local(): lax.all_to_all(coef, ('row', 'col', 'own'), 0, 0, axis_index_groups=[memb...  7.46 us
    ppermute x4, starting transfers between devices, swap(): return lax.ppermute(x, ('row', 'col', 'own'), pairs)  6.46 us
    all_to_all x1, starting transfers between devices, local(): lax.all_to_all(coef, ('row', 'col', 'own'), 0, 0, axis_index_groups=[memb...  4.2 us
  transfers between devices with their start and end apart: 5, of which 1 were waited for; matrix products, arithmetic and copies ran while one was open for 1% of the time, Pallas kernels for 18%

profile of v1, /device:TPU:0, one launch (start us, length us, event | category | flops | bytes accessed | tf_op | source)
XLA Modules:
  0.0 28.6 jit_solution(6968775775077703556)
XLA Ops:
  0.6 0.0 copy-start.2
  0.6 0.0 copy-start.3
  0.7 0.0 copy-start
  0.7 0.0 copy-start.1
  0.7 0.0 copy-start.4
  0.7 1.4 %ends.1 = (f32[56,128]{1,0:T(8,128)S(1)}, f32[56,128]{1,0:T(8,128)S(1)}) custom-call(f32[256,128]{1,0:T(8,128)} %visc.5, f32[256,128]{1,0:T(8,128)} %fric.5, f32[2,256,128]{2,1,0:T(8,128)} %driv.5, s32[256,128]{1,0:T(8,128)} %mask.5, f32[2,256,128]{2,1,0:T(8,128)} %obs.5), custom_call_target="tpu_custom_call" | custom-call | flops 1000000 | bytes 1000000 | tf_op jit(solution)/shard_map/ends/pallas_call | solution.py:74
  2.1 3.1 %collective-permute-start = (f32[56,128]{1,0:T(8,128)S(1)}, f32[56,128]{1,0:T(8,128)S(1)}, u32[]{:S(2)}, u32[]{:S(2)}) collective-permute-start(f32[56,128]{1,0:T(8,128)S(1)} %get-tuple-element.22), channel_id=1, source_target_pairs={{0,4},{4,0},{8,12},{12,8},{1,2},{5,6},{9,10},{13,14},{2,1},{6,5},{... | collective-permute-start | bytes 86024 | tf_op jit(solution)/shard_map/ppermute | solution.py:53
  5.2 0.0 collective-permute-start.1
  5.3 0.0 copy-done.3
  5.3 2.1 %interior.1 = (f32[768,128]{1,0:T(8,128)S(1)}, f32[256,128]{1,0:T(8,128)S(1)}, f32[256,128]{1,0:T(8,128)S(1)}, f32[256,128]{1,0:T(8,128)S(1)}, f32[256,128]{1,0:...) custom-call(f32[256,128]{1,0:T(8,128)S(1)} %copy-done.2, f32[256,128]{1,0:T(8,128)S(1)} %copy-done.3, ...), custom_call_target="tpu_custom_call" | custom-call | flops 8000000 | bytes 8000000 | tf_op jit(solution)/shard_map/interior/pallas_call | solution.py:74
  7.4 0.0 collective-permute-done.row_b
  7.4 0.0 collective-permute-done.1.row_a
  7.4 0.0 copy-start.10
  7.4 0.0 copy-start.5
  7.4 0.1 columns.1
  7.5 0.0 copy-start.7
  7.5 0.5 %collective-permute-start.2 = (f32[88,128]{1,0:T(8,128)S(1)}, f32[88,128]{1,0:T(8,128)S(1)}, u32[]{:S(2)}, u32[]{:S(2)}) collective-permute-start(f32[88,128]{1,0:T(8,128)S(1)} %get-tuple-element.33), channel_id=1, source_target_pairs={{0,1},{4,8},{8,4},{12,13},{1,0},{5,9},{9,5},{13,12},{2,3},{6,10},{... | collective-permute-start | bytes 135176 | tf_op jit(solution)/shard_map/ppermute | solution.py:53
  8.1 2.8 %collective-permute-start.3 = (f32[88,128]{1,0:T(8,128)S(1)}, f32[88,128]{1,0:T(8,128)S(1)}, u32[]{:S(2)}, u32[]{:S(2)}) collective-permute-start(f32[88,128]{1,0:T(8,128)S(1)} %get-tuple-element.34), channel_id=1, source_target_pairs={{0,4},{4,0},{8,12},{12,8},{1,5},{5,1},{9,13},{13,9},{2,6},{6,2},{1... | collective-permute-start | bytes 135176 | tf_op jit(solution)/shard_map/ppermute | solution.py:53
  10.9 0.1 copy.15.block
  11.0 0.0 copy-done.7
  11.0 0.0 copy-start.8
  11.0 2.2 %adjoint.1 = (f32[32,128]{1,0:T(8,128)S(1)}, f32[32,128]{1,0:T(8,128)S(1)}, f32[840,128]{1,0:T(8,128)S(1)}, f32[24,128]{1,0:T(8,128)S(1)}) custom-call(f32[56,128]{1,0:T(8,128)S(1)} %collective-permute-done.row_b, f32[56,128]{1,0:T(8,128)S(1)} %collective-permute-done.1.row_a, f32[256,128]{1,0:T(8,128)S(1)} %copy-done.2, f32[256,128]{1,0:T(8,128)S(1)} %copy-done.3, ...), custom_call_target="tpu_custom_call" | custom-call | flops 8000000 | bytes 8000000 | tf_op jit(solution)/shard_map/adjoint/pallas_call | solution.py:74
  13.1 0.0 collective-permute-done.2.col_b
  13.1 0.0 collective-permute-done.3.col_a
  13.1 0.0 copy-done.6
  13.2 0.0 copy-done.8
  13.2 2.0 %left_right.1 = (f32[840,128]{1,0:T(8,128)S(1)}, f32[240,128]{1,0:T(8,128)S(1)}, f32[288,128]{1,0:T(8,128)}) custom-call(f32[840,128]{1,0:T(8,128)S(1)} %get-tuple-element.31._, f32[24,128]{1,0:T(8,128)S(1)} %get-tuple-element.32.seams, f32[88,128]{1,0:T(8,128)S(1)} %collective-permute-done.2.col_b, ...), custom_call_target="tpu_custom_call", output_to_operand_aliasing={{0}: (0, {})} | custom-call | flops 4000000 | bytes 4000000 | tf_op jit(solution)/shard_map/left_right/pallas_call | solution.py:74
  15.2 4.2 %all-to-all-start = ((f32[32,1,1152]{2,1,0:T(1,128)}), f32[32,1,1152]{2,1,0:T(1,128)S(1)}, u32[]{:S(2)}, u32[]{:S(2)}) async-start(f32[32,1,1152]{2,1,0:T(1,128)} %bitcast), calls=%async_computation | async-start | bytes 294912 | tf_op jit(solution)/shard_map/all_to_all | solution.py:778
  19.4 0.1 reshape.13.owners
  19.5 0.9 %join.1 = f32[2,256,128]{2,1,0:T(8,128)} custom-call(f32[256,128]{1,0:T(8,128)S(1)} %get-tuple-element.20.v0, f32[256,128]{1,0:T(8,128)S(1)} %get-tuple-element.21.v1, f32[32,128]{1,0:T(8,128)S(1)} %get-tuple-element.30.vel_ends, f32[240,128]{1,0:T(8,128)S(1)} %get-tuple-element.36.strips), custom_call_target="tpu_custom_call" | custom-call | flops 4000000 | bytes 4000000 | tf_op jit(solution)/shard_map/join/pallas_call | solution.py:74
  20.4 7.5 %all-to-all-done = f32[32,1,1152]{2,1,0:T(1,128)S(1)} async-done(((f32[32,1,1152]{2,1,0:T(1,128)}), f32[32,1,1152]{2,1,0:T(1,128)S(1)}, u32[]{:S(2)}, u32[]{:S(2)}) %all-to-all-start) | async-done | bytes 147488 | tf_op jit(solution)/shard_map/all_to_all | solution.py:778
  27.8 0.8 %pick.1 = f32[1,4,1024]{2,1,0:T(4,128)} custom-call(s32[4,4]{1,0:T(4,128)S(1)} %reshape.13.owners, f32[288,128]{1,0:T(8,128)S(1)} %bitcast.2), custom_call_target="tpu_custom_call" | custom-call | flops 100000 | bytes 100000 | tf_op jit(solution)/shard_map/pick/pallas_call | solution.py:74
  (9 shorter events, 0.0 us)
Async XLA Ops:
  0.6 4.6 %copy-start.2 = (f32[256,128]{1,0:T(8,128)S(1)}, f32[256,128]{1,0:T(8,128)}, u32[]{:S(2)}) copy-start(f32[256,128]{1,0:T(8,128)} %visc.5) | copy-start | bytes 393220
  0.6 4.6 %copy-start.3 = (f32[256,128]{1,0:T(8,128)S(1)}, f32[256,128]{1,0:T(8,128)}, u32[]{:S(2)}) copy-start(f32[256,128]{1,0:T(8,128)} %fric.5) | copy-start | bytes 393220
  0.7 4.6 %copy-start = (f32[2,256,128]{2,1,0:T(8,128)S(1)}, f32[2,256,128]{2,1,0:T(8,128)}, u32[]{:S(2)}) copy-start(f32[2,256,128]{2,1,0:T(8,128)} %driv.5) | copy-start | bytes 786436
  0.7 4.6 %copy-start.1 = (f32[2,256,128]{2,1,0:T(8,128)S(1)}, f32[2,256,128]{2,1,0:T(8,128)}, u32[]{:S(2)}) copy-start(f32[2,256,128]{2,1,0:T(8,128)} %obs.5) | copy-start | bytes 786436
  0.7 4.6 %copy-start.4 = (s32[256,128]{1,0:T(8,128)S(1)}, s32[256,128]{1,0:T(8,128)}, u32[]{:S(2)}) copy-start(s32[256,128]{1,0:T(8,128)} %mask.5) | copy-start | bytes 393220
  2.1 5.2 %collective-permute-start = (f32[56,128]{1,0:T(8,128)S(1)}, f32[56,128]{1,0:T(8,128)S(1)}, u32[]{:S(2)}, u32[]{:S(2)}) collective-permute-start(f32[56,128]{1,0:T(8,128)S(1)} %get-tuple-element.22), channel_id=1, source_target_pairs={{0,4},{4,0},{8,12},{12,8},{1,2},{5,6},{9,10},{13,14},{2,1},{6,5},{... | collective-permute-start | bytes 86024 | tf_op jit(solution)/shard_map/ppermute | solution.py:53
  5.2 2.2 %collective-permute-start.1 = (f32[56,128]{1,0:T(8,128)S(1)}, f32[56,128]{1,0:T(8,128)S(1)}, u32[]{:S(2)}, u32[]{:S(2)}) collective-permute-start(f32[56,128]{1,0:T(8,128)S(1)} %get-tuple-element.23), channel_id=1, source_target_pairs={{0,1},{4,5},{8,9},{12,13},{1,0},{5,4},{9,8},{13,12},{2,3},{6,7},{1... | collective-permute-start | bytes 86024 | tf_op jit(solution)/shard_map/ppermute | solution.py:53
  7.4 3.5 %copy-start.10 = (s32[2,1]{0,1:T(1,128)S(1)}, s32[2,1]{0,1:T(1,128)}, u32[]{:S(2)}) copy-start(s32[2,1]{0,1:T(1,128)} %param.16) | copy-start | bytes 28
  7.4 3.6 %copy-start.5 = (f32[128,128]{1,0:T(8,128)S(1)}, f32[128,128]{1,0:T(8,128)}, u32[]{:S(2)}) copy-start(f32[128,128]{1,0:T(8,128)} %constant.9.clone.basis_q) | copy-start | bytes 196612
  7.5 3.5 %copy-start.7 = (f32[32,128]{1,0:T(8,128)S(1)}, f32[32,128]{1,0:T(8,128)}, u32[]{:S(2)}) copy-start(f32[32,128]{1,0:T(8,128)} %constant.8.clone.basis_p) | copy-start | bytes 49156
  7.5 5.6 %collective-permute-start.2 = (f32[88,128]{1,0:T(8,128)S(1)}, f32[88,128]{1,0:T(8,128)S(1)}, u32[]{:S(2)}, u32[]{:S(2)}) collective-permute-start(f32[88,128]{1,0:T(8,128)S(1)} %get-tuple-element.33), channel_id=1, source_target_pairs={{0,1},{4,8},{8,4},{12,13},{1,0},{5,9},{9,5},{13,12},{2,3},{6,10},{... | collective-permute-start | bytes 135176 | tf_op jit(solution)/shard_map/ppermute | solution.py:53
  8.1 5.1 %collective-permute-start.3 = (f32[88,128]{1,0:T(8,128)S(1)}, f32[88,128]{1,0:T(8,128)S(1)}, u32[]{:S(2)}, u32[]{:S(2)}) collective-permute-start(f32[88,128]{1,0:T(8,128)S(1)} %get-tuple-element.34), channel_id=1, source_target_pairs={{0,4},{4,0},{8,12},{12,8},{1,5},{5,1},{9,13},{13,9},{2,6},{6,2},{1... | collective-permute-start | bytes 135176 | tf_op jit(solution)/shard_map/ppermute | solution.py:53
  11.0 2.2 %copy-start.6 = (bf16[32,768]{1,0:T(8,128)(2,1)S(1)}, bf16[32,768]{1,0:T(8,128)(2,1)}, u32[]{:S(2)}) copy-start(bf16[32,768]{1,0:T(8,128)(2,1)} %constant.10.clone.basis_rows) | copy-start | bytes 147460
  11.0 2.2 %copy-start.8 = (bf16[48,128]{1,0:T(8,128)(2,1)S(1)}, bf16[48,128]{1,0:T(8,128)(2,1)}, u32[]{:S(2)}) copy-start(bf16[48,128]{1,0:T(8,128)(2,1)} %constant.11.clone.basis_cols) | copy-start | bytes 36868
  15.2 4.2 %copy-start.9 = (s32[16]{0:T(128)S(1)}, s32[16]{0:T(128)}, u32[]{:S(2)}) copy-start(s32[16]{0:T(128)} %param.17) | copy-start | bytes 196
  15.2 12.6 %all-to-all-start = ((f32[32,1,1152]{2,1,0:T(1,128)}), f32[32,1,1152]{2,1,0:T(1,128)S(1)}, u32[]{:S(2)}, u32[]{:S(2)}) async-start(f32[32,1,1152]{2,1,0:T(1,128)} %bitcast), calls=%async_computation | async-start | bytes 294912 | tf_op jit(solution)/shard_map/all_to_all | solution.py:778

commit v2 on v0

--- a/solution.py
+++ b/solution.py
@@ -19,6 +19,7 @@
 KEPT = 12
 OUTER = (LEAD, STRIP - 2 * HALO)
 NEAR, FAR = 7, 6
+PADDED = 48
 ARRAYS = 7
 VISC, FRIC, DRIV, MASK, OBS = 0, 1, 2, 4, 5
 EDGE = ARRAYS * HALO
@@ -34,22 +35,34 @@
 LIMIT = 40 * 1024 * 1024
 
 
-def swap(x, axis, first):
-    sizes = lax.axis_size(ROW_AXES), lax.axis_size(COL_AXES)
-    owners = lax.axis_size("own")
+def swap_rows(x, first):
+    def partner(i, j, rows, cols):
+        if first and i in (0, rows - 1):
+            return i, j ^ 1
+        return ((i + first) ^ 1) - first, j
+
+    return exchange(x, partner)
+
+
+def swap_cols(x, first):
+    def partner(i, j, rows, cols):
+        offset = first ^ (i % 2 == 0)
+        if offset and j in (0, cols - 1):
+            return i ^ 2, j
+        return i, ((j + offset) ^ 1) - offset
+
+    return exchange(x, partner)
+
+
+def exchange(x, partner):
+    rows, cols, owners = lax.axis_size(ROW_AXES), lax.axis_size(COL_AXES), lax.axis_size("own")
 
     def device(i, j):
-        return (i // owners * sizes[1] + j) * owners + i % owners
-
-    pairs = []
-    for i in range(sizes[0]):
-        for j in range(sizes[1]):
-            place = [i, j]
-            if first and place[axis] in (0, sizes[axis] - 1):
-                place[1 - axis] ^= 1
-            else:
-                place[axis] = ((place[axis] + first) ^ 1) - first
-            pairs.append((device(i, j), device(*place)))
+        return (i // owners * cols + j) * owners + i % owners
+
+    pairs = [
+        (device(i, j), device(*partner(i, j, rows, cols))) for i in range(rows) for j in range(cols)
+    ]
     return lax.ppermute(x, ("row", "col", "own"), pairs)
 
 
@@ -364,13 +377,14 @@
     halo = jnp.concatenate([above, below, jnp.zeros((TILE - 2 * EDGE, TILE), F32)], axis=0).T
     turned[:INNER, :] = halo[TILE - INNER :]
     turned[INNER:, :] = halo[:INNER]
-    even, at_end = position(COL_AXES)
+    row_even, (col_even, at_end) = even, position(COL_AXES)
+    even = row_even != col_even
     row = lax.broadcasted_iota(jnp.int32, (SUB, TILE), 0)
 
     def put(out, right, left):
         right = pltpu.roll(right, LEAD, 0)
-        to_a[out : out + HALO, :] = jnp.where(even, right, left)
-        to_b[out : out + HALO, :] = jnp.where(at_end, 0.0, jnp.where(even, left, right))
+        to_a[out : out + HALO, :] = jnp.where(at_end & row_even, 0.0, jnp.where(even, right, left))
+        to_b[out : out + HALO, :] = jnp.where(at_end & ~row_even, 0.0, jnp.where(even, left, right))
 
     for part in range(2):
         right, left = [], []
@@ -410,13 +424,11 @@
             plain[pl.ds(base + STRIP * k + j, SUB, stride=domain.span), :] = domain.refs[6 + k][at, :]
 
 
-def density(domain, plain, base, out, place):
-    w0, w1 = domain.refs[6:8]
-    for j in range(domain.span):
-        at = domain.at(j)
-        v0, v1 = (plain[pl.ds(base + STRIP * k + j, SUB, stride=domain.span), :] for k in range(2))
-        value = -domain.source(FRIC, j) * (w0[at, :] * v0 + w1[at, :] * v1)
-        out[pl.ds(place + j, SUB, stride=domain.span), :] = value
+def density(domain, plain, base, j):
+    at = domain.at(j)
+    w0, w1 = (w[at, :] for w in domain.refs[6:8])
+    v0, v1 = (plain[pl.ds(base + STRIP * k + j, SUB, stride=domain.span), :] for k in range(2))
+    return -domain.source(FRIC, j) * (w0 * v0 + w1 * v1)
 
 
 def beside():
@@ -466,7 +478,8 @@
         at = interior.at(j)
         value = -interior.source(FRIC, j) * (w0[at, :] * v0[at, :] + w1[at, :] * v1[at, :])
         dens[pl.ds(j, SUB, stride=span), :] = value
-    density(strips, plain, 0, dens, rows)
+    for j in range(strips.span):
+        dens[pl.ds(rows + j, SUB, stride=strips.span), :] = density(strips, plain, 0, j)
 
     side = beside()
     for s in range(0, TILE, SUB):
@@ -523,9 +536,9 @@
 def left_right_kernel(
     _, seams, col_b, col_a, wide_in, block, basis_rows, basis_cols,
     stack, strips, coef,
-    plain, *refs,
+    *refs,
 ):
-    even = is_even(COL_AXES)
+    even = is_even(COL_AXES) != is_even(ROW_AXES)
     lane = lanes()
     row = lax.broadcasted_iota(jnp.int32, (SUB, TILE), 0)
     upper = (lane >= UPPER + HALO) & (lane < UPPER + SLOT)
@@ -573,40 +586,30 @@
         velocity(domain, strips, 2 * STRIP * part)
         domain.retarget(True)
     run(domains, True)
-    for part, domain in enumerate(domains):
-        density(domain, strips, 2 * STRIP * part, plain, STRIP * part)
-
-    def side(part):
-        base = STRIP * part
-        return jnp.concatenate(
-            [plain[base + at : base + at + HALO, :] for at in OUTER], axis=0
-        )
-
-    lane = lax.broadcasted_iota(jnp.int32, (2 * HALO, TILE), 1)
-    row = lax.broadcasted_iota(jnp.int32, (2 * HALO, TILE), 0)
-    right = (row < NEAR) | (row >= 2 * HALO - FAR)
     straight = (lane >= HALO) & (lane < TILE - HALO)
     seam = (lane < HALO) | (lane >= TILE - HALO)
     top = (lane >= UPPER + HALO) & (lane < UPPER + 2 * HALO)
     bottom = (lane >= LOWER + INNER) & (lane < LOWER + INNER + HALO)
-    dens = jnp.concatenate(
-        [
-            jnp.where(right & straight, side(0) + side(1), 0.0),
-            jnp.where(right & (seam | top | bottom), side(2), 0.0),
-        ],
-        axis=1,
-    )
+    span = STRIP // SUB
+    dens = []
+    for j in range(span):
+        at = span * row + j
+        right = ((at >= OUTER[0]) & (at < OUTER[0] + NEAR)) | (
+            (at >= OUTER[1] + HALO - FAR) & (at < OUTER[1] + HALO)
+        )
+        value = [density(domain, strips, 2 * STRIP * part, j) for part, domain in enumerate(domains)]
+        both = jnp.where(right & straight, value[0] + value[1], 0.0)
+        dens.append(jnp.concatenate([both, jnp.where(right & (seam | top | bottom), value[2], 0.0)], axis=1))
+    dens = jnp.concatenate(dens + [jnp.zeros((PADDED - STRIP, 2 * TILE), F32)], axis=0)
     half = lax.dot_general(
         basis_rows[...], split(dens, 1), (((1,), (1,)), ((), ())), preferred_element_type=F32
     )
     wide = wide_in[...] + jnp.dot(split(half, 1), basis_cols[...], preferred_element_type=F32)
-    lane = lanes()
     which = lax.div(lane, MODES)
     flat = wide[:SUB]
     for j in range(1, MODES // SUB):
         flat = jnp.where(which == j, wide[SUB * j : SUB * (j + 1)], flat)
     mark = jnp.broadcast_to(block[:1, :].astype(F32), (SUB, TILE))
-    row = lax.broadcasted_iota(jnp.int32, (SUB, TILE), 0)
     moved = [flat] + [pltpu.roll(flat, r, 0) for r in range(1, SUB)] + [flat]
     lines = [flat] + [
         jnp.where(row < r - 1, moved[r - 1], jnp.where(row == r - 1, mark, moved[r])) for r in range(1, SUB + 1)
@@ -656,7 +659,14 @@
         part, lane = right_part(row)
         at = lane + (TILE if part == 2 else 0)
         placed[at : at + SUB] = rows[row % TILE : row % TILE + SUB]
-    outer = np.concatenate([cols[:HALO], cols[TILE - HALO :]])
+    outer = np.zeros((PADDED, TILE))
+    for j in range(STRIP // SUB):
+        for k in range(SUB):
+            at = STRIP // SUB * k + j
+            if OUTER[0] <= at < OUTER[0] + NEAR:
+                outer[SUB * j + k] = cols[at - OUTER[0]]
+            if OUTER[1] + HALO - FAR <= at < OUTER[1] + HALO:
+                outer[SUB * j + k] = cols[TILE - HALO + at - OUTER[1]]
     return jnp.asarray(rows.T, F32), jnp.asarray(cols, F32), split_constant(placed.T, 1), split_constant(outer, 0)
 
 
@@ -707,8 +717,8 @@
         10**6,
         *(pltpu.with_memory_space_constraint(x, pltpu.HBM) for x in inputs),
     )
-    row_b = swap(to_b, 0, 1)
-    row_a = swap(to_a, 0, 0)
+    row_b = swap_rows(to_b, 1)
+    row_a = swap_rows(to_a, 0)
     edge, *forward = call(
         interior_kernel,
         "interior",
@@ -727,8 +737,8 @@
         row_a,
         edge,
     )
-    col_b = swap(to_b, 1, 1)
-    col_a = swap(to_a, 1, 0)
+    col_a = swap_cols(to_a, 0)
+    col_b = swap_cols(to_b, 1)
     vel_ends, wide, sides, seams = call(
         adjoint_kernel,
         "adjoint",
@@ -760,7 +770,7 @@
             vmem(PARTS * 2 * STRIP, TILE),
             vmem(devices * (SUB + 1), TILE),
         ),
-        [vmem(PARTS * STRIP, TILE)] * (STRIP_FIELDS + 1),
+        [vmem(PARTS * STRIP, TILE)] * STRIP_FIELDS,
         4 * 10**6,
         sides,
         seams,

time: 29 us -> 29.5 us (1.017)
  waiting for transfers between devices: 7.68 us -> 8.08 us
    ppermute x4, waiting for transfers between devices: 0.01 us -> 0.41 us  [exchange(): return lax.ppermute(x, ('row', 'col', 'own'), pairs)]
    all_to_all x1, starting transfers between devices: 4.2 us -> 4.53 us  [local(): parts = lax.all_to_all(coef, ROW_AXES + COL_AXES, 0, 0, tiled=True)]
  transfers between devices with their start and end apart: 5 -> 5, of which waited for: 1 -> 2; matrix products, arithmetic and copies ran while one was open for 1% -> 1% of each run, Pallas kernels for 18% -> 17%
where the time goes in v2:
time: 29.5 us; the launch traced here: 29.3 us
  starting transfers between devices  10.8 us (37%)
  Pallas kernels  9.43 us (32%)
  waiting for transfers between devices  8.08 us (27%)
  between operations  0.77 us (3%)
    pallas_call x7, Pallas kernels, call(): pl.pallas_call(kernel, out_shape=outs, scratch_shapes=scratch, input_outp...  9.43 us
    all_to_all x1, waiting for transfers between devices, local(): parts = lax.all_to_all(coef, ROW_AXES + COL_AXES, 0, 0, tiled=True)  7.67 us
    ppermute x4, starting transfers between devices, exchange(): return lax.ppermute(x, ('row', 'col', 'own'), pairs)  6.25 us
    all_to_all x1, starting transfers between devices, local(): parts = lax.all_to_all(coef, ROW_AXES + COL_AXES, 0, 0, tiled=True)  4.53 us
  transfers between devices with their start and end apart: 5, of which 2 were waited for; matrix products, arithmetic and copies ran while one was open for 1% of the time, Pallas kernels for 17%

profile of v2, /device:TPU:0, one launch (start us, length us, event | category | flops | bytes accessed | tf_op | source)
XLA Modules:
  0.0 29.3 jit_solution(4903151148806449122)
XLA Ops:
  0.6 0.0 copy-start.2
  0.6 0.0 copy-start.3
  0.7 0.0 copy-start
  0.7 0.0 copy-start.1
  0.7 1.4 %ends.1 = (f32[56,128]{1,0:T(8,128)S(1)}, f32[56,128]{1,0:T(8,128)S(1)}) custom-call(f32[256,128]{1,0:T(8,128)} %visc.5, f32[256,128]{1,0:T(8,128)} %fric.5, f32[2,256,128]{2,1,0:T(8,128)} %driv.5, s32[256,128]{1,0:T(8,128)} %mask.5, f32[2,256,128]{2,1,0:T(8,128)} %obs.5), custom_call_target="tpu_custom_call" | custom-call | flops 1000000 | bytes 1000000 | tf_op jit(solution)/shard_map/ends/pallas_call | solution.py:87
  2.1 3.1 %collective-permute-start = (f32[56,128]{1,0:T(8,128)S(1)}, f32[56,128]{1,0:T(8,128)S(1)}, u32[]{:S(2)}, u32[]{:S(2)}) collective-permute-start(f32[56,128]{1,0:T(8,128)S(1)} %get-tuple-element.22), channel_id=1, source_target_pairs={{0,4},{4,0},{8,12},{12,8},{1,2},{5,6},{9,10},{13,14},{2,1},{6,5},{... | collective-permute-start | bytes 86024 | tf_op jit(solution)/shard_map/ppermute | solution.py:66
  5.2 0.0 collective-permute-start.1
  5.3 0.0 copy-done.2
  5.3 0.0 copy-done.4
  5.3 2.1 %interior.1 = (f32[768,128]{1,0:T(8,128)S(1)}, f32[256,128]{1,0:T(8,128)S(1)}, f32[256,128]{1,0:T(8,128)S(1)}, f32[256,128]{1,0:T(8,128)S(1)}, f32[256,128]{1,0:...) custom-call(f32[256,128]{1,0:T(8,128)S(1)} %copy-done.2, f32[256,128]{1,0:T(8,128)S(1)} %copy-done.3, ...), custom_call_target="tpu_custom_call" | custom-call | flops 8000000 | bytes 8000000 | tf_op jit(solution)/shard_map/interior/pallas_call | solution.py:87
  7.4 0.0 collective-permute-done.row_b
  7.4 0.0 collective-permute-done.1.row_a
  7.4 0.0 copy-start.10
  7.4 0.0 copy-start.5
  7.4 0.1 columns.1
  7.5 0.0 copy-start.8
  7.5 1.8 %collective-permute-start.2 = (f32[88,128]{1,0:T(8,128)S(1)}, f32[88,128]{1,0:T(8,128)S(1)}, u32[]{:S(2)}, u32[]{:S(2)}) collective-permute-start(f32[88,128]{1,0:T(8,128)S(1)} %get-tuple-element.33), channel_id=1, source_target_pairs={{0,4},{4,0},{8,12},{12,8},{1,3},{5,9},{9,5},{13,15},{2,6},{6,2},{1... | collective-permute-start | bytes 135176 | tf_op jit(solution)/shard_map/ppermute | solution.py:66
  9.3 1.4 %collective-permute-start.3 = (f32[88,128]{1,0:T(8,128)S(1)}, f32[88,128]{1,0:T(8,128)S(1)}, u32[]{:S(2)}, u32[]{:S(2)}) collective-permute-start(f32[88,128]{1,0:T(8,128)S(1)} %get-tuple-element.34), channel_id=1, source_target_pairs={{0,2},{4,8},{8,4},{12,14},{1,5},{5,1},{9,13},{13,9},{2,0},{6,10},{... | collective-permute-start | bytes 135176 | tf_op jit(solution)/shard_map/ppermute | solution.py:66
  10.7 0.0 copy-done.10
  10.7 0.1 copy.15.block
  10.8 0.0 copy-done.5
  10.8 0.0 copy-start.7
  10.8 2.2 %adjoint.1 = (f32[32,128]{1,0:T(8,128)S(1)}, f32[32,128]{1,0:T(8,128)S(1)}, f32[840,128]{1,0:T(8,128)S(1)}, f32[24,128]{1,0:T(8,128)S(1)}) custom-call(f32[56,128]{1,0:T(8,128)S(1)} %collective-permute-done.row_b, f32[56,128]{1,0:T(8,128)S(1)} %collective-permute-done.1.row_a, f32[256,128]{1,0:T(8,128)S(1)} %copy-done.2, f32[256,128]{1,0:T(8,128)S(1)} %copy-done.3, ...), custom_call_target="tpu_custom_call" | custom-call | flops 8000000 | bytes 8000000 | tf_op jit(solution)/shard_map/adjoint/pallas_call | solution.py:87
  12.9 0.0 collective-permute-done.2.col_b
  12.9 0.4 %collective-permute-done.3.col_a = f32[88,128]{1,0:T(8,128)S(1)} collective-permute-done((f32[88,128]{1,0:T(8,128)S(1)}, f32[88,128]{1,0:T(8,128)S(1)}, u32[]{:S(2)}, u32[]{:S(2)}) %collective-permute-start.3) | collective-permute-done | bytes 45088 | tf_op jit(solution)/shard_map/ppermute | solution.py:66
  13.3 0.0 copy-done.7
  13.3 2.0 %left_right.1 = (f32[840,128]{1,0:T(8,128)S(1)}, f32[240,128]{1,0:T(8,128)S(1)}, f32[288,128]{1,0:T(8,128)}) custom-call(f32[840,128]{1,0:T(8,128)S(1)} %get-tuple-element.31._, f32[24,128]{1,0:T(8,128)S(1)} %get-tuple-element.32.seams, f32[88,128]{1,0:T(8,128)S(1)} %collective-permute-done.2.col_b, ...), custom_call_target="tpu_custom_call", output_to_operand_aliasing={{0}: (0, {})} | custom-call | flops 4000000 | bytes 4000000 | tf_op jit(solution)/shard_map/left_right/pallas_call | solution.py:87
  15.4 4.5 %all-to-all-start = ((f32[32,1,1152]{2,1,0:T(1,128)}), f32[32,1,1152]{2,1,0:T(1,128)S(1)}, u32[]{:S(2)}, u32[]{:S(2)}) async-start(f32[32,1,1152]{2,1,0:T(1,128)} %bitcast), calls=%async_computation | async-start | bytes 294912 | tf_op jit(solution)/shard_map/all_to_all | solution.py:786
  19.9 0.1 reshape.13.owners
  20.0 0.9 %join.1 = f32[2,256,128]{2,1,0:T(8,128)} custom-call(f32[256,128]{1,0:T(8,128)S(1)} %get-tuple-element.20.v0, f32[256,128]{1,0:T(8,128)S(1)} %get-tuple-element.21.v1, f32[32,128]{1,0:T(8,128)S(1)} %get-tuple-element.30.vel_ends, f32[240,128]{1,0:T(8,128)S(1)} %get-tuple-element.36.strips), custom_call_target="tpu_custom_call" | custom-call | flops 4000000 | bytes 4000000 | tf_op jit(solution)/shard_map/join/pallas_call | solution.py:87
  20.9 7.7 %all-to-all-done = f32[32,1,1152]{2,1,0:T(1,128)S(1)} async-done(((f32[32,1,1152]{2,1,0:T(1,128)}), f32[32,1,1152]{2,1,0:T(1,128)S(1)}, u32[]{:S(2)}, u32[]{:S(2)}) %all-to-all-start) | async-done | bytes 147488 | tf_op jit(solution)/shard_map/all_to_all | solution.py:786
  28.5 0.8 %pick.1 = f32[1,4,1024]{2,1,0:T(4,128)} custom-call(s32[4,4]{1,0:T(4,128)S(1)} %reshape.13.owners, f32[288,128]{1,0:T(8,128)S(1)} %bitcast.2), custom_call_target="tpu_custom_call" | custom-call | flops 100000 | bytes 100000 | tf_op jit(solution)/shard_map/pick/pallas_call | solution.py:87
  (9 shorter events, 0.0 us)
Async XLA Ops:
  0.6 4.6 %copy-start.2 = (f32[256,128]{1,0:T(8,128)S(1)}, f32[256,128]{1,0:T(8,128)}, u32[]{:S(2)}) copy-start(f32[256,128]{1,0:T(8,128)} %visc.5) | copy-start | bytes 393220
  0.6 4.6 %copy-start.3 = (f32[256,128]{1,0:T(8,128)S(1)}, f32[256,128]{1,0:T(8,128)}, u32[]{:S(2)}) copy-start(f32[256,128]{1,0:T(8,128)} %fric.5) | copy-start | bytes 393220
  0.7 4.6 %copy-start = (f32[2,256,128]{2,1,0:T(8,128)S(1)}, f32[2,256,128]{2,1,0:T(8,128)}, u32[]{:S(2)}) copy-start(f32[2,256,128]{2,1,0:T(8,128)} %driv.5) | copy-start | bytes 786436
  0.7 4.6 %copy-start.1 = (f32[2,256,128]{2,1,0:T(8,128)S(1)}, f32[2,256,128]{2,1,0:T(8,128)}, u32[]{:S(2)}) copy-start(f32[2,256,128]{2,1,0:T(8,128)} %obs.5) | copy-start | bytes 786436
  0.7 4.6 %copy-start.4 = (s32[256,128]{1,0:T(8,128)S(1)}, s32[256,128]{1,0:T(8,128)}, u32[]{:S(2)}) copy-start(s32[256,128]{1,0:T(8,128)} %mask.5) | copy-start | bytes 393220
  2.1 5.2 %collective-permute-start = (f32[56,128]{1,0:T(8,128)S(1)}, f32[56,128]{1,0:T(8,128)S(1)}, u32[]{:S(2)}, u32[]{:S(2)}) collective-permute-start(f32[56,128]{1,0:T(8,128)S(1)} %get-tuple-element.22), channel_id=1, source_target_pairs={{0,4},{4,0},{8,12},{12,8},{1,2},{5,6},{9,10},{13,14},{2,1},{6,5},{... | collective-permute-start | bytes 86024 | tf_op jit(solution)/shard_map/ppermute | solution.py:66
  5.2 2.2 %collective-permute-start.1 = (f32[56,128]{1,0:T(8,128)S(1)}, f32[56,128]{1,0:T(8,128)S(1)}, u32[]{:S(2)}, u32[]{:S(2)}) collective-permute-start(f32[56,128]{1,0:T(8,128)S(1)} %get-tuple-element.23), channel_id=1, source_target_pairs={{0,1},{4,5},{8,9},{12,13},{1,0},{5,4},{9,8},{13,12},{2,3},{6,7},{1... | collective-permute-start | bytes 86024 | tf_op jit(solution)/shard_map/ppermute | solution.py:66
  7.4 3.3 %copy-start.10 = (s32[2,1]{0,1:T(1,128)S(1)}, s32[2,1]{0,1:T(1,128)}, u32[]{:S(2)}) copy-start(s32[2,1]{0,1:T(1,128)} %param.16) | copy-start | bytes 28
  7.4 3.4 %copy-start.5 = (f32[128,128]{1,0:T(8,128)S(1)}, f32[128,128]{1,0:T(8,128)}, u32[]{:S(2)}) copy-start(f32[128,128]{1,0:T(8,128)} %constant.9.clone.basis_q) | copy-start | bytes 196612
  7.5 3.2 %copy-start.8 = (f32[32,128]{1,0:T(8,128)S(1)}, f32[32,128]{1,0:T(8,128)}, u32[]{:S(2)}) copy-start(f32[32,128]{1,0:T(8,128)} %constant.8.clone.basis_p) | copy-start | bytes 49156
  7.5 5.4 %collective-permute-start.2 = (f32[88,128]{1,0:T(8,128)S(1)}, f32[88,128]{1,0:T(8,128)S(1)}, u32[]{:S(2)}, u32[]{:S(2)}) collective-permute-start(f32[88,128]{1,0:T(8,128)S(1)} %get-tuple-element.33), channel_id=1, source_target_pairs={{0,4},{4,0},{8,12},{12,8},{1,3},{5,9},{9,5},{13,15},{2,6},{6,2},{1... | collective-permute-start | bytes 135176 | tf_op jit(solution)/shard_map/ppermute | solution.py:66
  9.3 4.0 %collective-permute-start.3 = (f32[88,128]{1,0:T(8,128)S(1)}, f32[88,128]{1,0:T(8,128)S(1)}, u32[]{:S(2)}, u32[]{:S(2)}) collective-permute-start(f32[88,128]{1,0:T(8,128)S(1)} %get-tuple-element.34), channel_id=1, source_target_pairs={{0,2},{4,8},{8,4},{12,14},{1,5},{5,1},{9,13},{13,9},{2,0},{6,10},{... | collective-permute-start | bytes 135176 | tf_op jit(solution)/shard_map/ppermute | solution.py:66
  10.8 2.6 %copy-start.6 = (bf16[32,768]{1,0:T(8,128)(2,1)S(1)}, bf16[32,768]{1,0:T(8,128)(2,1)}, u32[]{:S(2)}) copy-start(bf16[32,768]{1,0:T(8,128)(2,1)} %constant.10.clone.basis_rows) | copy-start | bytes 147460
  10.8 2.6 %copy-start.7 = (bf16[144,128]{1,0:T(8,128)(2,1)S(1)}, bf16[144,128]{1,0:T(8,128)(2,1)}, u32[]{:S(2)}) copy-start(bf16[144,128]{1,0:T(8,128)(2,1)} %constant.11.clone.basis_cols) | copy-start | bytes 110596
  15.4 4.5 %copy-start.9 = (s32[16]{0:T(128)S(1)}, s32[16]{0:T(128)}, u32[]{:S(2)}) copy-start(s32[16]{0:T(128)} %param.17) | copy-start | bytes 196
  15.4 13.2 %all-to-all-start = ((f32[32,1,1152]{2,1,0:T(1,128)}), f32[32,1,1152]{2,1,0:T(1,128)S(1)}, u32[]{:S(2)}, u32[]{:S(2)}) async-start(f32[32,1,1152]{2,1,0:T(1,128)} %bitcast), calls=%async_computation | async-start | bytes 294912 | tf_op jit(solution)/shard_map/all_to_all | solution.py:786

commit v3 on v0

--- a/solution.py
+++ b/solution.py
@@ -87,7 +87,7 @@
 
 
 FIELDS = 14
-STRIP_FIELDS = 24
+STRIP_FIELDS = 16
 
 
 class Domain:
@@ -135,6 +135,10 @@
                 b[at, :] = value
                 self.write(k, at, value + value)
 
+    def sweep(self):
+        self.differences()
+        self.update()
+
     def differences(self):
         n2, n4 = self.refs[:2]
         fields = self.refs[6:10]
@@ -204,9 +208,8 @@
             for now, later in zip(self.refs[4:6], self.refs[12:14]):
                 later[at, :] = pltpu.roll(now[at, :], TILE - 1, 1)
 
-    def differences(self):
+    def sweep(self):
         fields = self.refs[6:10]
-        kept, turned, kept_next, turned_next = (self.refs[16 + 2 * k : 18 + 2 * k] for k in range(4))
 
         def corners(halves, quarters, j, here, below):
             w0, w1, r0, r1 = here
@@ -226,38 +229,28 @@
 
         top, end = load(0), load(self.span - 1)
         up = corners(*self.refs[14:16], 0, [pltpu.roll(v, 1, 0) for v in end], top)
+        bottom = [pltpu.roll(v, SUB - 1, 0) for v in top]
         here = top
         for j in range(self.span):
             at = self.at(j)
-            below = load(j + 1) if j < self.span - 1 else [pltpu.roll(v, SUB - 1, 0) for v in top]
+            below = load(j + 1) if j < self.span - 1 else bottom
             p, q, r = corners(*self.refs[:2], j, here, below)
             g, t = up[0] - p, up[1] + q
             gq, tr = up[1] - q, up[2] + r
             for k, (stay, move) in enumerate(((g - t, g + t), (gq - tr, gq + tr))):
-                kept[k][at, :] = stay
-                turned_next[k][at, :] = move
-                turned[k][at, :] = pltpu.roll(move, 1, 1)
-                kept_next[k][at, :] = pltpu.roll(stay, TILE - 1, 1)
+                changes = stay + pltpu.roll(move, 1, 1), pltpu.roll(stay, TILE - 1, 1) + move
+                for change, first, offset in zip(changes, (2, 10), (0, 2)):
+                    c, i = self.refs[first : first + 2]
+                    b = self.refs[first + 2 + k]
+                    kept = (c[at, :] * here[offset + k] + b[at, :]) - i[at, :] * change
+                    self.refs[6 + offset + k][at, :] = kept
             up, here = (p, q, r), below
-
-    def update(self):
-        for first, offset, parts in ((2, 6, (16, 18)), (10, 8, (20, 22))):
-            c, i, *b = self.refs[first : first + 4]
-            for j in range(self.span):
-                at = self.at(j)
-                cv, iv = c[at, :], i[at, :]
-                for k in range(2):
-                    w = self.refs[offset + k]
-                    change = self.refs[parts[0] + k][at, :] + self.refs[parts[1] + k][at, :]
-                    w[at, :] = (cv * w[at, :] + b[k][at, :]) - iv * change
 
 
 def run(domains, written_out=False):
     def body(_, carry):
         for domain in domains:
-            domain.differences()
-        for domain in domains:
-            domain.update()
+            domain.sweep()
         return carry
 
     if written_out:
@@ -596,10 +589,8 @@
         ],
         axis=1,
     )
-    half = lax.dot_general(
-        basis_rows[...], split(dens, 1), (((1,), (1,)), ((), ())), preferred_element_type=F32
-    )
-    wide = wide_in[...] + jnp.dot(split(half, 1), basis_cols[...], preferred_element_type=F32)
+    half = jnp.dot(split(dens, 1), basis_rows[...], preferred_element_type=F32)
+    wide = wide_in[...] + jnp.dot(split(half.T, 1), basis_cols[...], preferred_element_type=F32)
     lane = lanes()
     which = lax.div(lane, MODES)
     flat = wide[:SUB]
@@ -657,7 +648,7 @@
         at = lane + (TILE if part == 2 else 0)
         placed[at : at + SUB] = rows[row % TILE : row % TILE + SUB]
     outer = np.concatenate([cols[:HALO], cols[TILE - HALO :]])
-    return jnp.asarray(rows.T, F32), jnp.asarray(cols, F32), split_constant(placed.T, 1), split_constant(outer, 0)
+    return jnp.asarray(rows.T, F32), jnp.asarray(cols, F32), split_constant(placed, 0), split_constant(outer, 0)
 
 
 def pick_kernel(owners, every, out):

time: 29 us -> 29.1 us (level)
  no operation moved by 1% of the time
where the time goes in v3:
time: 29.1 us; the launch traced here: 28.9 us
  starting transfers between devices  10.7 us (37%)
  Pallas kernels  9.51 us (33%)
  waiting for transfers between devices  7.68 us (26%)
  between operations  0.79 us (3%)
    pallas_call x7, Pallas kernels, call(): pl.pallas_call(kernel, out_shape=outs, scratch_shapes=scratch, input_outp...  9.51 us
    all_to_all x1, waiting for transfers between devices, local(): parts = lax.all_to_all(coef, ROW_AXES + COL_AXES, 0, 0, tiled=True)  7.67 us
    ppermute x4, starting transfers between devices, swap(): return lax.ppermute(x, ('row', 'col', 'own'), pairs)  6.46 us
    all_to_all x1, starting transfers between devices, local(): parts = lax.all_to_all(coef, ROW_AXES + COL_AXES, 0, 0, tiled=True)  4.22 us
  transfers between devices with their start and end apart: 5, of which 1 were waited for; matrix products, arithmetic and copies ran while one was open for 1% of the time, Pallas kernels for 18%

profile of v3, /device:TPU:0, one launch (start us, length us, event | category | flops | bytes accessed | tf_op | source)
XLA Modules:
  0.0 28.9 jit_solution(2079544042263246858)
XLA Ops:
  0.6 0.0 copy-start.2
  0.6 0.0 copy-start.3
  0.7 0.0 copy-start
  0.7 0.0 copy-start.1
  0.7 0.0 copy-start.4
  0.7 1.4 %ends.1 = (f32[56,128]{1,0:T(8,128)S(1)}, f32[56,128]{1,0:T(8,128)S(1)}) custom-call(f32[256,128]{1,0:T(8,128)} %visc.5, f32[256,128]{1,0:T(8,128)} %fric.5, f32[2,256,128]{2,1,0:T(8,128)} %driv.5, s32[256,128]{1,0:T(8,128)} %mask.5, f32[2,256,128]{2,1,0:T(8,128)} %obs.5), custom_call_target="tpu_custom_call" | custom-call | flops 1000000 | bytes 1000000 | tf_op jit(solution)/shard_map/ends/pallas_call | solution.py:74
  2.1 3.1 %collective-permute-start = (f32[56,128]{1,0:T(8,128)S(1)}, f32[56,128]{1,0:T(8,128)S(1)}, u32[]{:S(2)}, u32[]{:S(2)}) collective-permute-start(f32[56,128]{1,0:T(8,128)S(1)} %get-tuple-element.22), channel_id=1, source_target_pairs={{0,4},{4,0},{8,12},{12,8},{1,2},{5,6},{9,10},{13,14},{2,1},{6,5},{... | collective-permute-start | bytes 86024 | tf_op jit(solution)/shard_map/ppermute | solution.py:53
  5.2 0.0 collective-permute-start.1
  5.3 0.0 copy-done.2
  5.3 0.0 copy-done.3
  5.3 0.0 copy-done.4
  5.3 2.1 %interior.1 = (f32[768,128]{1,0:T(8,128)S(1)}, f32[256,128]{1,0:T(8,128)S(1)}, f32[256,128]{1,0:T(8,128)S(1)}, f32[256,128]{1,0:T(8,128)S(1)}, f32[256,128]{1,0:...) custom-call(f32[256,128]{1,0:T(8,128)S(1)} %copy-done.2, f32[256,128]{1,0:T(8,128)S(1)} %copy-done.3, ...), custom_call_target="tpu_custom_call" | custom-call | flops 8000000 | bytes 8000000 | tf_op jit(solution)/shard_map/interior/pallas_call | solution.py:74
  7.4 0.0 collective-permute-done.row_b
  7.4 0.0 collective-permute-done.1.row_a
  7.4 0.0 copy-start.10
  7.4 0.0 copy-start.6
  7.4 0.1 columns.1
  7.5 0.0 copy-start.7
  7.5 0.5 %collective-permute-start.2 = (f32[88,128]{1,0:T(8,128)S(1)}, f32[88,128]{1,0:T(8,128)S(1)}, u32[]{:S(2)}, u32[]{:S(2)}) collective-permute-start(f32[88,128]{1,0:T(8,128)S(1)} %get-tuple-element.33), channel_id=1, source_target_pairs={{0,1},{4,8},{8,4},{12,13},{1,0},{5,9},{9,5},{13,12},{2,3},{6,10},{... | collective-permute-start | bytes 135176 | tf_op jit(solution)/shard_map/ppermute | solution.py:53
  8.1 2.8 %collective-permute-start.3 = (f32[88,128]{1,0:T(8,128)S(1)}, f32[88,128]{1,0:T(8,128)S(1)}, u32[]{:S(2)}, u32[]{:S(2)}) collective-permute-start(f32[88,128]{1,0:T(8,128)S(1)} %get-tuple-element.34), channel_id=1, source_target_pairs={{0,4},{4,0},{8,12},{12,8},{1,5},{5,1},{9,13},{13,9},{2,6},{6,2},{1... | collective-permute-start | bytes 135176 | tf_op jit(solution)/shard_map/ppermute | solution.py:53
  10.9 0.1 copy.15.block
  11.0 0.0 copy-done.6
  11.0 0.0 copy-start.8
  11.0 2.1 %adjoint.1 = (f32[32,128]{1,0:T(8,128)S(1)}, f32[32,128]{1,0:T(8,128)S(1)}, f32[840,128]{1,0:T(8,128)S(1)}, f32[24,128]{1,0:T(8,128)S(1)}) custom-call(f32[56,128]{1,0:T(8,128)S(1)} %collective-permute-done.row_b, f32[56,128]{1,0:T(8,128)S(1)} %collective-permute-done.1.row_a, f32[256,128]{1,0:T(8,128)S(1)} %copy-done.2, f32[256,128]{1,0:T(8,128)S(1)} %copy-done.3, ...), custom_call_target="tpu_custom_call" | custom-call | flops 8000000 | bytes 8000000 | tf_op jit(solution)/shard_map/adjoint/pallas_call | solution.py:74
  13.1 0.0 collective-permute-done.2.col_b
  13.1 0.0 collective-permute-done.3.col_a
  13.1 2.1 %left_right.1 = (f32[840,128]{1,0:T(8,128)S(1)}, f32[240,128]{1,0:T(8,128)S(1)}, f32[288,128]{1,0:T(8,128)}) custom-call(f32[840,128]{1,0:T(8,128)S(1)} %get-tuple-element.31._, f32[24,128]{1,0:T(8,128)S(1)} %get-tuple-element.32.seams, f32[88,128]{1,0:T(8,128)S(1)} %collective-permute-done.2.col_b, ...), custom_call_target="tpu_custom_call", output_to_operand_aliasing={{0}: (0, {})} | custom-call | flops 4000000 | bytes 4000000 | tf_op jit(solution)/shard_map/left_right/pallas_call | solution.py:74
  15.3 4.2 %all-to-all-start = ((f32[32,1,1152]{2,1,0:T(1,128)}), f32[32,1,1152]{2,1,0:T(1,128)S(1)}, u32[]{:S(2)}, u32[]{:S(2)}) async-start(f32[32,1,1152]{2,1,0:T(1,128)} %bitcast), calls=%async_computation | async-start | bytes 294912 | tf_op jit(solution)/shard_map/all_to_all | solution.py:767
  19.5 0.1 reshape.13.owners
  19.6 0.9 %join.1 = f32[2,256,128]{2,1,0:T(8,128)} custom-call(f32[256,128]{1,0:T(8,128)S(1)} %get-tuple-element.20.v0, f32[256,128]{1,0:T(8,128)S(1)} %get-tuple-element.21.v1, f32[32,128]{1,0:T(8,128)S(1)} %get-tuple-element.30.vel_ends, f32[240,128]{1,0:T(8,128)S(1)} %get-tuple-element.36.strips), custom_call_target="tpu_custom_call" | custom-call | flops 4000000 | bytes 4000000 | tf_op jit(solution)/shard_map/join/pallas_call | solution.py:74
  20.5 7.7 %all-to-all-done = f32[32,1,1152]{2,1,0:T(1,128)S(1)} async-done(((f32[32,1,1152]{2,1,0:T(1,128)}), f32[32,1,1152]{2,1,0:T(1,128)S(1)}, u32[]{:S(2)}, u32[]{:S(2)}) %all-to-all-start) | async-done | bytes 147488 | tf_op jit(solution)/shard_map/all_to_all | solution.py:767
  28.1 0.8 %pick.1 = f32[1,4,1024]{2,1,0:T(4,128)} custom-call(s32[4,4]{1,0:T(4,128)S(1)} %reshape.13.owners, f32[288,128]{1,0:T(8,128)S(1)} %bitcast.2), custom_call_target="tpu_custom_call" | custom-call | flops 100000 | bytes 100000 | tf_op jit(solution)/shard_map/pick/pallas_call | solution.py:74
  (9 shorter events, 0.0 us)
Async XLA Ops:
  0.6 4.6 %copy-start.2 = (f32[256,128]{1,0:T(8,128)S(1)}, f32[256,128]{1,0:T(8,128)}, u32[]{:S(2)}) copy-start(f32[256,128]{1,0:T(8,128)} %visc.5) | copy-start | bytes 393220
  0.6 4.6 %copy-start.3 = (f32[256,128]{1,0:T(8,128)S(1)}, f32[256,128]{1,0:T(8,128)}, u32[]{:S(2)}) copy-start(f32[256,128]{1,0:T(8,128)} %fric.5) | copy-start | bytes 393220
  0.7 4.6 %copy-start = (f32[2,256,128]{2,1,0:T(8,128)S(1)}, f32[2,256,128]{2,1,0:T(8,128)}, u32[]{:S(2)}) copy-start(f32[2,256,128]{2,1,0:T(8,128)} %driv.5) | copy-start | bytes 786436
  0.7 4.6 %copy-start.1 = (f32[2,256,128]{2,1,0:T(8,128)S(1)}, f32[2,256,128]{2,1,0:T(8,128)}, u32[]{:S(2)}) copy-start(f32[2,256,128]{2,1,0:T(8,128)} %obs.5) | copy-start | bytes 786436
  0.7 4.6 %copy-start.4 = (s32[256,128]{1,0:T(8,128)S(1)}, s32[256,128]{1,0:T(8,128)}, u32[]{:S(2)}) copy-start(s32[256,128]{1,0:T(8,128)} %mask.5) | copy-start | bytes 393220
  2.1 5.2 %collective-permute-start = (f32[56,128]{1,0:T(8,128)S(1)}, f32[56,128]{1,0:T(8,128)S(1)}, u32[]{:S(2)}, u32[]{:S(2)}) collective-permute-start(f32[56,128]{1,0:T(8,128)S(1)} %get-tuple-element.22), channel_id=1, source_target_pairs={{0,4},{4,0},{8,12},{12,8},{1,2},{5,6},{9,10},{13,14},{2,1},{6,5},{... | collective-permute-start | bytes 86024 | tf_op jit(solution)/shard_map/ppermute | solution.py:53
  5.2 2.2 %collective-permute-start.1 = (f32[56,128]{1,0:T(8,128)S(1)}, f32[56,128]{1,0:T(8,128)S(1)}, u32[]{:S(2)}, u32[]{:S(2)}) collective-permute-start(f32[56,128]{1,0:T(8,128)S(1)} %get-tuple-element.23), channel_id=1, source_target_pairs={{0,1},{4,5},{8,9},{12,13},{1,0},{5,4},{9,8},{13,12},{2,3},{6,7},{1... | collective-permute-start | bytes 86024 | tf_op jit(solution)/shard_map/ppermute | solution.py:53
  7.4 3.5 %copy-start.10 = (s32[2,1]{0,1:T(1,128)S(1)}, s32[2,1]{0,1:T(1,128)}, u32[]{:S(2)}) copy-start(s32[2,1]{0,1:T(1,128)} %param.16) | copy-start | bytes 28
  7.4 3.6 %copy-start.6 = (f32[128,128]{1,0:T(8,128)S(1)}, f32[128,128]{1,0:T(8,128)}, u32[]{:S(2)}) copy-start(f32[128,128]{1,0:T(8,128)} %constant.9.clone.basis_q) | copy-start | bytes 196612
  7.5 3.5 %copy-start.7 = (f32[32,128]{1,0:T(8,128)S(1)}, f32[32,128]{1,0:T(8,128)}, u32[]{:S(2)}) copy-start(f32[32,128]{1,0:T(8,128)} %constant.8.clone.basis_p) | copy-start | bytes 49156
  7.5 5.6 %collective-permute-start.2 = (f32[88,128]{1,0:T(8,128)S(1)}, f32[88,128]{1,0:T(8,128)S(1)}, u32[]{:S(2)}, u32[]{:S(2)}) collective-permute-start(f32[88,128]{1,0:T(8,128)S(1)} %get-tuple-element.33), channel_id=1, source_target_pairs={{0,1},{4,8},{8,4},{12,13},{1,0},{5,9},{9,5},{13,12},{2,3},{6,10},{... | collective-permute-start | bytes 135176 | tf_op jit(solution)/shard_map/ppermute | solution.py:53
  8.1 5.1 %collective-permute-start.3 = (f32[88,128]{1,0:T(8,128)S(1)}, f32[88,128]{1,0:T(8,128)S(1)}, u32[]{:S(2)}, u32[]{:S(2)}) collective-permute-start(f32[88,128]{1,0:T(8,128)S(1)} %get-tuple-element.34), channel_id=1, source_target_pairs={{0,4},{4,0},{8,12},{12,8},{1,5},{5,1},{9,13},{13,9},{2,6},{6,2},{1... | collective-permute-start | bytes 135176 | tf_op jit(solution)/shard_map/ppermute | solution.py:53
  11.0 2.2 %copy-start.5 = (bf16[768,32]{1,0:T(8,128)(2,1)S(1)}, bf16[768,32]{1,0:T(8,128)(2,1)}, u32[]{:S(2)}) copy-start(bf16[768,32]{1,0:T(8,128)(2,1)} %constant.10.clone.basis_rows) | copy-start | bytes 147460
  11.0 2.2 %copy-start.8 = (bf16[48,128]{1,0:T(8,128)(2,1)S(1)}, bf16[48,128]{1,0:T(8,128)(2,1)}, u32[]{:S(2)}) copy-start(bf16[48,128]{1,0:T(8,128)(2,1)} %constant.11.clone.basis_cols) | copy-start | bytes 36868
  15.3 4.2 %copy-start.9 = (s32[16]{0:T(128)S(1)}, s32[16]{0:T(128)}, u32[]{:S(2)}) copy-start(s32[16]{0:T(128)} %param.17) | copy-start | bytes 196
  15.3 12.9 %all-to-all-start = ((f32[32,1,1152]{2,1,0:T(1,128)}), f32[32,1,1152]{2,1,0:T(1,128)S(1)}, u32[]{:S(2)}, u32[]{:S(2)}) async-start(f32[32,1,1152]{2,1,0:T(1,128)} %bitcast), calls=%async_computation | async-start | bytes 294912 | tf_op jit(solution)/shard_map/all_to_all | solution.py:767

commit v4 on v0

--- a/solution.py
+++ b/solution.py
@@ -98,7 +98,7 @@
         return pl.ds(self.base + SUB * j, SUB)
 
     def prepare(self, flipped):
-        n2, n4, c, i, b0, b1 = self.refs[:6]
+        n2, n4, c, i = self.refs[:4]
         visc = [self.source(VISC, j) for j in range(self.span)]
         for j in range(self.span):
             at = self.at(j)
@@ -116,24 +116,25 @@
             n4[at, :] = 0.5 * half
             c[at, :] = 1.0 - fric * inv
             i[at, :] = inv
-            for k, b in enumerate((b0, b1)):
-                value = inv * self.source(DRIV + (1 - k if flipped else k), j)
-                b[at, :] = value
-                self.write(k, at, value + value)
+            for k in range(2):
+                self.start(k, at, inv * self.source(DRIV + (1 - k if flipped else k), j))
+
+    def start(self, k, at, value):
+        self.refs[4 + k][at, :] = value
+        self.write(k, at, value + value)
 
     def write(self, k, at, value):
         self.refs[6 + k][at, :] = value
         self.refs[8 + k][at, :] = pltpu.roll(value, TILE - 1, 1)
 
     def retarget(self, flipped, velocity=None):
-        i, b0, b1 = self.refs[3:6]
-        w0, w1 = velocity or self.refs[6:8]
+        i = self.refs[3]
+        velocity = velocity or self.refs[6:8]
         for j in range(self.span):
             at = self.at(j)
-            for k, (b, w) in enumerate(((b0, w0), (b1, w1))):
-                value = i[at, :] * (w[at, :] - self.source(OBS + (1 - k if flipped else k), j))
-                b[at, :] = value
-                self.write(k, at, value + value)
+            for k in range(2):
+                seen = self.source(OBS + (1 - k if flipped else k), j)
+                self.start(k, at, i[at, :] * (velocity[k][at, :] - seen))
 
     def differences(self):
         n2, n4 = self.refs[:2]
@@ -192,17 +193,18 @@
         super().prepare(flipped)
         for j in range(self.span):
             at = self.at(j)
-            for now, later in zip(self.refs[2:6], self.refs[10:14]):
+            for now, later in zip(self.refs[2:4], self.refs[10:12]):
                 later[at, :] = pltpu.roll(now[at, :], TILE - 1, 1)
         for now, before in zip(self.refs[:2], self.refs[14:16]):
             before[self.at(0), :] = pltpu.roll(now[self.at(self.span - 1), :], 1, 0)
 
-    def retarget(self, flipped, velocity=None):
-        super().retarget(flipped, velocity)
-        for j in range(self.span):
-            at = self.at(j)
-            for now, later in zip(self.refs[4:6], self.refs[12:14]):
-                later[at, :] = pltpu.roll(now[at, :], TILE - 1, 1)
+    def start(self, k, at, value):
+        b, w, r, later = (self.refs[n + k] for n in (4, 6, 8, 12))
+        b[at, :] = value
+        w[at, :] = value + value
+        turned = pltpu.roll(value, TILE - 1, 1)
+        later[at, :] = turned
+        r[at, :] = turned + turned
 
     def differences(self):
         fields = self.refs[6:10]
@@ -599,7 +601,11 @@
     half = lax.dot_general(
         basis_rows[...], split(dens, 1), (((1,), (1,)), ((), ())), preferred_element_type=F32
     )
-    wide = wide_in[...] + jnp.dot(split(half, 1), basis_cols[...], preferred_element_type=F32)
+    high = half.astype(jnp.bfloat16)
+    low = (half - high.astype(F32)).astype(jnp.bfloat16)
+    both = jnp.dot(jnp.concatenate([high, low], axis=0), basis_cols[:INNER], preferred_element_type=F32)
+    rest = jnp.dot(high, basis_cols[INNER:], preferred_element_type=F32)
+    wide = wide_in[...] + (both[:MODES] + (both[MODES:] + rest))
     lane = lanes()
     which = lax.div(lane, MODES)
     flat = wide[:SUB]
@@ -657,7 +663,7 @@
         at = lane + (TILE if part == 2 else 0)
         placed[at : at + SUB] = rows[row % TILE : row % TILE + SUB]
     outer = np.concatenate([cols[:HALO], cols[TILE - HALO :]])
-    return jnp.asarray(rows.T, F32), jnp.asarray(cols, F32), split_constant(placed.T, 1), split_constant(outer, 0)
+    return jnp.asarray(rows.T, F32), jnp.asarray(cols, F32), split_constant(placed.T, 1), split_constant(outer, 0)[: 2 * INNER]
 
 
 def pick_kernel(owners, every, out):

time: 29 us -> 28.9 us (level)
  no operation moved by 1% of the time
where the time goes in v4:
time: 28.9 us; the launch traced here: 28.7 us
  starting transfers between devices  10.7 us (37%)
  Pallas kernels  9.36 us (32%)
  waiting for transfers between devices  7.68 us (27%)
  between operations  0.79 us (3%)
    pallas_call x7, Pallas kernels, call(): pl.pallas_call(kernel, out_shape=outs, scratch_shapes=scratch, input_outp...  9.36 us
    all_to_all x1, waiting for transfers between devices, local(): parts = lax.all_to_all(coef, ROW_AXES + COL_AXES, 0, 0, tiled=True)  7.67 us
    ppermute x4, starting transfers between devices, swap(): return lax.ppermute(x, ('row', 'col', 'own'), pairs)  6.46 us
    all_to_all x1, starting transfers between devices, local(): parts = lax.all_to_all(coef, ROW_AXES + COL_AXES, 0, 0, tiled=True)  4.21 us
  transfers between devices with their start and end apart: 5, of which 1 were waited for; matrix products, arithmetic and copies ran while one was open for 1% of the time, Pallas kernels for 18%

profile of v4, /device:TPU:0, one launch (start us, length us, event | category | flops | bytes accessed | tf_op | source)
XLA Modules:
  0.0 28.7 jit_solution(1937185672738369353)
XLA Ops:
  0.6 0.0 copy-start.2
  0.6 0.0 copy-start.3
  0.7 0.0 copy-start
  0.7 0.0 copy-start.1
  0.7 0.0 copy-start.4
  0.7 1.4 %ends.1 = (f32[56,128]{1,0:T(8,128)S(1)}, f32[56,128]{1,0:T(8,128)S(1)}) custom-call(f32[256,128]{1,0:T(8,128)} %visc.5, f32[256,128]{1,0:T(8,128)} %fric.5, f32[2,256,128]{2,1,0:T(8,128)} %driv.5, s32[256,128]{1,0:T(8,128)} %mask.5, f32[2,256,128]{2,1,0:T(8,128)} %obs.5), custom_call_target="tpu_custom_call" | custom-call | flops 1000000 | bytes 1000000 | tf_op jit(solution)/shard_map/ends/pallas_call | solution.py:74
  2.1 3.1 %collective-permute-start = (f32[56,128]{1,0:T(8,128)S(1)}, f32[56,128]{1,0:T(8,128)S(1)}, u32[]{:S(2)}, u32[]{:S(2)}) collective-permute-start(f32[56,128]{1,0:T(8,128)S(1)} %get-tuple-element.22), channel_id=1, source_target_pairs={{0,4},{4,0},{8,12},{12,8},{1,2},{5,6},{9,10},{13,14},{2,1},{6,5},{... | collective-permute-start | bytes 86024 | tf_op jit(solution)/shard_map/ppermute | solution.py:53
  5.2 0.0 collective-permute-start.1
  5.3 0.0 copy-done.2
  5.3 0.0 copy-done.3
  5.3 0.0 copy-done.4
  5.3 2.1 %interior.1 = (f32[768,128]{1,0:T(8,128)S(1)}, f32[256,128]{1,0:T(8,128)S(1)}, f32[256,128]{1,0:T(8,128)S(1)}, f32[256,128]{1,0:T(8,128)S(1)}, f32[256,128]{1,0:...) custom-call(f32[256,128]{1,0:T(8,128)S(1)} %copy-done.2, f32[256,128]{1,0:T(8,128)S(1)} %copy-done.3, ...), custom_call_target="tpu_custom_call" | custom-call | flops 8000000 | bytes 8000000 | tf_op jit(solution)/shard_map/interior/pallas_call | solution.py:74
  7.4 0.0 collective-permute-done.row_b
  7.4 0.0 collective-permute-done.1.row_a
  7.4 0.0 copy-start.10
  7.4 0.0 copy-start.5
  7.4 0.1 columns.1
  7.5 0.0 copy-start.7
  7.5 0.5 %collective-permute-start.2 = (f32[88,128]{1,0:T(8,128)S(1)}, f32[88,128]{1,0:T(8,128)S(1)}, u32[]{:S(2)}, u32[]{:S(2)}) collective-permute-start(f32[88,128]{1,0:T(8,128)S(1)} %get-tuple-element.33), channel_id=1, source_target_pairs={{0,1},{4,8},{8,4},{12,13},{1,0},{5,9},{9,5},{13,12},{2,3},{6,10},{... | collective-permute-start | bytes 135176 | tf_op jit(solution)/shard_map/ppermute | solution.py:53
  8.1 2.8 %collective-permute-start.3 = (f32[88,128]{1,0:T(8,128)S(1)}, f32[88,128]{1,0:T(8,128)S(1)}, u32[]{:S(2)}, u32[]{:S(2)}) collective-permute-start(f32[88,128]{1,0:T(8,128)S(1)} %get-tuple-element.34), channel_id=1, source_target_pairs={{0,4},{4,0},{8,12},{12,8},{1,5},{5,1},{9,13},{13,9},{2,6},{6,2},{1... | collective-permute-start | bytes 135176 | tf_op jit(solution)/shard_map/ppermute | solution.py:53
  10.9 0.1 copy.15.block
  11.0 0.0 copy-done.5
  11.0 0.0 copy-start.8
  11.0 2.1 %adjoint.1 = (f32[32,128]{1,0:T(8,128)S(1)}, f32[32,128]{1,0:T(8,128)S(1)}, f32[840,128]{1,0:T(8,128)S(1)}, f32[24,128]{1,0:T(8,128)S(1)}) custom-call(f32[56,128]{1,0:T(8,128)S(1)} %collective-permute-done.row_b, f32[56,128]{1,0:T(8,128)S(1)} %collective-permute-done.1.row_a, f32[256,128]{1,0:T(8,128)S(1)} %copy-done.2, f32[256,128]{1,0:T(8,128)S(1)} %copy-done.3, ...), custom_call_target="tpu_custom_call" | custom-call | flops 8000000 | bytes 8000000 | tf_op jit(solution)/shard_map/adjoint/pallas_call | solution.py:74
  13.1 0.0 collective-permute-done.2.col_b
  13.1 0.0 collective-permute-done.3.col_a
  13.1 2.0 %left_right.1 = (f32[840,128]{1,0:T(8,128)S(1)}, f32[240,128]{1,0:T(8,128)S(1)}, f32[288,128]{1,0:T(8,128)}) custom-call(f32[840,128]{1,0:T(8,128)S(1)} %get-tuple-element.31._, f32[24,128]{1,0:T(8,128)S(1)} %get-tuple-element.32.seams, f32[88,128]{1,0:T(8,128)S(1)} %collective-permute-done.2.col_b, ...), custom_call_target="tpu_custom_call", output_to_operand_aliasing={{0}: (0, {})} | custom-call | flops 4000000 | bytes 4000000 | tf_op jit(solution)/shard_map/left_right/pallas_call | solution.py:74
  15.1 4.2 %all-to-all-start = ((f32[32,1,1152]{2,1,0:T(1,128)}), f32[32,1,1152]{2,1,0:T(1,128)S(1)}, u32[]{:S(2)}, u32[]{:S(2)}) async-start(f32[32,1,1152]{2,1,0:T(1,128)} %bitcast), calls=%async_computation | async-start | bytes 294912 | tf_op jit(solution)/shard_map/all_to_all | solution.py:782
  19.3 0.1 reshape.13.owners
  19.4 0.9 %join.1 = f32[2,256,128]{2,1,0:T(8,128)} custom-call(f32[256,128]{1,0:T(8,128)S(1)} %get-tuple-element.20.v0, f32[256,128]{1,0:T(8,128)S(1)} %get-tuple-element.21.v1, f32[32,128]{1,0:T(8,128)S(1)} %get-tuple-element.30.vel_ends, f32[240,128]{1,0:T(8,128)S(1)} %get-tuple-element.36.strips), custom_call_target="tpu_custom_call" | custom-call | flops 4000000 | bytes 4000000 | tf_op jit(solution)/shard_map/join/pallas_call | solution.py:74
  20.3 7.7 %all-to-all-done = f32[32,1,1152]{2,1,0:T(1,128)S(1)} async-done(((f32[32,1,1152]{2,1,0:T(1,128)}), f32[32,1,1152]{2,1,0:T(1,128)S(1)}, u32[]{:S(2)}, u32[]{:S(2)}) %all-to-all-start) | async-done | bytes 147488 | tf_op jit(solution)/shard_map/all_to_all | solution.py:782
  28.0 0.8 %pick.1 = f32[1,4,1024]{2,1,0:T(4,128)} custom-call(s32[4,4]{1,0:T(4,128)S(1)} %reshape.13.owners, f32[288,128]{1,0:T(8,128)S(1)} %bitcast.2), custom_call_target="tpu_custom_call" | custom-call | flops 100000 | bytes 100000 | tf_op jit(solution)/shard_map/pick/pallas_call | solution.py:74
  (9 shorter events, 0.0 us)
Async XLA Ops:
  0.6 4.6 %copy-start.2 = (f32[256,128]{1,0:T(8,128)S(1)}, f32[256,128]{1,0:T(8,128)}, u32[]{:S(2)}) copy-start(f32[256,128]{1,0:T(8,128)} %visc.5) | copy-start | bytes 393220
  0.6 4.6 %copy-start.3 = (f32[256,128]{1,0:T(8,128)S(1)}, f32[256,128]{1,0:T(8,128)}, u32[]{:S(2)}) copy-start(f32[256,128]{1,0:T(8,128)} %fric.5) | copy-start | bytes 393220
  0.7 4.6 %copy-start = (f32[2,256,128]{2,1,0:T(8,128)S(1)}, f32[2,256,128]{2,1,0:T(8,128)}, u32[]{:S(2)}) copy-start(f32[2,256,128]{2,1,0:T(8,128)} %driv.5) | copy-start | bytes 786436
  0.7 4.6 %copy-start.1 = (f32[2,256,128]{2,1,0:T(8,128)S(1)}, f32[2,256,128]{2,1,0:T(8,128)}, u32[]{:S(2)}) copy-start(f32[2,256,128]{2,1,0:T(8,128)} %obs.5) | copy-start | bytes 786436
  0.7 4.6 %copy-start.4 = (s32[256,128]{1,0:T(8,128)S(1)}, s32[256,128]{1,0:T(8,128)}, u32[]{:S(2)}) copy-start(s32[256,128]{1,0:T(8,128)} %mask.5) | copy-start | bytes 393220
  2.1 5.2 %collective-permute-start = (f32[56,128]{1,0:T(8,128)S(1)}, f32[56,128]{1,0:T(8,128)S(1)}, u32[]{:S(2)}, u32[]{:S(2)}) collective-permute-start(f32[56,128]{1,0:T(8,128)S(1)} %get-tuple-element.22), channel_id=1, source_target_pairs={{0,4},{4,0},{8,12},{12,8},{1,2},{5,6},{9,10},{13,14},{2,1},{6,5},{... | collective-permute-start | bytes 86024 | tf_op jit(solution)/shard_map/ppermute | solution.py:53
  5.2 2.2 %collective-permute-start.1 = (f32[56,128]{1,0:T(8,128)S(1)}, f32[56,128]{1,0:T(8,128)S(1)}, u32[]{:S(2)}, u32[]{:S(2)}) collective-permute-start(f32[56,128]{1,0:T(8,128)S(1)} %get-tuple-element.23), channel_id=1, source_target_pairs={{0,1},{4,5},{8,9},{12,13},{1,0},{5,4},{9,8},{13,12},{2,3},{6,7},{1... | collective-permute-start | bytes 86024 | tf_op jit(solution)/shard_map/ppermute | solution.py:53
  7.4 3.5 %copy-start.10 = (s32[2,1]{0,1:T(1,128)S(1)}, s32[2,1]{0,1:T(1,128)}, u32[]{:S(2)}) copy-start(s32[2,1]{0,1:T(1,128)} %param.16) | copy-start | bytes 28
  7.4 3.6 %copy-start.5 = (f32[128,128]{1,0:T(8,128)S(1)}, f32[128,128]{1,0:T(8,128)}, u32[]{:S(2)}) copy-start(f32[128,128]{1,0:T(8,128)} %constant.9.clone.basis_q) | copy-start | bytes 196612
  7.5 3.5 %copy-start.7 = (f32[32,128]{1,0:T(8,128)S(1)}, f32[32,128]{1,0:T(8,128)}, u32[]{:S(2)}) copy-start(f32[32,128]{1,0:T(8,128)} %constant.8.clone.basis_p) | copy-start | bytes 49156
  7.5 5.6 %collective-permute-start.2 = (f32[88,128]{1,0:T(8,128)S(1)}, f32[88,128]{1,0:T(8,128)S(1)}, u32[]{:S(2)}, u32[]{:S(2)}) collective-permute-start(f32[88,128]{1,0:T(8,128)S(1)} %get-tuple-element.33), channel_id=1, source_target_pairs={{0,1},{4,8},{8,4},{12,13},{1,0},{5,9},{9,5},{13,12},{2,3},{6,10},{... | collective-permute-start | bytes 135176 | tf_op jit(solution)/shard_map/ppermute | solution.py:53
  8.1 5.1 %collective-permute-start.3 = (f32[88,128]{1,0:T(8,128)S(1)}, f32[88,128]{1,0:T(8,128)S(1)}, u32[]{:S(2)}, u32[]{:S(2)}) collective-permute-start(f32[88,128]{1,0:T(8,128)S(1)} %get-tuple-element.34), channel_id=1, source_target_pairs={{0,4},{4,0},{8,12},{12,8},{1,5},{5,1},{9,13},{13,9},{2,6},{6,2},{1... | collective-permute-start | bytes 135176 | tf_op jit(solution)/shard_map/ppermute | solution.py:53
  11.0 2.2 %copy-start.6 = (bf16[32,768]{1,0:T(8,128)(2,1)S(1)}, bf16[32,768]{1,0:T(8,128)(2,1)}, u32[]{:S(2)}) copy-start(bf16[32,768]{1,0:T(8,128)(2,1)} %constant.10.clone.basis_rows) | copy-start | bytes 147460
  11.0 2.2 %copy-start.8 = (bf16[32,128]{1,0:T(8,128)(2,1)S(1)}, bf16[32,128]{1,0:T(8,128)(2,1)}, u32[]{:S(2)}) copy-start(bf16[32,128]{1,0:T(8,128)(2,1)} %constant.13.basis_cols) | copy-start | bytes 24580
  15.1 4.2 %copy-start.9 = (s32[16]{0:T(128)S(1)}, s32[16]{0:T(128)}, u32[]{:S(2)}) copy-start(s32[16]{0:T(128)} %param.17) | copy-start | bytes 196
  15.1 12.9 %all-to-all-start = ((f32[32,1,1152]{2,1,0:T(1,128)}), f32[32,1,1152]{2,1,0:T(1,128)S(1)}, u32[]{:S(2)}, u32[]{:S(2)}) async-start(f32[32,1,1152]{2,1,0:T(1,128)} %bitcast), calls=%async_computation | async-start | bytes 294912 | tf_op jit(solution)/shard_map/all_to_all | solution.py:782

commit v5 on v4

--- a/solution.py
+++ b/solution.py
@@ -127,9 +127,9 @@
         self.refs[6 + k][at, :] = value
         self.refs[8 + k][at, :] = pltpu.roll(value, TILE - 1, 1)
 
-    def retarget(self, flipped, velocity=None):
+    def retarget(self, flipped):
         i = self.refs[3]
-        velocity = velocity or self.refs[6:8]
+        velocity = self.refs[6:8]
         for j in range(self.span):
             at = self.at(j)
             for k in range(2):
@@ -298,19 +298,6 @@
         to_b[at, :] = jnp.where(at_end, 0.0, jnp.where(even, head, tail))
 
 
-def field_of(visc, fric, driv, mask, obs):
-    def field(a, at):
-        if a == MASK:
-            return mask[at, :].astype(F32)
-        if a >= OBS:
-            return obs[a - OBS, at, :]
-        if a >= DRIV:
-            return driv[a - DRIV, at, :]
-        return (visc, fric)[a][at, :]
-
-    return field
-
-
 def first_row(part, lane):
     if part < 2:
         return TILE * part + lane
@@ -335,9 +322,37 @@
     return TILE * (2 * part + a // PER) + SLOT * (a % PER)
 
 
-def interior_kernel(visc, fric, driv, mask, obs, edge, n2, n4, c, i, v0, v1, *refs):
-    span = visc.shape[0] // SUB
-    field = field_of(visc, fric, driv, mask, obs)
+def field_in(every):
+    rows = every.shape[0] // ARRAYS
+
+    def field(a, at):
+        return every[rows * a + at.start : rows * a + at.stop, :]
+
+    return field
+
+
+def load_kernel(visc, fric, driv, mask, obs, _, every, edge, flags, sems):
+    rows = visc.shape[0]
+
+    def place(a):
+        return every.at[pl.ds(rows * a, rows)]
+
+    pieces = [
+        (visc, place(VISC)),
+        (fric, place(FRIC)),
+        (mask, flags),
+        (driv.at[0], place(DRIV)),
+        (driv.at[1], place(DRIV + 1)),
+        (obs.at[0], place(OBS)),
+        (obs.at[1], place(OBS + 1)),
+    ]
+    copies = [pltpu.make_async_copy(*piece, sems.at[n]) for n, piece in enumerate(pieces)]
+    for copy in copies:
+        copy.start()
+    for copy in copies:
+        copy.wait()
+    every[MASK * rows : (MASK + 1) * rows, :] = flags[...].astype(F32)
+    field = field_in(every)
     lane = lanes()
     for part in range(PARTS):
         for m in range(-(-ARRAYS // PER)):
@@ -353,11 +368,6 @@
                 strips.append(packed)
             base = TILE * (2 * part + m)
             edge[base : base + TILE, :] = jnp.concatenate(strips, axis=0).T
-    refs = (n2, n4, c, i, *refs[:2], v0, v1, *refs[2:])
-    domain = Domain(refs, 0, span, lambda a, j: field(a, pl.ds(j, SUB, stride=span)))
-    domain.prepare(False)
-    run([domain])
-
 
 def columns_kernel(row_b, row_a, edge, to_b, to_a, turned):
     even = is_even(ROW_AXES)
@@ -432,14 +442,14 @@
 
 
 def adjoint_kernel(
-    row_b, row_a, visc, fric, driv, mask, obs, n2, n4, c, i, v0, v1, basis_p, basis_q, edge, turned,
-    vel, wide, sides, seams,
+    row_b, row_a, every, basis_p, basis_q, edge, turned,
+    vel, wide, sides, seams, v0, v1,
     stack, plain, dens, total, *refs,
 ):
-    rows = visc.shape[0]
+    rows = every.shape[0] // ARRAYS
     span = rows // SUB
     even = is_even(ROW_AXES)
-    field = field_of(visc, fric, driv, mask, obs)
+    field = field_in(every)
     for a in range(ARRAYS):
         at = slice(HALO * a, HALO * (a + 1))
         got_a, got_b = row_a[at, :], row_b[at, :]
@@ -449,19 +459,22 @@
         fill(stack, base, first, last)
         stack[base : base + LEAD, :] = jnp.where(even, got_b, got_a)[HALO - LEAD :]
         stack[base + STRIP - HALO : base + STRIP, :] = jnp.where(even, got_a, got_b)
-    strips = Strips(refs[:STRIP_FIELDS], 0, STRIP // SUB, strided(stack, 0), lambda: visc[rows - KEPT - 1 : rows - KEPT, :])
+    strips = Strips(refs[:STRIP_FIELDS], 0, STRIP // SUB, strided(stack, 0), lambda: every[rows - KEPT - 1 : rows - KEPT, :])
+    interior = Domain(
+        refs[STRIP_FIELDS:], 0, span, lambda a, j: every[pl.ds(rows * a + j, SUB, stride=span), :]
+    )
     strips.prepare(False)
-    run([strips])
+    interior.prepare(False)
+    run([interior, strips])
+    v0[...] = interior.refs[6][...]
+    v1[...] = interior.refs[7][...]
     velocity(strips, plain, 0)
     for k in range(2):
         for e in range(2):
             out = HALO * (2 * k + e)
             vel[out : out + HALO, :] = plain[STRIP * k + OUTER[e] : STRIP * k + OUTER[e] + HALO, :]
-    interior = Domain(
-        (n2, n4, c, i, *refs[STRIP_FIELDS:]), 0, span, lambda a, j: field(a, pl.ds(j, SUB, stride=span))
-    )
     strips.retarget(False)
-    interior.retarget(False, (v0, v1))
+    interior.retarget(False)
     run([interior, strips])
     w0, w1 = interior.refs[6:8]
     for j in range(span):
@@ -698,7 +711,7 @@
     rows, cols = viscosity.shape
     assert (rows, cols) == (2 * TILE, TILE)
     inputs = (viscosity, friction, driving, ice_mask, observed)
-    near = [pltpu.with_memory_space_constraint(x, pltpu.VMEM) for x in inputs]
+    far = [pltpu.with_memory_space_constraint(x, pltpu.HBM) for x in inputs]
     basis_p, basis_q, basis_rows, basis_cols = bases()
     to_b, to_a = call(
         ends_kernel,
@@ -711,17 +724,18 @@
             pltpu.SemaphoreType.DMA((2, 5)),
         ],
         10**6,
-        *(pltpu.with_memory_space_constraint(x, pltpu.HBM) for x in inputs),
+        *far,
     )
     row_b = swap(to_b, 0, 1)
     row_a = swap(to_a, 0, 0)
-    edge, *forward = call(
-        interior_kernel,
-        "interior",
-        (vmem(2 * PARTS * TILE, TILE),) + (vmem(rows, cols),) * 6,
-        [vmem(rows, cols)] * (FIELDS - 6),
+    every, edge = call(
+        load_kernel,
+        "load",
+        (vmem(ARRAYS * rows, cols), vmem(2 * PARTS * TILE, TILE)),
+        [pltpu.VMEM((rows, cols), jnp.int32), pltpu.SemaphoreType.DMA((ARRAYS,))],
         8 * 10**6,
-        *near,
+        *far,
+        to_b,
     )
     to_b, to_a, turned = call(
         columns_kernel,
@@ -735,7 +749,7 @@
     )
     col_b = swap(to_b, 1, 1)
     col_a = swap(to_a, 1, 0)
-    vel_ends, wide, sides, seams = call(
+    vel_ends, wide, sides, seams, *vel_inner = call(
         adjoint_kernel,
         "adjoint",
         (
@@ -743,15 +757,16 @@
             vmem(MODES, TILE),
             vmem(PARTS * ARRAYS * STRIP, TILE),
             vmem(PARTS * SUB, TILE),
+            vmem(rows, cols),
+            vmem(rows, cols),
         ),
         [vmem(ARRAYS * STRIP, cols), vmem(2 * STRIP, cols), vmem(rows + STRIP, cols), vmem(TILE, cols)]
         + [vmem(STRIP, cols)] * STRIP_FIELDS
-        + [vmem(rows, cols)] * (FIELDS - 4),
+        + [vmem(rows, cols)] * FIELDS,
         8 * 10**6,
         row_b,
         row_a,
-        *near,
-        *forward,
+        every,
         basis_p,
         basis_q,
         edge,
@@ -786,7 +801,7 @@
         jax.ShapeDtypeStruct((2, rows, cols), F32),
         [vmem(2 * PARTS * TILE, TILE)],
         4 * 10**6,
-        *forward[4:],
+        *vel_inner,
         vel_ends,
         strips,
     )

time: 28.9 us -> 29.1 us (level)
  Pallas kernels: 9.36 us -> 11.1 us
  starting transfers between devices: 10.7 us -> 9.1 us
    pallas_call x7, Pallas kernels: 9.36 us -> 11.1 us  [call(): pl.pallas_call(kernel, out_shape=outs, scratch_shapes=scratch, input_outp...]
    all_to_all x1, starting transfers between devices: 4.21 us -> 2.77 us  [local(): parts = lax.all_to_all(coef, ROW_AXES + COL_AXES, 0, 0, tiled=True)]
  transfers between devices with their start and end apart: 5 -> 5, of which waited for: 1 -> 1; matrix products, arithmetic and copies ran while one was open for 1% -> 1% of each run, Pallas kernels for 18% -> 24%
where the time goes in v5:
time: 29.1 us; the launch traced here: 28.9 us
  Pallas kernels  11.1 us (38%)
  starting transfers between devices  9.1 us (31%)
  waiting for transfers between devices  7.68 us (26%)
  between operations  0.74 us (3%)
    pallas_call x7, Pallas kernels, call(): pl.pallas_call(kernel, out_shape=outs, scratch_shapes=scratch, input_outp...  11.1 us
    all_to_all x1, waiting for transfers between devices, local(): parts = lax.all_to_all(coef, ROW_AXES + COL_AXES, 0, 0, tiled=True)  7.67 us
    ppermute x4, starting transfers between devices, swap(): return lax.ppermute(x, ('row', 'col', 'own'), pairs)  6.34 us
    all_to_all x1, starting transfers between devices, local(): parts = lax.all_to_all(coef, ROW_AXES + COL_AXES, 0, 0, tiled=True)  2.77 us
  transfers between devices with their start and end apart: 5, of which 1 were waited for; matrix products, arithmetic and copies ran while one was open for 1% of the time, Pallas kernels for 24%

profile of v5, /device:TPU:0, one launch (start us, length us, event | category | flops | bytes accessed | tf_op | source)
XLA Modules:
  0.0 28.9 jit_solution(18270810647151894218)
XLA Ops:
  0.6 1.4 %ends.1 = (f32[56,128]{1,0:T(8,128)S(1)}, f32[56,128]{1,0:T(8,128)S(1)}) custom-call(f32[256,128]{1,0:T(8,128)} %visc.3, f32[256,128]{1,0:T(8,128)} %fric.3, f32[2,256,128]{2,1,0:T(8,128)} %driv.3, s32[256,128]{1,0:T(8,128)} %mask.3, f32[2,256,128]{2,1,0:T(8,128)} %obs.3), custom_call_target="tpu_custom_call" | custom-call | flops 1000000 | bytes 1000000 | tf_op jit(solution)/shard_map/ends/pallas_call | solution.py:74
  2.0 3.1 %collective-permute-start = (f32[56,128]{1,0:T(8,128)S(1)}, f32[56,128]{1,0:T(8,128)S(1)}, u32[]{:S(2)}, u32[]{:S(2)}) collective-permute-start(f32[56,128]{1,0:T(8,128)S(1)} %get-tuple-element.17._), channel_id=1, source_target_pairs={{0,4},{4,0},{8,12},{12,8},{1,2},{5,6},{9,10},{13,14},{2,1},{6,5},{... | collective-permute-start | bytes 86024 | tf_op jit(solution)/shard_map/ppermute | solution.py:53
  5.1 0.0 collective-permute-start.1
  5.1 3.1 %load.1 = (f32[1792,128]{1,0:T(8,128)S(1)}, f32[768,128]{1,0:T(8,128)S(1)}) custom-call(f32[256,128]{1,0:T(8,128)} %visc.3, f32[256,128]{1,0:T(8,128)} %fric.3, f32[2,256,128]{2,1,0:T(8,128)} %driv.3, s32[256,128]{1,0:T(8,128)} %mask.3, f32[2,256,128]{2,1,0:T(8,128)} %obs.3, f32[56,128]{1,0:T(8,128)S(1)} %get-tuple-element.17._), custom_call_target="tpu_custom_call" | custom-call | flops 8000000 | bytes 8000000 | tf_op jit(solution)/shard_map/load/pallas_call | solution.py:74
  8.2 0.0 collective-permute-done.row_b
  8.2 0.0 collective-permute-done.1.row_a
  8.3 0.0 copy-start
  8.3 0.0 copy-start.2
  8.3 0.1 columns.1
  8.4 0.0 copy-start.5
  8.4 0.5 %collective-permute-start.2 = (f32[88,128]{1,0:T(8,128)S(1)}, f32[88,128]{1,0:T(8,128)S(1)}, u32[]{:S(2)}, u32[]{:S(2)}) collective-permute-start(f32[88,128]{1,0:T(8,128)S(1)} %get-tuple-element.27), channel_id=1, source_target_pairs={{0,1},{4,8},{8,4},{12,13},{1,0},{5,9},{9,5},{13,12},{2,3},{6,10},{... | collective-permute-start | bytes 135176 | tf_op jit(solution)/shard_map/ppermute | solution.py:53
  8.9 2.7 %collective-permute-start.3 = (f32[88,128]{1,0:T(8,128)S(1)}, f32[88,128]{1,0:T(8,128)S(1)}, u32[]{:S(2)}, u32[]{:S(2)}) collective-permute-start(f32[88,128]{1,0:T(8,128)S(1)} %get-tuple-element.28), channel_id=1, source_target_pairs={{0,4},{4,0},{8,12},{12,8},{1,5},{5,1},{9,13},{13,9},{2,6},{6,2},{1... | collective-permute-start | bytes 135176 | tf_op jit(solution)/shard_map/ppermute | solution.py:53
  11.6 0.0 copy-done.5
  11.6 0.1 copy.15.block
  11.7 0.0 copy-done
  11.7 0.0 copy-done.2
  11.7 0.0 copy-start.1
  11.7 0.0 copy-start.3
  11.7 3.0 %adjoint.1 = (f32[32,128]{1,0:T(8,128)S(1)}, f32[32,128]{1,0:T(8,128)S(1)}, f32[840,128]{1,0:T(8,128)S(1)}, f32[24,128]{1,0:T(8,128)S(1)}, f32[256,128]{1,0:T(8,128)S(1)}, /*index=5*/f32[256,128]{1,0:T(8,128)S(1)}) custom-call(f32[56,128]{1,0:T(8,128)S(1)} %collective-permute-done.row_b, f32[56,128]{1,0:T(8,128)S(1)} %collective-permute-done.1.row_a, ...), custom_call_target="tpu_custom_call" | custom-call | flops 8000000 | bytes 8000000 | tf_op jit(solution)/shard_map/adjoint/pallas_call | solution.py:74
  14.7 0.0 collective-permute-done.2.col_b
  14.7 0.0 collective-permute-done.3.col_a
  14.7 0.0 copy-done.1
  14.7 0.0 copy-done.3
  14.7 2.0 %left_right.1 = (f32[840,128]{1,0:T(8,128)S(1)}, f32[240,128]{1,0:T(8,128)S(1)}, f32[288,128]{1,0:T(8,128)}) custom-call(f32[840,128]{1,0:T(8,128)S(1)} %get-tuple-element.25._, f32[24,128]{1,0:T(8,128)S(1)} %get-tuple-element.26.seams, f32[88,128]{1,0:T(8,128)S(1)} %collective-permute-done.2.col_b, ...), custom_call_target="tpu_custom_call", output_to_operand_aliasing={{0}: (0, {})} | custom-call | flops 4000000 | bytes 4000000 | tf_op jit(solution)/shard_map/left_right/pallas_call | solution.py:74
  16.7 0.0 copy-start.4
  16.7 2.8 %all-to-all-start = ((f32[32,1,1152]{2,1,0:T(1,128)}), f32[32,1,1152]{2,1,0:T(1,128)S(1)}, u32[]{:S(2)}, u32[]{:S(2)}) async-start(f32[32,1,1152]{2,1,0:T(1,128)} %bitcast), calls=%async_computation | async-start | bytes 294912 | tf_op jit(solution)/shard_map/all_to_all | solution.py:797
  19.5 0.0 copy-done.4
  19.5 0.1 reshape.13.owners
  19.6 0.9 %join.1 = f32[2,256,128]{2,1,0:T(8,128)} custom-call(f32[256,128]{1,0:T(8,128)S(1)} %get-tuple-element.22.v0, f32[256,128]{1,0:T(8,128)S(1)} %get-tuple-element.23.v1, f32[32,128]{1,0:T(8,128)S(1)} %get-tuple-element.24.vel_ends, f32[240,128]{1,0:T(8,128)S(1)} %get-tuple-element.30.strips), custom_call_target="tpu_custom_call" | custom-call | flops 4000000 | bytes 4000000 | tf_op jit(solution)/shard_map/join/pallas_call | solution.py:74
  20.4 7.7 %all-to-all-done = f32[32,1,1152]{2,1,0:T(1,128)S(1)} async-done(((f32[32,1,1152]{2,1,0:T(1,128)}), f32[32,1,1152]{2,1,0:T(1,128)S(1)}, u32[]{:S(2)}, u32[]{:S(2)}) %all-to-all-start) | async-done | bytes 147488 | tf_op jit(solution)/shard_map/all_to_all | solution.py:797
  28.1 0.8 %pick.1 = f32[1,4,1024]{2,1,0:T(4,128)} custom-call(s32[4,4]{1,0:T(4,128)S(1)} %reshape.13.owners, f32[288,128]{1,0:T(8,128)S(1)} %bitcast.2), custom_call_target="tpu_custom_call" | custom-call | flops 100000 | bytes 100000 | tf_op jit(solution)/shard_map/pick/pallas_call | solution.py:74
Async XLA Ops:
  2.0 6.2 %collective-permute-start = (f32[56,128]{1,0:T(8,128)S(1)}, f32[56,128]{1,0:T(8,128)S(1)}, u32[]{:S(2)}, u32[]{:S(2)}) collective-permute-start(f32[56,128]{1,0:T(8,128)S(1)} %get-tuple-element.17._), channel_id=1, source_target_pairs={{0,4},{4,0},{8,12},{12,8},{1,2},{5,6},{9,10},{13,14},{2,1},{6,5},{... | collective-permute-start | bytes 86024 | tf_op jit(solution)/shard_map/ppermute | solution.py:53
  5.1 3.1 %collective-permute-start.1 = (f32[56,128]{1,0:T(8,128)S(1)}, f32[56,128]{1,0:T(8,128)S(1)}, u32[]{:S(2)}, u32[]{:S(2)}) collective-permute-start(f32[56,128]{1,0:T(8,128)S(1)} %get-tuple-element.18), channel_id=1, source_target_pairs={{0,1},{4,5},{8,9},{12,13},{1,0},{5,4},{9,8},{13,12},{2,3},{6,7},{1... | collective-permute-start | bytes 86024 | tf_op jit(solution)/shard_map/ppermute | solution.py:53
  8.3 3.5 %copy-start = (f32[128,128]{1,0:T(8,128)S(1)}, f32[128,128]{1,0:T(8,128)}, u32[]{:S(2)}) copy-start(f32[128,128]{1,0:T(8,128)} %constant.9.clone.basis_q) | copy-start | bytes 196612
  8.3 3.4 %copy-start.2 = (f32[32,128]{1,0:T(8,128)S(1)}, f32[32,128]{1,0:T(8,128)}, u32[]{:S(2)}) copy-start(f32[32,128]{1,0:T(8,128)} %constant.8.clone.basis_p) | copy-start | bytes 49156
  8.4 3.2 %copy-start.5 = (s32[2,1]{0,1:T(1,128)S(1)}, s32[2,1]{0,1:T(1,128)}, u32[]{:S(2)}) copy-start(s32[2,1]{0,1:T(1,128)} %param.16) | copy-start | bytes 28
  8.4 6.3 %collective-permute-start.2 = (f32[88,128]{1,0:T(8,128)S(1)}, f32[88,128]{1,0:T(8,128)S(1)}, u32[]{:S(2)}, u32[]{:S(2)}) collective-permute-start(f32[88,128]{1,0:T(8,128)S(1)} %get-tuple-element.27), channel_id=1, source_target_pairs={{0,1},{4,8},{8,4},{12,13},{1,0},{5,9},{9,5},{13,12},{2,3},{6,10},{... | collective-permute-start | bytes 135176 | tf_op jit(solution)/shard_map/ppermute | solution.py:53
  8.9 5.8 %collective-permute-start.3 = (f32[88,128]{1,0:T(8,128)S(1)}, f32[88,128]{1,0:T(8,128)S(1)}, u32[]{:S(2)}, u32[]{:S(2)}) collective-permute-start(f32[88,128]{1,0:T(8,128)S(1)} %get-tuple-element.28), channel_id=1, source_target_pairs={{0,4},{4,0},{8,12},{12,8},{1,5},{5,1},{9,13},{13,9},{2,6},{6,2},{1... | collective-permute-start | bytes 135176 | tf_op jit(solution)/shard_map/ppermute | solution.py:53
  11.7 3.0 %copy-start.1 = (bf16[32,768]{1,0:T(8,128)(2,1)S(1)}, bf16[32,768]{1,0:T(8,128)(2,1)}, u32[]{:S(2)}) copy-start(bf16[32,768]{1,0:T(8,128)(2,1)} %constant.10.clone.basis_rows) | copy-start | bytes 147460
  11.7 3.0 %copy-start.3 = (bf16[32,128]{1,0:T(8,128)(2,1)S(1)}, bf16[32,128]{1,0:T(8,128)(2,1)}, u32[]{:S(2)}) copy-start(bf16[32,128]{1,0:T(8,128)(2,1)} %constant.13.basis_cols) | copy-start | bytes 24580
  16.7 2.8 %copy-start.4 = (s32[16]{0:T(128)S(1)}, s32[16]{0:T(128)}, u32[]{:S(2)}) copy-start(s32[16]{0:T(128)} %param.17) | copy-start | bytes 196
  16.7 11.4 %all-to-all-start = ((f32[32,1,1152]{2,1,0:T(1,128)}), f32[32,1,1152]{2,1,0:T(1,128)S(1)}, u32[]{:S(2)}, u32[]{:S(2)}) async-start(f32[32,1,1152]{2,1,0:T(1,128)} %bitcast), calls=%async_computation | async-start | bytes 294912 | tf_op jit(solution)/shard_map/all_to_all | solution.py:797

commit v6 on v4

--- a/solution.py
+++ b/solution.py
@@ -779,7 +779,14 @@
         aliases={0: 0},
     )
     coef = coef.reshape(devices, 1, (SUB + 1) * TILE)
-    parts = lax.all_to_all(coef, ROW_AXES + COL_AXES, 0, 0, tiled=True)
+    sizes = [lax.axis_size(axis) for axis in ("col", "row", "own")]
+    members = [
+        (row * sizes[0] + col) * sizes[2] + own
+        for col in range(sizes[0])
+        for row in range(sizes[1])
+        for own in range(sizes[2])
+    ]
+    parts = lax.all_to_all(coef, ("row", "col", "own"), 0, 0, axis_index_groups=[members], tiled=True)
     state = call(
         join_kernel,
         "join",

time: 28.9 us -> 28.7 us (level)
  no operation moved by 1% of the time
where the time goes in v6:
time: 28.7 us; the launch traced here: 28.5 us
  starting transfers between devices  10.7 us (37%)
  Pallas kernels  9.36 us (33%)
  waiting for transfers between devices  7.46 us (26%)
  between operations  0.79 us (3%)
    pallas_call x7, Pallas kernels, call(): pl.pallas_call(kernel, out_shape=outs, scratch_shapes=scratch, input_outp...  9.36 us
    all_to_all x1, waiting for transfers between devices, local(): lax.all_to_all(coef, ('row', 'col', 'own'), 0, 0, axis_index_groups=[memb...  7.45 us
    ppermute x4, starting transfers between devices, swap(): return lax.ppermute(x, ('row', 'col', 'own'), pairs)  6.46 us
    all_to_all x1, starting transfers between devices, local(): lax.all_to_all(coef, ('row', 'col', 'own'), 0, 0, axis_index_groups=[memb...  4.21 us
  transfers between devices with their start and end apart: 5, of which 1 were waited for; matrix products, arithmetic and copies ran while one was open for 1% of the time, Pallas kernels for 18%

profile of v6, /device:TPU:0, one launch (start us, length us, event | category | flops | bytes accessed | tf_op | source)
XLA Modules:
  0.0 28.5 jit_solution(13716366064465508718)
XLA Ops:
  0.6 0.0 copy-start.2
  0.6 0.0 copy-start.3
  0.7 0.0 copy-start
  0.7 0.0 copy-start.1
  0.7 0.0 copy-start.4
  0.7 1.4 %ends.1 = (f32[56,128]{1,0:T(8,128)S(1)}, f32[56,128]{1,0:T(8,128)S(1)}) custom-call(f32[256,128]{1,0:T(8,128)} %visc.5, f32[256,128]{1,0:T(8,128)} %fric.5, f32[2,256,128]{2,1,0:T(8,128)} %driv.5, s32[256,128]{1,0:T(8,128)} %mask.5, f32[2,256,128]{2,1,0:T(8,128)} %obs.5), custom_call_target="tpu_custom_call" | custom-call | flops 1000000 | bytes 1000000 | tf_op jit(solution)/shard_map/ends/pallas_call | solution.py:74
  2.1 3.1 %collective-permute-start = (f32[56,128]{1,0:T(8,128)S(1)}, f32[56,128]{1,0:T(8,128)S(1)}, u32[]{:S(2)}, u32[]{:S(2)}) collective-permute-start(f32[56,128]{1,0:T(8,128)S(1)} %get-tuple-element.22), channel_id=1, source_target_pairs={{0,4},{4,0},{8,12},{12,8},{1,2},{5,6},{9,10},{13,14},{2,1},{6,5},{... | collective-permute-start | bytes 86024 | tf_op jit(solution)/shard_map/ppermute | solution.py:53
  5.2 0.0 collective-permute-start.1
  5.3 0.0 copy-done.2
  5.3 0.0 copy-done.3
  5.3 0.0 copy-done.4
  5.3 2.1 %interior.1 = (f32[768,128]{1,0:T(8,128)S(1)}, f32[256,128]{1,0:T(8,128)S(1)}, f32[256,128]{1,0:T(8,128)S(1)}, f32[256,128]{1,0:T(8,128)S(1)}, f32[256,128]{1,0:...) custom-call(f32[256,128]{1,0:T(8,128)S(1)} %copy-done.2, f32[256,128]{1,0:T(8,128)S(1)} %copy-done.3, ...), custom_call_target="tpu_custom_call" | custom-call | flops 8000000 | bytes 8000000 | tf_op jit(solution)/shard_map/interior/pallas_call | solution.py:74
  7.4 0.0 collective-permute-done.row_b
  7.4 0.0 collective-permute-done.1.row_a
  7.4 0.0 copy-start.10
  7.4 0.0 copy-start.5
  7.4 0.1 columns.1
  7.5 0.0 copy-start.7
  7.5 0.5 %collective-permute-start.2 = (f32[88,128]{1,0:T(8,128)S(1)}, f32[88,128]{1,0:T(8,128)S(1)}, u32[]{:S(2)}, u32[]{:S(2)}) collective-permute-start(f32[88,128]{1,0:T(8,128)S(1)} %get-tuple-element.33), channel_id=1, source_target_pairs={{0,1},{4,8},{8,4},{12,13},{1,0},{5,9},{9,5},{13,12},{2,3},{6,10},{... | collective-permute-start | bytes 135176 | tf_op jit(solution)/shard_map/ppermute | solution.py:53
  8.1 2.8 %collective-permute-start.3 = (f32[88,128]{1,0:T(8,128)S(1)}, f32[88,128]{1,0:T(8,128)S(1)}, u32[]{:S(2)}, u32[]{:S(2)}) collective-permute-start(f32[88,128]{1,0:T(8,128)S(1)} %get-tuple-element.34), channel_id=1, source_target_pairs={{0,4},{4,0},{8,12},{12,8},{1,5},{5,1},{9,13},{13,9},{2,6},{6,2},{1... | collective-permute-start | bytes 135176 | tf_op jit(solution)/shard_map/ppermute | solution.py:53
  10.9 0.1 copy.15.block
  11.0 0.0 copy-done.5
  11.0 0.0 copy-start.8
  11.0 2.1 %adjoint.1 = (f32[32,128]{1,0:T(8,128)S(1)}, f32[32,128]{1,0:T(8,128)S(1)}, f32[840,128]{1,0:T(8,128)S(1)}, f32[24,128]{1,0:T(8,128)S(1)}) custom-call(f32[56,128]{1,0:T(8,128)S(1)} %collective-permute-done.row_b, f32[56,128]{1,0:T(8,128)S(1)} %collective-permute-done.1.row_a, f32[256,128]{1,0:T(8,128)S(1)} %copy-done.2, f32[256,128]{1,0:T(8,128)S(1)} %copy-done.3, ...), custom_call_target="tpu_custom_call" | custom-call | flops 8000000 | bytes 8000000 | tf_op jit(solution)/shard_map/adjoint/pallas_call | solution.py:74
  13.1 0.0 collective-permute-done.2.col_b
  13.1 0.0 collective-permute-done.3.col_a
  13.1 2.0 %left_right.1 = (f32[840,128]{1,0:T(8,128)S(1)}, f32[240,128]{1,0:T(8,128)S(1)}, f32[288,128]{1,0:T(8,128)}) custom-call(f32[840,128]{1,0:T(8,128)S(1)} %get-tuple-element.31._, f32[24,128]{1,0:T(8,128)S(1)} %get-tuple-element.32.seams, f32[88,128]{1,0:T(8,128)S(1)} %collective-permute-done.2.col_b, ...), custom_call_target="tpu_custom_call", output_to_operand_aliasing={{0}: (0, {})} | custom-call | flops 4000000 | bytes 4000000 | tf_op jit(solution)/shard_map/left_right/pallas_call | solution.py:74
  15.1 4.2 %all-to-all-start = ((f32[32,1,1152]{2,1,0:T(1,128)}), f32[32,1,1152]{2,1,0:T(1,128)S(1)}, u32[]{:S(2)}, u32[]{:S(2)}) async-start(f32[32,1,1152]{2,1,0:T(1,128)} %bitcast), calls=%async_computation | async-start | bytes 294912 | tf_op jit(solution)/shard_map/all_to_all | solution.py:789
  19.3 0.1 reshape.13.owners
  19.4 0.9 %join.1 = f32[2,256,128]{2,1,0:T(8,128)} custom-call(f32[256,128]{1,0:T(8,128)S(1)} %get-tuple-element.20.v0, f32[256,128]{1,0:T(8,128)S(1)} %get-tuple-element.21.v1, f32[32,128]{1,0:T(8,128)S(1)} %get-tuple-element.30.vel_ends, f32[240,128]{1,0:T(8,128)S(1)} %get-tuple-element.36.strips), custom_call_target="tpu_custom_call" | custom-call | flops 4000000 | bytes 4000000 | tf_op jit(solution)/shard_map/join/pallas_call | solution.py:74
  20.3 7.5 %all-to-all-done = f32[32,1,1152]{2,1,0:T(1,128)S(1)} async-done(((f32[32,1,1152]{2,1,0:T(1,128)}), f32[32,1,1152]{2,1,0:T(1,128)S(1)}, u32[]{:S(2)}, u32[]{:S(2)}) %all-to-all-start) | async-done | bytes 147488 | tf_op jit(solution)/shard_map/all_to_all | solution.py:789
  27.7 0.8 %pick.1 = f32[1,4,1024]{2,1,0:T(4,128)} custom-call(s32[4,4]{1,0:T(4,128)S(1)} %reshape.13.owners, f32[288,128]{1,0:T(8,128)S(1)} %bitcast.2), custom_call_target="tpu_custom_call" | custom-call | flops 100000 | bytes 100000 | tf_op jit(solution)/shard_map/pick/pallas_call | solution.py:74
  (9 shorter events, 0.0 us)
Async XLA Ops:
  0.6 4.6 %copy-start.2 = (f32[256,128]{1,0:T(8,128)S(1)}, f32[256,128]{1,0:T(8,128)}, u32[]{:S(2)}) copy-start(f32[256,128]{1,0:T(8,128)} %visc.5) | copy-start | bytes 393220
  0.6 4.6 %copy-start.3 = (f32[256,128]{1,0:T(8,128)S(1)}, f32[256,128]{1,0:T(8,128)}, u32[]{:S(2)}) copy-start(f32[256,128]{1,0:T(8,128)} %fric.5) | copy-start | bytes 393220
  0.7 4.6 %copy-start = (f32[2,256,128]{2,1,0:T(8,128)S(1)}, f32[2,256,128]{2,1,0:T(8,128)}, u32[]{:S(2)}) copy-start(f32[2,256,128]{2,1,0:T(8,128)} %driv.5) | copy-start | bytes 786436
  0.7 4.6 %copy-start.1 = (f32[2,256,128]{2,1,0:T(8,128)S(1)}, f32[2,256,128]{2,1,0:T(8,128)}, u32[]{:S(2)}) copy-start(f32[2,256,128]{2,1,0:T(8,128)} %obs.5) | copy-start | bytes 786436
  0.7 4.6 %copy-start.4 = (s32[256,128]{1,0:T(8,128)S(1)}, s32[256,128]{1,0:T(8,128)}, u32[]{:S(2)}) copy-start(s32[256,128]{1,0:T(8,128)} %mask.5) | copy-start | bytes 393220
  2.1 5.2 %collective-permute-start = (f32[56,128]{1,0:T(8,128)S(1)}, f32[56,128]{1,0:T(8,128)S(1)}, u32[]{:S(2)}, u32[]{:S(2)}) collective-permute-start(f32[56,128]{1,0:T(8,128)S(1)} %get-tuple-element.22), channel_id=1, source_target_pairs={{0,4},{4,0},{8,12},{12,8},{1,2},{5,6},{9,10},{13,14},{2,1},{6,5},{... | collective-permute-start | bytes 86024 | tf_op jit(solution)/shard_map/ppermute | solution.py:53
  5.2 2.2 %collective-permute-start.1 = (f32[56,128]{1,0:T(8,128)S(1)}, f32[56,128]{1,0:T(8,128)S(1)}, u32[]{:S(2)}, u32[]{:S(2)}) collective-permute-start(f32[56,128]{1,0:T(8,128)S(1)} %get-tuple-element.23), channel_id=1, source_target_pairs={{0,1},{4,5},{8,9},{12,13},{1,0},{5,4},{9,8},{13,12},{2,3},{6,7},{1... | collective-permute-start | bytes 86024 | tf_op jit(solution)/shard_map/ppermute | solution.py:53
  7.4 3.5 %copy-start.10 = (s32[2,1]{0,1:T(1,128)S(1)}, s32[2,1]{0,1:T(1,128)}, u32[]{:S(2)}) copy-start(s32[2,1]{0,1:T(1,128)} %param.16) | copy-start | bytes 28
  7.4 3.6 %copy-start.5 = (f32[128,128]{1,0:T(8,128)S(1)}, f32[128,128]{1,0:T(8,128)}, u32[]{:S(2)}) copy-start(f32[128,128]{1,0:T(8,128)} %constant.9.clone.basis_q) | copy-start | bytes 196612
  7.5 3.5 %copy-start.7 = (f32[32,128]{1,0:T(8,128)S(1)}, f32[32,128]{1,0:T(8,128)}, u32[]{:S(2)}) copy-start(f32[32,128]{1,0:T(8,128)} %constant.8.clone.basis_p) | copy-start | bytes 49156
  7.5 5.6 %collective-permute-start.2 = (f32[88,128]{1,0:T(8,128)S(1)}, f32[88,128]{1,0:T(8,128)S(1)}, u32[]{:S(2)}, u32[]{:S(2)}) collective-permute-start(f32[88,128]{1,0:T(8,128)S(1)} %get-tuple-element.33), channel_id=1, source_target_pairs={{0,1},{4,8},{8,4},{12,13},{1,0},{5,9},{9,5},{13,12},{2,3},{6,10},{... | collective-permute-start | bytes 135176 | tf_op jit(solution)/shard_map/ppermute | solution.py:53
  8.1 5.1 %collective-permute-start.3 = (f32[88,128]{1,0:T(8,128)S(1)}, f32[88,128]{1,0:T(8,128)S(1)}, u32[]{:S(2)}, u32[]{:S(2)}) collective-permute-start(f32[88,128]{1,0:T(8,128)S(1)} %get-tuple-element.34), channel_id=1, source_target_pairs={{0,4},{4,0},{8,12},{12,8},{1,5},{5,1},{9,13},{13,9},{2,6},{6,2},{1... | collective-permute-start | bytes 135176 | tf_op jit(solution)/shard_map/ppermute | solution.py:53
  11.0 2.2 %copy-start.6 = (bf16[32,768]{1,0:T(8,128)(2,1)S(1)}, bf16[32,768]{1,0:T(8,128)(2,1)}, u32[]{:S(2)}) copy-start(bf16[32,768]{1,0:T(8,128)(2,1)} %constant.10.clone.basis_rows) | copy-start | bytes 147460
  11.0 2.2 %copy-start.8 = (bf16[32,128]{1,0:T(8,128)(2,1)S(1)}, bf16[32,128]{1,0:T(8,128)(2,1)}, u32[]{:S(2)}) copy-start(bf16[32,128]{1,0:T(8,128)(2,1)} %constant.13.basis_cols) | copy-start | bytes 24580
  15.1 4.2 %copy-start.9 = (s32[16]{0:T(128)S(1)}, s32[16]{0:T(128)}, u32[]{:S(2)}) copy-start(s32[16]{0:T(128)} %param.17) | copy-start | bytes 196
  15.1 12.6 %all-to-all-start = ((f32[32,1,1152]{2,1,0:T(1,128)}), f32[32,1,1152]{2,1,0:T(1,128)S(1)}, u32[]{:S(2)}, u32[]{:S(2)}) async-start(f32[32,1,1152]{2,1,0:T(1,128)} %bitcast), calls=%async_computation | async-start | bytes 294912 | tf_op jit(solution)/shard_map/all_to_all | solution.py:789

commit v7 on v6

--- a/solution.py
+++ b/solution.py
@@ -782,7 +782,7 @@
     sizes = [lax.axis_size(axis) for axis in ("col", "row", "own")]
     members = [
         (row * sizes[0] + col) * sizes[2] + own
-        for col in range(sizes[0])
+        for col in reversed(range(sizes[0]))
         for row in range(sizes[1])
         for own in range(sizes[2])
     ]

time: 28.7 us -> 29 us (1.010)
  no operation moved by 1% of the time
where the time goes in v7:
time: 29 us; the launch traced here: 28.8 us
  starting transfers between devices  10.7 us (37%)
  Pallas kernels  9.36 us (32%)
  waiting for transfers between devices  7.73 us (27%)
  between operations  0.79 us (3%)
    pallas_call x7, Pallas kernels, call(): pl.pallas_call(kernel, out_shape=outs, scratch_shapes=scratch, input_outp...  9.36 us
    all_to_all x1, waiting for transfers between devices, local(): lax.all_to_all(coef, ('row', 'col', 'own'), 0, 0, axis_index_groups=[memb...  7.72 us
    ppermute x4, starting transfers between devices, swap(): return lax.ppermute(x, ('row', 'col', 'own'), pairs)  6.46 us
    all_to_all x1, starting transfers between devices, local(): lax.all_to_all(coef, ('row', 'col', 'own'), 0, 0, axis_index_groups=[memb...  4.21 us
  transfers between devices with their start and end apart: 5, of which 1 were waited for; matrix products, arithmetic and copies ran while one was open for 1% of the time, Pallas kernels for 18%

profile of v7, /device:TPU:0, one launch (start us, length us, event | category | flops | bytes accessed | tf_op | source)
XLA Modules:
  0.0 28.8 jit_solution(12230405245233917799)
XLA Ops:
  0.6 0.0 copy-start.2
  0.6 0.0 copy-start.3
  0.7 0.0 copy-start
  0.7 0.0 copy-start.1
  0.7 0.0 copy-start.4
  0.7 1.4 %ends.1 = (f32[56,128]{1,0:T(8,128)S(1)}, f32[56,128]{1,0:T(8,128)S(1)}) custom-call(f32[256,128]{1,0:T(8,128)} %visc.5, f32[256,128]{1,0:T(8,128)} %fric.5, f32[2,256,128]{2,1,0:T(8,128)} %driv.5, s32[256,128]{1,0:T(8,128)} %mask.5, f32[2,256,128]{2,1,0:T(8,128)} %obs.5), custom_call_target="tpu_custom_call" | custom-call | flops 1000000 | bytes 1000000 | tf_op jit(solution)/shard_map/ends/pallas_call | solution.py:74
  2.1 3.1 %collective-permute-start = (f32[56,128]{1,0:T(8,128)S(1)}, f32[56,128]{1,0:T(8,128)S(1)}, u32[]{:S(2)}, u32[]{:S(2)}) collective-permute-start(f32[56,128]{1,0:T(8,128)S(1)} %get-tuple-element.22), channel_id=1, source_target_pairs={{0,4},{4,0},{8,12},{12,8},{1,2},{5,6},{9,10},{13,14},{2,1},{6,5},{... | collective-permute-start | bytes 86024 | tf_op jit(solution)/shard_map/ppermute | solution.py:53
  5.2 0.0 collective-permute-start.1
  5.3 0.0 copy-done.2
  5.3 0.0 copy-done.3
  5.3 0.0 copy-done.4
  5.3 2.1 %interior.1 = (f32[768,128]{1,0:T(8,128)S(1)}, f32[256,128]{1,0:T(8,128)S(1)}, f32[256,128]{1,0:T(8,128)S(1)}, f32[256,128]{1,0:T(8,128)S(1)}, f32[256,128]{1,0:...) custom-call(f32[256,128]{1,0:T(8,128)S(1)} %copy-done.2, f32[256,128]{1,0:T(8,128)S(1)} %copy-done.3, ...), custom_call_target="tpu_custom_call" | custom-call | flops 8000000 | bytes 8000000 | tf_op jit(solution)/shard_map/interior/pallas_call | solution.py:74
  7.4 0.0 collective-permute-done.row_b
  7.4 0.0 collective-permute-done.1.row_a
  7.4 0.0 copy-start.10
  7.4 0.0 copy-start.5
  7.4 0.1 columns.1
  7.5 0.0 copy-start.7
  7.5 0.5 %collective-permute-start.2 = (f32[88,128]{1,0:T(8,128)S(1)}, f32[88,128]{1,0:T(8,128)S(1)}, u32[]{:S(2)}, u32[]{:S(2)}) collective-permute-start(f32[88,128]{1,0:T(8,128)S(1)} %get-tuple-element.33), channel_id=1, source_target_pairs={{0,1},{4,8},{8,4},{12,13},{1,0},{5,9},{9,5},{13,12},{2,3},{6,10},{... | collective-permute-start | bytes 135176 | tf_op jit(solution)/shard_map/ppermute | solution.py:53
  8.1 2.8 %collective-permute-start.3 = (f32[88,128]{1,0:T(8,128)S(1)}, f32[88,128]{1,0:T(8,128)S(1)}, u32[]{:S(2)}, u32[]{:S(2)}) collective-permute-start(f32[88,128]{1,0:T(8,128)S(1)} %get-tuple-element.34), channel_id=1, source_target_pairs={{0,4},{4,0},{8,12},{12,8},{1,5},{5,1},{9,13},{13,9},{2,6},{6,2},{1... | collective-permute-start | bytes 135176 | tf_op jit(solution)/shard_map/ppermute | solution.py:53
  10.9 0.1 copy.15.block
  11.0 0.0 copy-done.5
  11.0 0.0 copy-start.8
  11.0 2.1 %adjoint.1 = (f32[32,128]{1,0:T(8,128)S(1)}, f32[32,128]{1,0:T(8,128)S(1)}, f32[840,128]{1,0:T(8,128)S(1)}, f32[24,128]{1,0:T(8,128)S(1)}) custom-call(f32[56,128]{1,0:T(8,128)S(1)} %collective-permute-done.row_b, f32[56,128]{1,0:T(8,128)S(1)} %collective-permute-done.1.row_a, f32[256,128]{1,0:T(8,128)S(1)} %copy-done.2, f32[256,128]{1,0:T(8,128)S(1)} %copy-done.3, ...), custom_call_target="tpu_custom_call" | custom-call | flops 8000000 | bytes 8000000 | tf_op jit(solution)/shard_map/adjoint/pallas_call | solution.py:74
  13.1 0.0 collective-permute-done.2.col_b
  13.1 0.0 collective-permute-done.3.col_a
  13.1 2.0 %left_right.1 = (f32[840,128]{1,0:T(8,128)S(1)}, f32[240,128]{1,0:T(8,128)S(1)}, f32[288,128]{1,0:T(8,128)}) custom-call(f32[840,128]{1,0:T(8,128)S(1)} %get-tuple-element.31._, f32[24,128]{1,0:T(8,128)S(1)} %get-tuple-element.32.seams, f32[88,128]{1,0:T(8,128)S(1)} %collective-permute-done.2.col_b, ...), custom_call_target="tpu_custom_call", output_to_operand_aliasing={{0}: (0, {})} | custom-call | flops 4000000 | bytes 4000000 | tf_op jit(solution)/shard_map/left_right/pallas_call | solution.py:74
  15.1 4.2 %all-to-all-start = ((f32[32,1,1152]{2,1,0:T(1,128)}), f32[32,1,1152]{2,1,0:T(1,128)S(1)}, u32[]{:S(2)}, u32[]{:S(2)}) async-start(f32[32,1,1152]{2,1,0:T(1,128)} %bitcast), calls=%async_computation | async-start | bytes 294912 | tf_op jit(solution)/shard_map/all_to_all | solution.py:789
  19.3 0.1 reshape.13.owners
  19.4 0.9 %join.1 = f32[2,256,128]{2,1,0:T(8,128)} custom-call(f32[256,128]{1,0:T(8,128)S(1)} %get-tuple-element.20.v0, f32[256,128]{1,0:T(8,128)S(1)} %get-tuple-element.21.v1, f32[32,128]{1,0:T(8,128)S(1)} %get-tuple-element.30.vel_ends, f32[240,128]{1,0:T(8,128)S(1)} %get-tuple-element.36.strips), custom_call_target="tpu_custom_call" | custom-call | flops 4000000 | bytes 4000000 | tf_op jit(solution)/shard_map/join/pallas_call | solution.py:74
  20.3 7.7 %all-to-all-done = f32[32,1,1152]{2,1,0:T(1,128)S(1)} async-done(((f32[32,1,1152]{2,1,0:T(1,128)}), f32[32,1,1152]{2,1,0:T(1,128)S(1)}, u32[]{:S(2)}, u32[]{:S(2)}) %all-to-all-start) | async-done | bytes 147488 | tf_op jit(solution)/shard_map/all_to_all | solution.py:789
  28.0 0.8 %pick.1 = f32[1,4,1024]{2,1,0:T(4,128)} custom-call(s32[4,4]{1,0:T(4,128)S(1)} %reshape.13.owners, f32[288,128]{1,0:T(8,128)S(1)} %bitcast.2), custom_call_target="tpu_custom_call" | custom-call | flops 100000 | bytes 100000 | tf_op jit(solution)/shard_map/pick/pallas_call | solution.py:74
  (9 shorter events, 0.0 us)
Async XLA Ops:
  0.6 4.6 %copy-start.2 = (f32[256,128]{1,0:T(8,128)S(1)}, f32[256,128]{1,0:T(8,128)}, u32[]{:S(2)}) copy-start(f32[256,128]{1,0:T(8,128)} %visc.5) | copy-start | bytes 393220
  0.6 4.6 %copy-start.3 = (f32[256,128]{1,0:T(8,128)S(1)}, f32[256,128]{1,0:T(8,128)}, u32[]{:S(2)}) copy-start(f32[256,128]{1,0:T(8,128)} %fric.5) | copy-start | bytes 393220
  0.7 4.6 %copy-start = (f32[2,256,128]{2,1,0:T(8,128)S(1)}, f32[2,256,128]{2,1,0:T(8,128)}, u32[]{:S(2)}) copy-start(f32[2,256,128]{2,1,0:T(8,128)} %driv.5) | copy-start | bytes 786436
  0.7 4.6 %copy-start.1 = (f32[2,256,128]{2,1,0:T(8,128)S(1)}, f32[2,256,128]{2,1,0:T(8,128)}, u32[]{:S(2)}) copy-start(f32[2,256,128]{2,1,0:T(8,128)} %obs.5) | copy-start | bytes 786436
  0.7 4.6 %copy-start.4 = (s32[256,128]{1,0:T(8,128)S(1)}, s32[256,128]{1,0:T(8,128)}, u32[]{:S(2)}) copy-start(s32[256,128]{1,0:T(8,128)} %mask.5) | copy-start | bytes 393220
  2.1 5.2 %collective-permute-start = (f32[56,128]{1,0:T(8,128)S(1)}, f32[56,128]{1,0:T(8,128)S(1)}, u32[]{:S(2)}, u32[]{:S(2)}) collective-permute-start(f32[56,128]{1,0:T(8,128)S(1)} %get-tuple-element.22), channel_id=1, source_target_pairs={{0,4},{4,0},{8,12},{12,8},{1,2},{5,6},{9,10},{13,14},{2,1},{6,5},{... | collective-permute-start | bytes 86024 | tf_op jit(solution)/shard_map/ppermute | solution.py:53
  5.2 2.2 %collective-permute-start.1 = (f32[56,128]{1,0:T(8,128)S(1)}, f32[56,128]{1,0:T(8,128)S(1)}, u32[]{:S(2)}, u32[]{:S(2)}) collective-permute-start(f32[56,128]{1,0:T(8,128)S(1)} %get-tuple-element.23), channel_id=1, source_target_pairs={{0,1},{4,5},{8,9},{12,13},{1,0},{5,4},{9,8},{13,12},{2,3},{6,7},{1... | collective-permute-start | bytes 86024 | tf_op jit(solution)/shard_map/ppermute | solution.py:53
  7.4 3.5 %copy-start.10 = (s32[2,1]{0,1:T(1,128)S(1)}, s32[2,1]{0,1:T(1,128)}, u32[]{:S(2)}) copy-start(s32[2,1]{0,1:T(1,128)} %param.16) | copy-start | bytes 28
  7.4 3.6 %copy-start.5 = (f32[128,128]{1,0:T(8,128)S(1)}, f32[128,128]{1,0:T(8,128)}, u32[]{:S(2)}) copy-start(f32[128,128]{1,0:T(8,128)} %constant.9.clone.basis_q) | copy-start | bytes 196612
  7.5 3.5 %copy-start.7 = (f32[32,128]{1,0:T(8,128)S(1)}, f32[32,128]{1,0:T(8,128)}, u32[]{:S(2)}) copy-start(f32[32,128]{1,0:T(8,128)} %constant.8.clone.basis_p) | copy-start | bytes 49156
  7.5 5.6 %collective-permute-start.2 = (f32[88,128]{1,0:T(8,128)S(1)}, f32[88,128]{1,0:T(8,128)S(1)}, u32[]{:S(2)}, u32[]{:S(2)}) collective-permute-start(f32[88,128]{1,0:T(8,128)S(1)} %get-tuple-element.33), channel_id=1, source_target_pairs={{0,1},{4,8},{8,4},{12,13},{1,0},{5,9},{9,5},{13,12},{2,3},{6,10},{... | collective-permute-start | bytes 135176 | tf_op jit(solution)/shard_map/ppermute | solution.py:53
  8.1 5.1 %collective-permute-start.3 = (f32[88,128]{1,0:T(8,128)S(1)}, f32[88,128]{1,0:T(8,128)S(1)}, u32[]{:S(2)}, u32[]{:S(2)}) collective-permute-start(f32[88,128]{1,0:T(8,128)S(1)} %get-tuple-element.34), channel_id=1, source_target_pairs={{0,4},{4,0},{8,12},{12,8},{1,5},{5,1},{9,13},{13,9},{2,6},{6,2},{1... | collective-permute-start | bytes 135176 | tf_op jit(solution)/shard_map/ppermute | solution.py:53
  11.0 2.2 %copy-start.6 = (bf16[32,768]{1,0:T(8,128)(2,1)S(1)}, bf16[32,768]{1,0:T(8,128)(2,1)}, u32[]{:S(2)}) copy-start(bf16[32,768]{1,0:T(8,128)(2,1)} %constant.10.clone.basis_rows) | copy-start | bytes 147460
  11.0 2.2 %copy-start.8 = (bf16[32,128]{1,0:T(8,128)(2,1)S(1)}, bf16[32,128]{1,0:T(8,128)(2,1)}, u32[]{:S(2)}) copy-start(bf16[32,128]{1,0:T(8,128)(2,1)} %constant.13.basis_cols) | copy-start | bytes 24580
  15.1 4.2 %copy-start.9 = (s32[16]{0:T(128)S(1)}, s32[16]{0:T(128)}, u32[]{:S(2)}) copy-start(s32[16]{0:T(128)} %param.17) | copy-start | bytes 196
  15.1 12.9 %all-to-all-start = ((f32[32,1,1152]{2,1,0:T(1,128)}), f32[32,1,1152]{2,1,0:T(1,128)S(1)}, u32[]{:S(2)}, u32[]{:S(2)}) async-start(f32[32,1,1152]{2,1,0:T(1,128)} %bitcast), calls=%async_computation | async-start | bytes 294912 | tf_op jit(solution)/shard_map/all_to_all | solution.py:789

commit v8 on v6

--- a/solution.py
+++ b/solution.py
@@ -272,30 +272,36 @@
 def ends_kernel(visc, fric, driv, mask, obs, to_b, to_a, one, two, flags, sems):
     rows = visc.shape[0]
     copies = []
-    for e, first in enumerate((0, rows - HALO)):
-        at = pl.ds(first, HALO)
-        pieces = [
-            (visc.at[at], one.at[e, 0]),
-            (fric.at[at], one.at[e, 1]),
-            (driv.at[:, at], two.at[e, 0]),
-            (mask.at[at], flags.at[e]),
-            (obs.at[:, at], two.at[e, 1]),
-        ]
-        for n, (source, place) in enumerate(pieces):
+    for n in range(5):
+        for e, first in enumerate((0, rows - HALO)):
+            at = pl.ds(first, HALO)
+            source, place = [
+                (visc.at[at], one.at[e, 0]),
+                (fric.at[at], one.at[e, 1]),
+                (mask.at[at], flags.at[e]),
+                (driv.at[:, at], two.at[e, 0]),
+                (obs.at[:, at], two.at[e, 1]),
+            ][n]
             copies.append(pltpu.make_async_copy(source, place, sems.at[e, n]))
     for copy in copies:
         copy.start()
-    for copy in copies:
-        copy.wait()
     even, at_end = position(ROW_AXES)
 
-    def edge(e):
-        return [one[e, 0], one[e, 1], two[e, 0, 0], two[e, 0, 1], flags[e].astype(F32), two[e, 1, 0], two[e, 1, 1]]
-
-    for a, (head, tail) in enumerate(zip(edge(0), edge(1))):
+    def put(a, head, tail):
         at = slice(HALO * a, HALO * (a + 1))
         to_a[at, :] = jnp.where(even, tail, head)
         to_b[at, :] = jnp.where(at_end, 0.0, jnp.where(even, head, tail))
+
+    for n in range(5):
+        copies[2 * n].wait()
+        copies[2 * n + 1].wait()
+        if n < 2:
+            put((VISC, FRIC)[n], one[0, n], one[1, n])
+        elif n == 2:
+            put(MASK, flags[0].astype(F32), flags[1].astype(F32))
+        else:
+            for k in range(2):
+                put((DRIV, OBS)[n - 3] + k, two[0, n - 3, k], two[1, n - 3, k])
 
 
 def field_of(visc, fric, driv, mask, obs):

time: 28.7 us -> 28.7 us (level)
  no operation moved by 1% of the time
where the time goes in v8:
time: 28.7 us; the launch traced here: 28.5 us
  starting transfers between devices  10.7 us (37%)
  Pallas kernels  9.36 us (33%)
  waiting for transfers between devices  7.46 us (26%)
  between operations  0.79 us (3%)
    pallas_call x7, Pallas kernels, call(): pl.pallas_call(kernel, out_shape=outs, scratch_shapes=scratch, input_outp...  9.36 us
    all_to_all x1, waiting for transfers between devices, local(): lax.all_to_all(coef, ('row', 'col', 'own'), 0, 0, axis_index_groups=[memb...  7.45 us
    ppermute x4, starting transfers between devices, swap(): return lax.ppermute(x, ('row', 'col', 'own'), pairs)  6.46 us
    all_to_all x1, starting transfers between devices, local(): lax.all_to_all(coef, ('row', 'col', 'own'), 0, 0, axis_index_groups=[memb...  4.21 us
  transfers between devices with their start and end apart: 5, of which 1 were waited for; matrix products, arithmetic and copies ran while one was open for 1% of the time, Pallas kernels for 18%

profile of v8, /device:TPU:0, one launch (start us, length us, event | category | flops | bytes accessed | tf_op | source)
XLA Modules:
  0.0 28.5 jit_solution(11711678584624928741)
XLA Ops:
  0.6 0.0 copy-start.2
  0.6 0.0 copy-start.3
  0.7 0.0 copy-start
  0.7 0.0 copy-start.1
  0.7 0.0 copy-start.4
  0.7 1.5 %ends.1 = (f32[56,128]{1,0:T(8,128)S(1)}, f32[56,128]{1,0:T(8,128)S(1)}) custom-call(f32[256,128]{1,0:T(8,128)} %visc.5, f32[256,128]{1,0:T(8,128)} %fric.5, f32[2,256,128]{2,1,0:T(8,128)} %driv.5, s32[256,128]{1,0:T(8,128)} %mask.5, f32[2,256,128]{2,1,0:T(8,128)} %obs.5), custom_call_target="tpu_custom_call" | custom-call | flops 1000000 | bytes 1000000 | tf_op jit(solution)/shard_map/ends/pallas_call | solution.py:74
  2.1 3.1 %collective-permute-start = (f32[56,128]{1,0:T(8,128)S(1)}, f32[56,128]{1,0:T(8,128)S(1)}, u32[]{:S(2)}, u32[]{:S(2)}) collective-permute-start(f32[56,128]{1,0:T(8,128)S(1)} %get-tuple-element.22), channel_id=1, source_target_pairs={{0,4},{4,0},{8,12},{12,8},{1,2},{5,6},{9,10},{13,14},{2,1},{6,5},{... | collective-permute-start | bytes 86024 | tf_op jit(solution)/shard_map/ppermute | solution.py:53
  5.2 0.0 collective-permute-start.1
  5.3 0.0 copy-done
  5.3 2.1 %interior.1 = (f32[768,128]{1,0:T(8,128)S(1)}, f32[256,128]{1,0:T(8,128)S(1)}, f32[256,128]{1,0:T(8,128)S(1)}, f32[256,128]{1,0:T(8,128)S(1)}, f32[256,128]{1,0:...) custom-call(f32[256,128]{1,0:T(8,128)S(1)} %copy-done.2, f32[256,128]{1,0:T(8,128)S(1)} %copy-done.3, ...), custom_call_target="tpu_custom_call" | custom-call | flops 8000000 | bytes 8000000 | tf_op jit(solution)/shard_map/interior/pallas_call | solution.py:74
  7.4 0.0 collective-permute-done.row_b
  7.4 0.0 collective-permute-done.1.row_a
  7.4 0.0 copy-start.10
  7.4 0.0 copy-start.5
  7.4 0.1 columns.1
  7.5 0.0 copy-start.7
  7.5 0.5 %collective-permute-start.2 = (f32[88,128]{1,0:T(8,128)S(1)}, f32[88,128]{1,0:T(8,128)S(1)}, u32[]{:S(2)}, u32[]{:S(2)}) collective-permute-start(f32[88,128]{1,0:T(8,128)S(1)} %get-tuple-element.33), channel_id=1, source_target_pairs={{0,1},{4,8},{8,4},{12,13},{1,0},{5,9},{9,5},{13,12},{2,3},{6,10},{... | collective-permute-start | bytes 135176 | tf_op jit(solution)/shard_map/ppermute | solution.py:53
  8.1 2.8 %collective-permute-start.3 = (f32[88,128]{1,0:T(8,128)S(1)}, f32[88,128]{1,0:T(8,128)S(1)}, u32[]{:S(2)}, u32[]{:S(2)}) collective-permute-start(f32[88,128]{1,0:T(8,128)S(1)} %get-tuple-element.34), channel_id=1, source_target_pairs={{0,4},{4,0},{8,12},{12,8},{1,5},{5,1},{9,13},{13,9},{2,6},{6,2},{1... | collective-permute-start | bytes 135176 | tf_op jit(solution)/shard_map/ppermute | solution.py:53
  10.9 0.1 copy.15.block
  11.0 0.0 copy-start.8
  11.0 2.1 %adjoint.1 = (f32[32,128]{1,0:T(8,128)S(1)}, f32[32,128]{1,0:T(8,128)S(1)}, f32[840,128]{1,0:T(8,128)S(1)}, f32[24,128]{1,0:T(8,128)S(1)}) custom-call(f32[56,128]{1,0:T(8,128)S(1)} %collective-permute-done.row_b, f32[56,128]{1,0:T(8,128)S(1)} %collective-permute-done.1.row_a, f32[256,128]{1,0:T(8,128)S(1)} %copy-done.2, f32[256,128]{1,0:T(8,128)S(1)} %copy-done.3, ...), custom_call_target="tpu_custom_call" | custom-call | flops 8000000 | bytes 8000000 | tf_op jit(solution)/shard_map/adjoint/pallas_call | solution.py:74
  13.1 0.0 collective-permute-done.2.col_b
  13.1 0.0 collective-permute-done.3.col_a
  13.1 0.0 copy-done.6
  13.1 0.0 copy-done.8
  13.2 2.0 %left_right.1 = (f32[840,128]{1,0:T(8,128)S(1)}, f32[240,128]{1,0:T(8,128)S(1)}, f32[288,128]{1,0:T(8,128)}) custom-call(f32[840,128]{1,0:T(8,128)S(1)} %get-tuple-element.31._, f32[24,128]{1,0:T(8,128)S(1)} %get-tuple-element.32.seams, f32[88,128]{1,0:T(8,128)S(1)} %collective-permute-done.2.col_b, ...), custom_call_target="tpu_custom_call", output_to_operand_aliasing={{0}: (0, {})} | custom-call | flops 4000000 | bytes 4000000 | tf_op jit(solution)/shard_map/left_right/pallas_call | solution.py:74
  15.1 4.2 %all-to-all-start = ((f32[32,1,1152]{2,1,0:T(1,128)}), f32[32,1,1152]{2,1,0:T(1,128)S(1)}, u32[]{:S(2)}, u32[]{:S(2)}) async-start(f32[32,1,1152]{2,1,0:T(1,128)} %bitcast), calls=%async_computation | async-start | bytes 294912 | tf_op jit(solution)/shard_map/all_to_all | solution.py:795
  19.3 0.0 copy-done.9
  19.4 0.1 reshape.13.owners
  19.4 0.9 %join.1 = f32[2,256,128]{2,1,0:T(8,128)} custom-call(f32[256,128]{1,0:T(8,128)S(1)} %get-tuple-element.20.v0, f32[256,128]{1,0:T(8,128)S(1)} %get-tuple-element.21.v1, f32[32,128]{1,0:T(8,128)S(1)} %get-tuple-element.30.vel_ends, f32[240,128]{1,0:T(8,128)S(1)} %get-tuple-element.36.strips), custom_call_target="tpu_custom_call" | custom-call | flops 4000000 | bytes 4000000 | tf_op jit(solution)/shard_map/join/pallas_call | solution.py:74
  20.3 7.5 %all-to-all-done = f32[32,1,1152]{2,1,0:T(1,128)S(1)} async-done(((f32[32,1,1152]{2,1,0:T(1,128)}), f32[32,1,1152]{2,1,0:T(1,128)S(1)}, u32[]{:S(2)}, u32[]{:S(2)}) %all-to-all-start) | async-done | bytes 147488 | tf_op jit(solution)/shard_map/all_to_all | solution.py:795
  27.8 0.8 %pick.1 = f32[1,4,1024]{2,1,0:T(4,128)} custom-call(s32[4,4]{1,0:T(4,128)S(1)} %reshape.13.owners, f32[288,128]{1,0:T(8,128)S(1)} %bitcast.2), custom_call_target="tpu_custom_call" | custom-call | flops 100000 | bytes 100000 | tf_op jit(solution)/shard_map/pick/pallas_call | solution.py:74
  (9 shorter events, 0.0 us)
Async XLA Ops:
  0.6 4.6 %copy-start.2 = (f32[256,128]{1,0:T(8,128)S(1)}, f32[256,128]{1,0:T(8,128)}, u32[]{:S(2)}) copy-start(f32[256,128]{1,0:T(8,128)} %visc.5) | copy-start | bytes 393220
  0.6 4.6 %copy-start.3 = (f32[256,128]{1,0:T(8,128)S(1)}, f32[256,128]{1,0:T(8,128)}, u32[]{:S(2)}) copy-start(f32[256,128]{1,0:T(8,128)} %fric.5) | copy-start | bytes 393220
  0.7 4.6 %copy-start = (f32[2,256,128]{2,1,0:T(8,128)S(1)}, f32[2,256,128]{2,1,0:T(8,128)}, u32[]{:S(2)}) copy-start(f32[2,256,128]{2,1,0:T(8,128)} %driv.5) | copy-start | bytes 786436
  0.7 4.6 %copy-start.1 = (f32[2,256,128]{2,1,0:T(8,128)S(1)}, f32[2,256,128]{2,1,0:T(8,128)}, u32[]{:S(2)}) copy-start(f32[2,256,128]{2,1,0:T(8,128)} %obs.5) | copy-start | bytes 786436
  0.7 4.6 %copy-start.4 = (s32[256,128]{1,0:T(8,128)S(1)}, s32[256,128]{1,0:T(8,128)}, u32[]{:S(2)}) copy-start(s32[256,128]{1,0:T(8,128)} %mask.5) | copy-start | bytes 393220
  2.1 5.2 %collective-permute-start = (f32[56,128]{1,0:T(8,128)S(1)}, f32[56,128]{1,0:T(8,128)S(1)}, u32[]{:S(2)}, u32[]{:S(2)}) collective-permute-start(f32[56,128]{1,0:T(8,128)S(1)} %get-tuple-element.22), channel_id=1, source_target_pairs={{0,4},{4,0},{8,12},{12,8},{1,2},{5,6},{9,10},{13,14},{2,1},{6,5},{... | collective-permute-start | bytes 86024 | tf_op jit(solution)/shard_map/ppermute | solution.py:53
  5.2 2.2 %collective-permute-start.1 = (f32[56,128]{1,0:T(8,128)S(1)}, f32[56,128]{1,0:T(8,128)S(1)}, u32[]{:S(2)}, u32[]{:S(2)}) collective-permute-start(f32[56,128]{1,0:T(8,128)S(1)} %get-tuple-element.23), channel_id=1, source_target_pairs={{0,1},{4,5},{8,9},{12,13},{1,0},{5,4},{9,8},{13,12},{2,3},{6,7},{1... | collective-permute-start | bytes 86024 | tf_op jit(solution)/shard_map/ppermute | solution.py:53
  7.4 3.5 %copy-start.10 = (s32[2,1]{0,1:T(1,128)S(1)}, s32[2,1]{0,1:T(1,128)}, u32[]{:S(2)}) copy-start(s32[2,1]{0,1:T(1,128)} %param.16) | copy-start | bytes 28
  7.4 3.6 %copy-start.5 = (f32[128,128]{1,0:T(8,128)S(1)}, f32[128,128]{1,0:T(8,128)}, u32[]{:S(2)}) copy-start(f32[128,128]{1,0:T(8,128)} %constant.9.clone.basis_q) | copy-start | bytes 196612
  7.5 3.5 %copy-start.7 = (f32[32,128]{1,0:T(8,128)S(1)}, f32[32,128]{1,0:T(8,128)}, u32[]{:S(2)}) copy-start(f32[32,128]{1,0:T(8,128)} %constant.8.clone.basis_p) | copy-start | bytes 49156
  7.5 5.6 %collective-permute-start.2 = (f32[88,128]{1,0:T(8,128)S(1)}, f32[88,128]{1,0:T(8,128)S(1)}, u32[]{:S(2)}, u32[]{:S(2)}) collective-permute-start(f32[88,128]{1,0:T(8,128)S(1)} %get-tuple-element.33), channel_id=1, source_target_pairs={{0,1},{4,8},{8,4},{12,13},{1,0},{5,9},{9,5},{13,12},{2,3},{6,10},{... | collective-permute-start | bytes 135176 | tf_op jit(solution)/shard_map/ppermute | solution.py:53
  8.1 5.1 %collective-permute-start.3 = (f32[88,128]{1,0:T(8,128)S(1)}, f32[88,128]{1,0:T(8,128)S(1)}, u32[]{:S(2)}, u32[]{:S(2)}) collective-permute-start(f32[88,128]{1,0:T(8,128)S(1)} %get-tuple-element.34), channel_id=1, source_target_pairs={{0,4},{4,0},{8,12},{12,8},{1,5},{5,1},{9,13},{13,9},{2,6},{6,2},{1... | collective-permute-start | bytes 135176 | tf_op jit(solution)/shard_map/ppermute | solution.py:53
  11.0 2.2 %copy-start.6 = (bf16[32,768]{1,0:T(8,128)(2,1)S(1)}, bf16[32,768]{1,0:T(8,128)(2,1)}, u32[]{:S(2)}) copy-start(bf16[32,768]{1,0:T(8,128)(2,1)} %constant.10.clone.basis_rows) | copy-start | bytes 147460
  11.0 2.2 %copy-start.8 = (bf16[32,128]{1,0:T(8,128)(2,1)S(1)}, bf16[32,128]{1,0:T(8,128)(2,1)}, u32[]{:S(2)}) copy-start(bf16[32,128]{1,0:T(8,128)(2,1)} %constant.13.basis_cols) | copy-start | bytes 24580
  15.1 4.2 %copy-start.9 = (s32[16]{0:T(128)S(1)}, s32[16]{0:T(128)}, u32[]{:S(2)}) copy-start(s32[16]{0:T(128)} %param.17) | copy-start | bytes 196
  15.1 12.6 %all-to-all-start = ((f32[32,1,1152]{2,1,0:T(1,128)}), f32[32,1,1152]{2,1,0:T(1,128)S(1)}, u32[]{:S(2)}, u32[]{:S(2)}) async-start(f32[32,1,1152]{2,1,0:T(1,128)} %bitcast), calls=%async_computation | async-start | bytes 294912 | tf_op jit(solution)/shard_map/all_to_all | solution.py:795

commit v9 on v6

--- a/solution.py
+++ b/solution.py
@@ -523,7 +523,7 @@
 
 
 def left_right_kernel(
-    _, seams, col_b, col_a, wide_in, block, basis_rows, basis_cols,
+    _, seams, col_a, col_b, wide_in, block, basis_rows, basis_cols,
     stack, strips, coef,
     plain, *refs,
 ):
@@ -770,8 +770,8 @@
         4 * 10**6,
         sides,
         seams,
+        col_a,
         col_b,
-        col_a,
         wide,
         tile_block,
         basis_rows,

time: 28.7 us -> 29.2 us (1.017)
  starting transfers between devices: 10.7 us -> 11.1 us
    all_to_all x1, starting transfers between devices: 4.21 us -> 6.2 us  [local(): lax.all_to_all(coef, ('row', 'col', 'own'), 0, 0, axis_index_groups=[memb...]
    ppermute x4, starting transfers between devices: 6.46 us -> 4.87 us  [swap(): return lax.ppermute(x, ('row', 'col', 'own'), pairs)]
  transfers between devices with their start and end apart: 5 -> 5, of which waited for: 1 -> 2; matrix products, arithmetic and copies ran while one was open for 1% -> 1% of each run, Pallas kernels for 18% -> 18%
where the time goes in v9:
time: 29.2 us; the launch traced here: 29 us
  starting transfers between devices  11.1 us (38%)
  Pallas kernels  9.36 us (32%)
  waiting for transfers between devices  7.56 us (26%)
  between operations  0.77 us (3%)
    pallas_call x7, Pallas kernels, call(): pl.pallas_call(kernel, out_shape=outs, scratch_shapes=scratch, input_outp...  9.36 us
    all_to_all x1, waiting for transfers between devices, local(): lax.all_to_all(coef, ('row', 'col', 'own'), 0, 0, axis_index_groups=[memb...  7.45 us
    all_to_all x1, starting transfers between devices, local(): lax.all_to_all(coef, ('row', 'col', 'own'), 0, 0, axis_index_groups=[memb...  6.2 us
    ppermute x4, starting transfers between devices, swap(): return lax.ppermute(x, ('row', 'col', 'own'), pairs)  4.87 us
  transfers between devices with their start and end apart: 5, of which 2 were waited for; matrix products, arithmetic and copies ran while one was open for 1% of the time, Pallas kernels for 18%

profile of v9, /device:TPU:0, one launch (start us, length us, event | category | flops | bytes accessed | tf_op | source)
XLA Modules:
  0.0 29.0 jit_solution(2437573302401557075)
XLA Ops:
  0.6 0.0 copy-start.2
  0.6 0.0 copy-start.3
  0.7 0.0 copy-start
  0.7 0.0 copy-start.1
  0.7 0.0 copy-start.4
  0.7 1.4 %ends.1 = (f32[56,128]{1,0:T(8,128)S(1)}, f32[56,128]{1,0:T(8,128)S(1)}) custom-call(f32[256,128]{1,0:T(8,128)} %visc.5, f32[256,128]{1,0:T(8,128)} %fric.5, f32[2,256,128]{2,1,0:T(8,128)} %driv.5, s32[256,128]{1,0:T(8,128)} %mask.5, f32[2,256,128]{2,1,0:T(8,128)} %obs.5), custom_call_target="tpu_custom_call" | custom-call | flops 1000000 | bytes 1000000 | tf_op jit(solution)/shard_map/ends/pallas_call | solution.py:74
  2.1 3.1 %collective-permute-start = (f32[56,128]{1,0:T(8,128)S(1)}, f32[56,128]{1,0:T(8,128)S(1)}, u32[]{:S(2)}, u32[]{:S(2)}) collective-permute-start(f32[56,128]{1,0:T(8,128)S(1)} %get-tuple-element.22), channel_id=1, source_target_pairs={{0,4},{4,0},{8,12},{12,8},{1,2},{5,6},{9,10},{13,14},{2,1},{6,5},{... | collective-permute-start | bytes 86024 | tf_op jit(solution)/shard_map/ppermute | solution.py:53
  5.2 0.0 collective-permute-start.1
  5.3 0.0 copy-done.2
  5.3 0.0 copy-done.3
  5.3 0.0 copy-done.4
  5.3 2.1 %interior.1 = (f32[768,128]{1,0:T(8,128)S(1)}, f32[256,128]{1,0:T(8,128)S(1)}, f32[256,128]{1,0:T(8,128)S(1)}, f32[256,128]{1,0:T(8,128)S(1)}, f32[256,128]{1,0:...) custom-call(f32[256,128]{1,0:T(8,128)S(1)} %copy-done.2, f32[256,128]{1,0:T(8,128)S(1)} %copy-done.3, ...), custom_call_target="tpu_custom_call" | custom-call | flops 8000000 | bytes 8000000 | tf_op jit(solution)/shard_map/interior/pallas_call | solution.py:74
  7.4 0.0 collective-permute-done.row_b
  7.4 0.0 collective-permute-done.1.row_a
  7.4 0.0 copy-start.10
  7.4 0.0 copy-start.5
  7.4 0.1 columns.1
  7.5 0.0 copy-start.7
  7.5 1.8 %collective-permute-start.2 = (f32[88,128]{1,0:T(8,128)S(1)}, f32[88,128]{1,0:T(8,128)S(1)}, u32[]{:S(2)}, u32[]{:S(2)}) collective-permute-start(f32[88,128]{1,0:T(8,128)S(1)} %get-tuple-element.33), channel_id=1, source_target_pairs={{0,4},{4,0},{8,12},{12,8},{1,5},{5,1},{9,13},{13,9},{2,6},{6,2},{1... | collective-permute-start | bytes 135176 | tf_op jit(solution)/shard_map/ppermute | solution.py:53
  9.3 0.0 collective-permute-start.3
  9.3 0.0 copy-done.10
  9.3 0.1 copy.15.block
  9.4 0.0 copy-start.8
  9.4 2.1 %adjoint.1 = (f32[32,128]{1,0:T(8,128)S(1)}, f32[32,128]{1,0:T(8,128)S(1)}, f32[840,128]{1,0:T(8,128)S(1)}, f32[24,128]{1,0:T(8,128)S(1)}) custom-call(f32[56,128]{1,0:T(8,128)S(1)} %collective-permute-done.row_b, f32[56,128]{1,0:T(8,128)S(1)} %collective-permute-done.1.row_a, f32[256,128]{1,0:T(8,128)S(1)} %copy-done.2, f32[256,128]{1,0:T(8,128)S(1)} %copy-done.3, ...), custom_call_target="tpu_custom_call" | custom-call | flops 8000000 | bytes 8000000 | tf_op jit(solution)/shard_map/adjoint/pallas_call | solution.py:74
  11.5 0.1 collective-permute-done.2.col_a
  11.6 0.0 collective-permute-done.3.col_b
  11.6 2.0 %left_right.1 = (f32[840,128]{1,0:T(8,128)S(1)}, f32[240,128]{1,0:T(8,128)S(1)}, f32[288,128]{1,0:T(8,128)}) custom-call(f32[840,128]{1,0:T(8,128)S(1)} %get-tuple-element.31._, f32[24,128]{1,0:T(8,128)S(1)} %get-tuple-element.32.seams, f32[88,128]{1,0:T(8,128)S(1)} %collective-permute-done.2.col_a, ...), custom_call_target="tpu_custom_call", output_to_operand_aliasing={{0}: (0, {})} | custom-call | flops 4000000 | bytes 4000000 | tf_op jit(solution)/shard_map/left_right/pallas_call | solution.py:74
  13.6 6.2 %all-to-all-start = ((f32[32,1,1152]{2,1,0:T(1,128)}), f32[32,1,1152]{2,1,0:T(1,128)S(1)}, u32[]{:S(2)}, u32[]{:S(2)}) async-start(f32[32,1,1152]{2,1,0:T(1,128)} %bitcast), calls=%async_computation | async-start | bytes 294912 | tf_op jit(solution)/shard_map/all_to_all | solution.py:789
  19.8 0.1 reshape.13.owners
  19.9 0.9 %join.1 = f32[2,256,128]{2,1,0:T(8,128)} custom-call(f32[256,128]{1,0:T(8,128)S(1)} %get-tuple-element.20.v0, f32[256,128]{1,0:T(8,128)S(1)} %get-tuple-element.21.v1, f32[32,128]{1,0:T(8,128)S(1)} %get-tuple-element.30.vel_ends, f32[240,128]{1,0:T(8,128)S(1)} %get-tuple-element.36.strips), custom_call_target="tpu_custom_call" | custom-call | flops 4000000 | bytes 4000000 | tf_op jit(solution)/shard_map/join/pallas_call | solution.py:74
  20.8 7.5 %all-to-all-done = f32[32,1,1152]{2,1,0:T(1,128)S(1)} async-done(((f32[32,1,1152]{2,1,0:T(1,128)}), f32[32,1,1152]{2,1,0:T(1,128)S(1)}, u32[]{:S(2)}, u32[]{:S(2)}) %all-to-all-start) | async-done | bytes 147488 | tf_op jit(solution)/shard_map/all_to_all | solution.py:789
  28.2 0.8 %pick.1 = f32[1,4,1024]{2,1,0:T(4,128)} custom-call(s32[4,4]{1,0:T(4,128)S(1)} %reshape.13.owners, f32[288,128]{1,0:T(8,128)S(1)} %bitcast.2), custom_call_target="tpu_custom_call" | custom-call | flops 100000 | bytes 100000 | tf_op jit(solution)/shard_map/pick/pallas_call | solution.py:74
  (9 shorter events, 0.0 us)
Async XLA Ops:
  0.6 4.6 %copy-start.2 = (f32[256,128]{1,0:T(8,128)S(1)}, f32[256,128]{1,0:T(8,128)}, u32[]{:S(2)}) copy-start(f32[256,128]{1,0:T(8,128)} %visc.5) | copy-start | bytes 393220
  0.6 4.6 %copy-start.3 = (f32[256,128]{1,0:T(8,128)S(1)}, f32[256,128]{1,0:T(8,128)}, u32[]{:S(2)}) copy-start(f32[256,128]{1,0:T(8,128)} %fric.5) | copy-start | bytes 393220
  0.7 4.6 %copy-start = (f32[2,256,128]{2,1,0:T(8,128)S(1)}, f32[2,256,128]{2,1,0:T(8,128)}, u32[]{:S(2)}) copy-start(f32[2,256,128]{2,1,0:T(8,128)} %driv.5) | copy-start | bytes 786436
  0.7 4.6 %copy-start.1 = (f32[2,256,128]{2,1,0:T(8,128)S(1)}, f32[2,256,128]{2,1,0:T(8,128)}, u32[]{:S(2)}) copy-start(f32[2,256,128]{2,1,0:T(8,128)} %obs.5) | copy-start | bytes 786436
  0.7 4.6 %copy-start.4 = (s32[256,128]{1,0:T(8,128)S(1)}, s32[256,128]{1,0:T(8,128)}, u32[]{:S(2)}) copy-start(s32[256,128]{1,0:T(8,128)} %mask.5) | copy-start | bytes 393220
  2.1 5.2 %collective-permute-start = (f32[56,128]{1,0:T(8,128)S(1)}, f32[56,128]{1,0:T(8,128)S(1)}, u32[]{:S(2)}, u32[]{:S(2)}) collective-permute-start(f32[56,128]{1,0:T(8,128)S(1)} %get-tuple-element.22), channel_id=1, source_target_pairs={{0,4},{4,0},{8,12},{12,8},{1,2},{5,6},{9,10},{13,14},{2,1},{6,5},{... | collective-permute-start | bytes 86024 | tf_op jit(solution)/shard_map/ppermute | solution.py:53
  5.2 2.2 %collective-permute-start.1 = (f32[56,128]{1,0:T(8,128)S(1)}, f32[56,128]{1,0:T(8,128)S(1)}, u32[]{:S(2)}, u32[]{:S(2)}) collective-permute-start(f32[56,128]{1,0:T(8,128)S(1)} %get-tuple-element.23), channel_id=1, source_target_pairs={{0,1},{4,5},{8,9},{12,13},{1,0},{5,4},{9,8},{13,12},{2,3},{6,7},{1... | collective-permute-start | bytes 86024 | tf_op jit(solution)/shard_map/ppermute | solution.py:53
  7.4 1.9 %copy-start.10 = (s32[2,1]{0,1:T(1,128)S(1)}, s32[2,1]{0,1:T(1,128)}, u32[]{:S(2)}) copy-start(s32[2,1]{0,1:T(1,128)} %param.16) | copy-start | bytes 28
  7.4 2.0 %copy-start.5 = (f32[128,128]{1,0:T(8,128)S(1)}, f32[128,128]{1,0:T(8,128)}, u32[]{:S(2)}) copy-start(f32[128,128]{1,0:T(8,128)} %constant.9.clone.basis_q) | copy-start | bytes 196612
  7.5 1.9 %copy-start.7 = (f32[32,128]{1,0:T(8,128)S(1)}, f32[32,128]{1,0:T(8,128)}, u32[]{:S(2)}) copy-start(f32[32,128]{1,0:T(8,128)} %constant.8.clone.basis_p) | copy-start | bytes 49156
  7.5 4.1 %collective-permute-start.2 = (f32[88,128]{1,0:T(8,128)S(1)}, f32[88,128]{1,0:T(8,128)S(1)}, u32[]{:S(2)}, u32[]{:S(2)}) collective-permute-start(f32[88,128]{1,0:T(8,128)S(1)} %get-tuple-element.33), channel_id=1, source_target_pairs={{0,4},{4,0},{8,12},{12,8},{1,5},{5,1},{9,13},{13,9},{2,6},{6,2},{1... | collective-permute-start | bytes 135176 | tf_op jit(solution)/shard_map/ppermute | solution.py:53
  9.3 2.4 %collective-permute-start.3 = (f32[88,128]{1,0:T(8,128)S(1)}, f32[88,128]{1,0:T(8,128)S(1)}, u32[]{:S(2)}, u32[]{:S(2)}) collective-permute-start(f32[88,128]{1,0:T(8,128)S(1)} %get-tuple-element.34), channel_id=1, source_target_pairs={{0,1},{4,8},{8,4},{12,13},{1,0},{5,9},{9,5},{13,12},{2,3},{6,10},{... | collective-permute-start | bytes 135176 | tf_op jit(solution)/shard_map/ppermute | solution.py:53
  9.4 2.3 %copy-start.6 = (bf16[32,768]{1,0:T(8,128)(2,1)S(1)}, bf16[32,768]{1,0:T(8,128)(2,1)}, u32[]{:S(2)}) copy-start(bf16[32,768]{1,0:T(8,128)(2,1)} %constant.10.clone.basis_rows) | copy-start | bytes 147460
  9.4 2.3 %copy-start.8 = (bf16[32,128]{1,0:T(8,128)(2,1)S(1)}, bf16[32,128]{1,0:T(8,128)(2,1)}, u32[]{:S(2)}) copy-start(bf16[32,128]{1,0:T(8,128)(2,1)} %constant.13.basis_cols) | copy-start | bytes 24580
  13.6 6.2 %copy-start.9 = (s32[16]{0:T(128)S(1)}, s32[16]{0:T(128)}, u32[]{:S(2)}) copy-start(s32[16]{0:T(128)} %param.17) | copy-start | bytes 196
  13.6 14.6 %all-to-all-start = ((f32[32,1,1152]{2,1,0:T(1,128)}), f32[32,1,1152]{2,1,0:T(1,128)S(1)}, u32[]{:S(2)}, u32[]{:S(2)}) async-start(f32[32,1,1152]{2,1,0:T(1,128)} %bitcast), calls=%async_computation | async-start | bytes 294912 | tf_op jit(solution)/shard_map/all_to_all | solution.py:789
